TPU v7x, 256 devices: a whole 4x4x8 slice. The times are simulated.
256 devices in a mesh: row: 32 (over x, z), col: 8 (over y, core).
Axes of the slice: x: 4, y: 4, z: 8, core: 2. Of those that a mesh axis runs over, the one named last changes fastest.
Arguments:
- prev_factor: float32 [2, 1024, 32768], P(None, None, ('row', 'col')), may hold values from -0.03125 to 0.03125
- prev_solved: float32 [21, 32768], P(None, ('row', 'col')), may hold values from -6 to 6
- rhs: float32 [2, 21, 1024], replicated, may hold values from -6 to 6
- inverses: float32 [2, 1024, 1024], P(None, 'col'), may hold values from -1 to 2, as said below
- coupling: float32 [1024, 1024], P('col'), may hold values from -0.1875 to 0.1875
- trailing_factor: float32 [131072, 2, 1024], P('row', None, 'col'), may hold values from -0.125 to 0.125
- trailing_rhs: float32 [21, 131072], P(None, 'row'), may hold values from -6 to 6
Outputs:
- solved: float32 [2, 21, 1024], P(None, None, 'col')
- trailing_updated: float32 [21, 131072], P(None, 'row')
Inputs may be any that keep to these rules, and one draw needn't show every extreme that they name: inverses[k] is lower triangular with a positive diagonal between 0.5 and 1.5.
All inputs are finite; a program needn't handle non-finite values.
Results may differ from a plain program's by a relative error of at most 0.000065.
Values sent between devices are 32-bit elements; how exact they have to be, the bound alone decides.
No kernel may reach another device: no remote copies, remote signals or barrier semaphores. Data moves between devices by JAX's collectives and lax.ppermute only.
A program may use at most 64 MiB of HBM per device.

v0:
```python
import jax
import jax.numpy as jnp
from jax import lax
from jax.sharding import PartitionSpec as P


def local(prev_factor, prev_solved, rhs, inverses, coupling, trailing_factor, trailing_rhs):
    highest = lax.Precision.HIGHEST
    width = inverses.shape[1]
    offset = lax.axis_index("col") * width
    first_part = jnp.einsum("ip,rp->ri", prev_factor[0], prev_solved, precision=highest)
    first_sum = lax.psum(first_part, ("row", "col"))
    first = rhs[0] - first_sum
    block0 = jnp.einsum("ij,rj->ri", inverses[0], first, precision=highest)
    whole_block0 = lax.all_gather(block0, "col", axis=1, tiled=True)
    carried = jnp.einsum("ij,rj->ri", coupling, whole_block0, precision=highest)
    second_part = jnp.einsum("ip,rp->ri", prev_factor[1], prev_solved, precision=highest)
    second_sum = lax.psum(second_part, ("row", "col"))
    own_sum = lax.dynamic_slice_in_dim(second_sum, offset, width, 1)
    own_rhs = lax.dynamic_slice_in_dim(rhs[1], offset, width, 1)
    second_rows = own_rhs - own_sum - carried
    second = lax.all_gather(second_rows, "col", axis=1, tiled=True)
    block1 = jnp.einsum("ij,rj->ri", inverses[1], second, precision=highest)
    solved = jnp.stack([block0, block1])
    products = jnp.einsum("tkj,krj->rt", trailing_factor, solved, precision=highest)
    trailing_sum = lax.psum(products, "col")
    return (solved, trailing_rhs - trailing_sum)


def solution(mesh):
    in_specs = (
        P(None, None, ("row", "col")),
        P(None, ("row", "col")),
        P(),
        P(None, "col", None),
        P("col", None),
        P("row", None, "col"),
        P(None, "row"),
    )
    out_specs = (P(None, None, "col"), P(None, "row"))
    return jax.shard_map(local, mesh=mesh, in_specs=in_specs, out_specs=out_specs, check_vma=False)
```

profile of v0, /device:TPU:1, one launch (start us, length us, event | category | flops | bytes accessed | tf_op | source)
XLA Modules:
  0.0 371.8 jit_solution(2518228940825773583)
XLA Ops:
  7.2 0.0 copy-start
  7.2 0.0 all-reduce.6.cloned.1.call-start
  7.2 2.3 fusion.2
  9.5 0.0 copy-start.1
  9.5 2.3 fusion.6
  11.8 0.0 all-reduce.6.cloned.1.call-update
  11.8 0.0 all-reduce.4.cloned.1.call-start
  11.9 1.2 fusion.15
  13.1 251.7 %all-reduce.6.cloned.1.call-done = (f32[21,1024]{1,0:T(8,128)}, f32[21,1024]{1,0:T(8,128)}) async-done(((f32[21,1024]{1,0:T(8,128)}, f32[21,1024]{1,0:T(8,128)}), (f32[21,1024]{1,0:T(8,128)}, f32[21,1024]{1,0:T(8,128)})) %all-reduce.6.cloned.1.call-update) | async-done | bytes 172048 | tf_op jit(solution)/shard_map/psum | solution.py:12
  264.8 1.6 fusion.4
  266.4 13.6 %all_gather.6 = f32[21,1024]{1,0:T(8,128)S(1)} all-gather(f32[21,128]{1,0:T(8,128)S(1)} %fusion.4), channel_id=1, replica_groups=mesh['row'=32,'col'=8] {'col'}, dimensions={1}, use_global_device_ids=true | all-gather | bytes 96768 | tf_op jit(solution)/shard_map/all_gather | solution.py:15
  280.0 0.0 copy-done
  280.0 1.2 convolution_subtract_fusion
  281.2 12.8 %all_gather.7 = f32[21,1024]{1,0:T(8,128)S(1)} all-gather(f32[21,128]{1,0:T(8,128)S(1)} %convolution_subtract_fusion), channel_id=1, replica_groups=mesh['row'=32,'col'=8] {'col'}, dimensions={1}, use_global_device_ids=true | all-gather | bytes 96768 | tf_op jit(solution)/shard_map/all_gather | solution.py:22
  294.0 1.6 convolution_bitcast_fusion.1
  295.5 6.4 %convolution_bitcast_fusion = f32[21,4096]{1,0:T(8,128)} fusion(f32[4096,2,128]{2,1,0:T(2,128)} %param.12, f32[1,21,128]{2,1,0:T(8,128)S(1)} %convolution_bitcast_fusion.1, f32[1,21,128]{2,1,0:T(8,128)S(1)} %bitcast.33), kind=kOutput, calls=%fused_computation | convolution fusion | flops 264246528 | bytes 4559872 | tf_op jit(solution)/shard_map/tkj,krj->rt/dot_general | solution.py:25
  302.0 0.0 all-reduce.4.cloned.1.call-update
  302.0 0.6 copy.14
  302.6 60.6 %all-reduce.4.cloned.1.call-done = f32[21,4096]{1,0:T(8,128)} async-done(((f32[21,4096]{1,0:T(8,128)}), f32[21,4096]{1,0:T(8,128)}) %all-reduce.4.cloned.1.call-update) | async-done | bytes 344080 | tf_op jit(solution)/shard_map/psum | solution.py:26
  363.2 0.0 copy-done.1
  363.2 1.8 sub.15
  (2 shorter events, 0.0 us)
Async XLA Ops:
  7.2 272.8 %copy-start = (f32[128,1024]{1,0:T(8,128)S(1)}, f32[128,1024]{1,0:T(8,128)}, u32[]{:S(2)}) copy-start(f32[128,1024]{1,0:T(8,128)} %param.11) | copy-start | bytes 1572868
  7.2 257.6 %all-reduce.6.cloned.1.call-start = ((), (), s32[]{:S(2)}) async-start(), calls=%async_computation.1 | async-start | bytes 393216 | tf_op jit(solution)/shard_map/psum | solution.py:12
  9.5 353.7 %copy-start.1 = (f32[21,4096]{1,0:T(8,128)S(1)}, f32[21,4096]{1,0:T(8,128)}, u32[]{:S(2)}) copy-start(f32[21,4096]{1,0:T(8,128)} %param.13) | copy-start | bytes 1032196
  11.8 351.4 %all-reduce.4.cloned.1.call-start = ((), (), s32[]{:S(2)}) async-start(), calls=%async_computation | async-start | bytes 786432 | tf_op jit(solution)/shard_map/psum | solution.py:26
Sparse Core Ops, SparseCore 0:
  14.2 250.5 all-reduce.5
  302.1 61.0 all-reduce.3
where the time goes:
time: 373 us; the launch traced here: 372 us
  waiting for transfers between devices  312 us (84%)
  blocking collectives  26.3 us (7%)
  matrix products  15.4 us (4%)
  between operations  14.1 us (4%)
    psum x1, waiting for transfers between devices, local(): first_sum = lax.psum(first_part, ('row', 'col'))  252 us
    psum x1, waiting for transfers between devices, local(): trailing_sum = lax.psum(products, 'col')  60.6 us
    all_gather x1, blocking collectives, local(): whole_block0 = lax.all_gather(block0, 'col', axis=1, tiled=True)  13.6 us
    all_gather x1, blocking collectives, local(): second = lax.all_gather(second_rows, 'col', axis=1, tiled=True)  12.8 us
  transfers between devices with their start and end apart: 2, of which 2 were waited for; matrix products, arithmetic and copies ran while one was open for 0% of the time, Pallas kernels for 0%

commit v1 on v0

v1 whole, which is shorter than its diff:
```python
import jax
import jax.numpy as jnp
from jax import lax
from jax.sharding import PartitionSpec as P

HIGH = lax.Precision.HIGH


def local(prev_factor, prev_solved, rhs, inverses, coupling, trailing_factor, trailing_rhs):
    width = inverses.shape[1]
    row, col = lax.axis_index("row"), lax.axis_index("col")
    core, y = col % 2, col // 2

    def swap(value, axis, mask):
        size = lax.axis_size(axis)
        return lax.ppermute(value, axis, [(i, i ^ mask) for i in range(size)])

    def col_sum(value):
        for mask in (1, 2, 6):
            value = value + swap(value, "col", mask)
        return value

    blocks = coupling.reshape(width, 4, 2, width)
    kept = lax.dynamic_index_in_dim(blocks, core, 2, keepdims=False)
    given = lax.dynamic_index_in_dim(blocks, 1 - core, 2, keepdims=False)
    taken = swap(given, "col", 1)
    pair = jnp.where(core == 0, jnp.concatenate([kept, taken]), jnp.concatenate([taken, kept]))
    columns = jnp.zeros((4, 2 * width, width), jnp.float32)
    for mask in range(4):
        block = lax.dynamic_index_in_dim(pair, y ^ mask, 1, keepdims=False)
        if mask:
            block = swap(block, "col", 2 * mask)
        columns = lax.dynamic_update_index_in_dim(columns, block, y ^ mask, 0)
    columns = columns.reshape(8 * width, width)

    partial0 = jnp.einsum("ip,rp->ri", prev_factor[0], prev_solved, precision=HIGH)
    partial1 = jnp.einsum("ip,rp->ri", prev_factor[1], prev_solved, precision=HIGH)
    first = jnp.where(row == 0, rhs[0], 0.0) - col_sum(partial0)
    block0 = jnp.einsum("ij,rj->ri", inverses[0], first, precision=HIGH)
    own1 = jnp.where((row == 0) & (col == 0), rhs[1], 0.0) - partial1
    second = col_sum(own1 - jnp.einsum("ij,rj->ri", columns, block0, precision=HIGH))
    block1 = jnp.einsum("ij,rj->ri", inverses[1], second, precision=HIGH)

    solved = jnp.stack([block0, block1])
    solved = solved + swap(solved, "row", 8)
    solved = solved + swap(solved, "row", 24)
    groups = [[8 * x + z for z in range(8)] for x in range(4)]
    copies = jnp.broadcast_to(solved[None], (8, *solved.shape))
    solved = jnp.sum(lax.all_to_all(copies, "row", 0, 0, axis_index_groups=groups), axis=0)

    products = jnp.einsum("tkj,krj->rt", trailing_factor, solved, precision=HIGH)
    half = products.shape[1] // 2
    mine = lax.dynamic_slice_in_dim(products, core * half, half, 1)
    other = lax.dynamic_slice_in_dim(products, (1 - core) * half, half, 1)
    mine = mine + swap(other, "col", 1)
    mine = mine + swap(mine, "col", 2)
    mine = mine + swap(mine, "col", 6)
    mine = lax.dynamic_slice_in_dim(trailing_rhs, core * half, half, 1) - mine
    other = swap(mine, "col", 1)
    updated = jnp.where(core == 0, jnp.concatenate([mine, other], 1), jnp.concatenate([other, mine], 1))
    return (solved, updated)


def solution(mesh):
    in_specs = (
        P(None, None, ("row", "col")),
        P(None, ("row", "col")),
        P(),
        P(None, "col", None),
        P("col", None),
        P("row", None, "col"),
        P(None, "row"),
    )
    out_specs = (P(None, None, "col"), P(None, "row"))
    return jax.shard_map(local, mesh=mesh, in_specs=in_specs, out_specs=out_specs, check_vma=False)
```

time: 373 us -> 89.9 us (0.24)
  waiting for transfers between devices: 312 us -> 45.3 us
  starting transfers between devices: 0.08 us -> 30 us
  blocking collectives: 26.3 us -> 0 us
  between operations: 14.1 us -> 0.94 us
  matrix products: 15.4 us -> 7.65 us
    psum x2 -> x0, waiting for transfers between devices: 312 us -> none  [the longest x1 252 us: local(): first_sum = lax.psum(first_part, ('row', 'col'))]
    ppermute x0 -> x16, waiting for transfers between devices: none -> 36.9 us  [swap(): return lax.ppermute(value, axis, [(i, i ^ mask) for i in range(size)])]
    all_gather x2 -> x0, blocking collectives: 26.3 us -> none  [the longest x1 13.6 us: local(): whole_block0 = lax.all_gather(block0, 'col', axis=1, tiled=True)]
    ppermute x0 -> x16, starting transfers between devices: none -> 23.2 us  [swap(): return lax.ppermute(value, axis, [(i, i ^ mask) for i in range(size)])]
    all_to_all x0 -> x1, waiting for transfers between devices: none -> 8.37 us  [local(): lax.all_to_all(copies, 'row', 0, 0, axis_index_groups=groups)]
    dot_general x6, matrix products: 15.4 us -> 7.65 us  [the longest x1 3.93 us: local(): jnp.einsum('tkj,krj->rt', trailing_factor, solved, precision=HIGH)]
    all_to_all x0 -> x1, starting transfers between devices: none -> 6.79 us  [local(): lax.all_to_all(copies, 'row', 0, 0, axis_index_groups=groups)]
  transfers between devices with their start and end apart: 2 -> 17, of which waited for: 2 -> 15; matrix products, arithmetic and copies ran while one was open for 0% -> 6% of each run, Pallas kernels for 0% -> 0%
where the time goes in v1:
time: 89.9 us; the launch traced here: 89.6 us
  waiting for transfers between devices  45.3 us (50%)
  starting transfers between devices  30 us (33%)
  matrix products  7.65 us (9%)
  local copies, waits for them, and re-layouts  4.49 us (5%)
  other arithmetic  1.21 us (1%)
  between operations  0.94 us (1%)
    ppermute x16, waiting for transfers between devices, swap(): return lax.ppermute(value, axis, [(i, i ^ mask) for i in range(size)])  36.9 us
    ppermute x16, starting transfers between devices, swap(): return lax.ppermute(value, axis, [(i, i ^ mask) for i in range(size)])  23.2 us
    all_to_all x1, waiting for transfers between devices, local(): lax.all_to_all(copies, 'row', 0, 0, axis_index_groups=groups)  8.37 us
    all_to_all x1, starting transfers between devices, local(): lax.all_to_all(copies, 'row', 0, 0, axis_index_groups=groups)  6.79 us
    dot_general x1, matrix products, local(): jnp.einsum('tkj,krj->rt', trailing_factor, solved, precision=HIGH)  3.93 us
  transfers between devices with their start and end apart: 17, of which 15 were waited for; matrix products, arithmetic and copies ran while one was open for 6% of the time, Pallas kernels for 0%

profile of v1, /device:TPU:1, one launch (start us, length us, event | category | flops | bytes accessed | tf_op | source)
XLA Modules:
  0.0 89.6 jit_solution(15218981206777715890)
XLA Ops:
  0.6 0.0 copy-start
  0.6 0.0 copy-start.1
  0.7 1.6 %reshape.18 = f32[128,4,2,128]{3,2,1,0:T(2,128)S(1)} reshape(f32[128,1024]{1,0:T(8,128)} %param.11) | data formatting | bytes 1048576 | tf_op jit(solution)/shard_map/reshape | solution.py:23
  2.3 0.5 constant_dynamic-slice_fusion.6
  2.7 3.3 %collective-permute-start.3 = (f32[128,4,128]{2,1,0:T(4,128)S(1)}, f32[128,4,128]{2,1,0:T(4,128)S(1)}, u32[]{:S(2)}, u32[]{:S(2)}) collective-permute-start(f32[128,4,128]{2,1,0:T(4,128)S(1)} %bitcast.51), channel_id=1, source_target_pairs={{0,1},{1,0},{2,3},{3,2},{4,5},{5,4},{6,7},{7,6},{8,9},{9,8},{10,11... | collective-permute-start | bytes 786440 | tf_op jit(solution)/shard_map/ppermute | solution.py:16
  6.0 0.0 copy-done
  6.0 1.4 %fusion.5 = f32[21,1024]{1,0:T(8,128)S(1)} fusion(f32[21,128]{1,0:T(8,128)S(1)} %copy-done, f32[2,1024,128]{2,1,0:T(8,128)} %param.7), kind=kOutput, calls=%fused_computation.10 | convolution fusion | flops 16515072 | bytes 621056 | tf_op jit(solution)/shard_map/ip,rp->ri/dot_general | solution.py:36
  7.4 0.1 collective-permute-start
  7.5 1.1 %fusion.22 = (f32[1,21,1024]{2,0,1:T(1,128)S(1)}, f32[1,21,1024]{2,0,1:T(1,128)S(1)}) fusion(f32[2,21,1024]{2,0,1:T(2,128)} %param.9), kind=kLoop, calls=%fused_computation.43 | loop fusion | bytes 344064 | tf_op jit(solution)/shard_map/slice | solution.py:38
  8.7 0.1 collective-permute-done
  8.8 0.1 collective-permute-start.1
  8.9 1.4 %convolution_subtract_fusion.1 = f32[21,1024]{1,0:T(8,128)S(1)} fusion(f32[21,128]{1,0:T(8,128)S(1)} %copy-done, f32[2,1024,128]{2,1,0:T(8,128)} %param.7, f32[1,21,1024]{2,0,1:T(1,128)S(1)} %get-tuple-element.9, pred[]{:T(512)S(6)} %and.15), kind=kOutput, calls=%fused_computation.3 | convolution fusion | flops 16558080 | bytes 707073 | tf_op jit(solution)/shard_map/ip,rp->ri/dot_general | solution.py:37
  10.4 2.5 %collective-permute-done.1 = f32[21,1024]{1,0:T(8,128)S(1)} collective-permute-done((f32[21,1024]{1,0:T(8,128)S(1)}, f32[21,1024]{1,0:T(8,128)S(1)}, u32[]{:S(2)}, u32[]{:S(2)}) %collective-permute-start.1) | collective-permute-done | bytes 86048 | tf_op jit(solution)/shard_map/ppermute | solution.py:16
  12.9 1.1 %collective-permute-start.2 = (f32[21,1024]{1,0:T(8,128)S(1)}, f32[21,1024]{1,0:T(8,128)S(1)}, u32[]{:S(2)}, u32[]{:S(2)}) collective-permute-start(f32[21,1024]{1,0:T(8,128)S(1)} %add.72), channel_id=1, source_target_pairs={{0,6},{1,7},{2,4},{3,5},{4,2},{5,3},{6,0},{7,1},{8,14},{9,15},{10,... | collective-permute-start | bytes 258056 | tf_op jit(solution)/shard_map/ppermute | solution.py:16
  14.0 0.0 collective-permute-done.3
  14.0 0.2 maximum_select_fusion
  14.2 0.5 constant_dynamic-slice_fusion.1
  14.7 0.1 collective-permute-start.4
  14.8 2.9 %collective-permute-done.2 = f32[21,1024]{1,0:T(8,128)S(1)} collective-permute-done((f32[21,1024]{1,0:T(8,128)S(1)}, f32[21,1024]{1,0:T(8,128)S(1)}, u32[]{:S(2)}, u32[]{:S(2)}) %collective-permute-start.2) | collective-permute-done | bytes 86048 | tf_op jit(solution)/shard_map/ppermute | solution.py:16
  17.7 0.0 copy-done.1
  17.7 0.3 fusion.3
  18.0 0.0 collective-permute-start.5
  18.0 1.5 %collective-permute-start.6 = (f32[256,128]{1,0:T(8,128)S(1)}, f32[256,128]{1,0:T(8,128)S(1)}, u32[]{:S(2)}, u32[]{:S(2)}) collective-permute-start(f32[256,128]{1,0:T(8,128)S(1)} %bitcast.52), channel_id=1, source_target_pairs={{0,6},{1,7},{2,4},{3,5},{4,2},{5,3},{6,0},{7,1},{8,14},{9,15},{10,... | collective-permute-start | bytes 393224 | tf_op jit(solution)/shard_map/ppermute | solution.py:16
  19.6 0.0 collective-permute-done.4
  19.6 3.8 %collective-permute-done.5 = f32[256,128]{1,0:T(8,128)S(1)} collective-permute-done((f32[256,128]{1,0:T(8,128)S(1)}, f32[256,128]{1,0:T(8,128)S(1)}, u32[]{:S(2)}, u32[]{:S(2)}) %collective-permute-start.5) | collective-permute-done | bytes 131104 | tf_op jit(solution)/shard_map/ppermute | solution.py:16
  23.5 1.1 %collective-permute-done.6 = f32[256,128]{1,0:T(8,128)S(1)} collective-permute-done((f32[256,128]{1,0:T(8,128)S(1)}, f32[256,128]{1,0:T(8,128)S(1)}, u32[]{:S(2)}, u32[]{:S(2)}) %collective-permute-start.6) | collective-permute-done | bytes 131104 | tf_op jit(solution)/shard_map/ppermute | solution.py:16
  24.6 0.3 convolution_subtract_fusion
  24.9 0.0 copy-start.3
  24.9 3.8 %collective-permute-start.7 = (f32[21,1024]{1,0:T(8,128)S(1)}, f32[21,1024]{1,0:T(8,128)S(1)}, u32[]{:S(2)}, u32[]{:S(2)}) collective-permute-start(f32[21,1024]{1,0:T(8,128)S(1)} %convolution_subtract_fusion), channel_id=1, source_target_pairs={{0,1},{1,0},{2,3},{3,2},{4,5},{5,4},{6,7},{7,6},{8,9},{9,8},{10,11... | collective-permute-start | bytes 258056 | tf_op jit(solution)/shard_map/ppermute | solution.py:16
  28.7 0.9 %collective-permute-done.7 = f32[21,1024]{1,0:T(8,128)S(1)} collective-permute-done((f32[21,1024]{1,0:T(8,128)S(1)}, f32[21,1024]{1,0:T(8,128)S(1)}, u32[]{:S(2)}, u32[]{:S(2)}) %collective-permute-start.7) | collective-permute-done | bytes 86048 | tf_op jit(solution)/shard_map/ppermute | solution.py:16
  29.6 0.1 collective-permute-start.8
  29.7 4.0 %collective-permute-done.8 = f32[21,1024]{1,0:T(8,128)S(1)} collective-permute-done((f32[21,1024]{1,0:T(8,128)S(1)}, f32[21,1024]{1,0:T(8,128)S(1)}, u32[]{:S(2)}, u32[]{:S(2)}) %collective-permute-start.8) | collective-permute-done | bytes 86048 | tf_op jit(solution)/shard_map/ppermute | solution.py:16
  33.8 1.1 %collective-permute-start.9 = (f32[21,1024]{1,0:T(8,128)S(1)}, f32[21,1024]{1,0:T(8,128)S(1)}, u32[]{:S(2)}, u32[]{:S(2)}) collective-permute-start(f32[21,1024]{1,0:T(8,128)S(1)} %add.82), channel_id=1, source_target_pairs={{0,6},{1,7},{2,4},{3,5},{4,2},{5,3},{6,0},{7,1},{8,14},{9,15},{10,... | collective-permute-start | bytes 258056 | tf_op jit(solution)/shard_map/ppermute | solution.py:16
  34.9 3.6 %collective-permute-done.9 = f32[21,1024]{1,0:T(8,128)S(1)} collective-permute-done((f32[21,1024]{1,0:T(8,128)S(1)}, f32[21,1024]{1,0:T(8,128)S(1)}, u32[]{:S(2)}, u32[]{:S(2)}) %collective-permute-start.9) | collective-permute-done | bytes 86048 | tf_op jit(solution)/shard_map/ppermute | solution.py:16
  38.5 0.3 convolution_bitcast_fusion.1
  38.9 0.1 collective-permute-start.10
  39.0 2.7 %collective-permute-done.10 = f32[2,21,128]{2,1,0:T(8,128)S(1)} collective-permute-done((f32[2,21,128]{2,1,0:T(8,128)S(1)}, f32[2,21,128]{2,1,0:T(8,128)S(1)}, u32[]{:S(2)}, u32[]{:S(2)}) %collective-permute-start.10) | collective-permute-done | bytes 21536 | tf_op jit(solution)/shard_map/ppermute | solution.py:16
  41.7 1.1 %collective-permute-start.11 = (f32[2,21,128]{2,1,0:T(8,128)S(1)}, f32[2,21,128]{2,1,0:T(8,128)S(1)}, u32[]{:S(2)}, u32[]{:S(2)}) collective-permute-start(f32[2,21,128]{2,1,0:T(8,128)S(1)} %fusion.21), channel_id=1, source_target_pairs={{0,192},{8,200},{16,208},{24,216},{32,224},{40,232},{48,240},{56,2... | collective-permute-start | bytes 64520 | tf_op jit(solution)/shard_map/ppermute | solution.py:16
  42.7 2.8 %collective-permute-done.11 = f32[2,21,128]{2,1,0:T(8,128)S(1)} collective-permute-done((f32[2,21,128]{2,1,0:T(8,128)S(1)}, f32[2,21,128]{2,1,0:T(8,128)S(1)}, u32[]{:S(2)}, u32[]{:S(2)}) %collective-permute-start.11) | collective-permute-done | bytes 21536 | tf_op jit(solution)/shard_map/ppermute | solution.py:16
  45.6 0.7 broadcast_in_dim.33
  46.3 6.8 %all-to-all-start = ((f32[8,2,21,128]{3,1,2,0:T(2,128)}), f32[8,2,21,128]{3,1,2,0:T(2,128)S(1)}, u32[]{:S(2)}, u32[]{:S(2)}) async-start(f32[8,2,21,128]{3,1,2,0:T(2,128)} %broadcast_in_dim.33), calls=%async_computation | async-start | bytes 344064 | tf_op jit(solution)/shard_map/all_to_all | solution.py:49
  53.1 8.4 %all-to-all-done = f32[8,2,21,128]{3,1,2,0:T(2,128)S(1)} async-done(((f32[8,2,21,128]{3,1,2,0:T(2,128)}), f32[8,2,21,128]{3,1,2,0:T(2,128)S(1)}, u32[]{:S(2)}, u32[]{:S(2)}) %all-to-all-start) | async-done | bytes 172064 | tf_op jit(solution)/shard_map/all_to_all | solution.py:49
  61.4 0.1 reduce_sum.9
  61.5 0.0 copy-start.2
  61.5 3.9 %convolution_bitcast_fusion = f32[21,4096]{1,0:T(8,128)S(1)} fusion(f32[4096,2,128]{2,1,0:T(2,128)} %param.12, f32[2,21,128]{2,0,1:T(2,128)S(1)} %reduce_sum.9), kind=kOutput, calls=%fused_computation | convolution fusion | flops 132120576 | bytes 4559872 | tf_op jit(solution)/shard_map/tkj,krj->rt/dot_general | solution.py:51
  65.5 6.2 %collective-permute-start.12 = (f32[21,2048]{1,0:T(8,128)S(1)}, f32[21,2048]{1,0:T(8,128)S(1)}, u32[]{:S(2)}, u32[]{:S(2)}) collective-permute-start(f32[21,2048]{1,0:T(8,128)S(1)} %constant_dynamic-slice_fusion), channel_id=1, source_target_pairs={{0,1},{1,0},{2,3},{3,2},{4,5},{5,4},{6,7},{7,6},{8,9},{9,8},{10,11... | collective-permute-start | bytes 516104 | tf_op jit(solution)/shard_map/ppermute | solution.py:16
  71.6 1.1 %collective-permute-done.12 = f32[21,2048]{1,0:T(8,128)S(1)} collective-permute-done((f32[21,2048]{1,0:T(8,128)S(1)}, f32[21,2048]{1,0:T(8,128)S(1)}, u32[]{:S(2)}, u32[]{:S(2)}) %collective-permute-start.12) | collective-permute-done | bytes 172064 | tf_op jit(solution)/shard_map/ppermute | solution.py:16
  72.7 0.1 collective-permute-start.13
  72.8 6.1 %collective-permute-done.13 = f32[21,2048]{1,0:T(8,128)S(1)} collective-permute-done((f32[21,2048]{1,0:T(8,128)S(1)}, f32[21,2048]{1,0:T(8,128)S(1)}, u32[]{:S(2)}, u32[]{:S(2)}) %collective-permute-start.13) | collective-permute-done | bytes 172064 | tf_op jit(solution)/shard_map/ppermute | solution.py:16
  79.0 2.3 %collective-permute-start.14 = (f32[21,2048]{1,0:T(8,128)S(1)}, f32[21,2048]{1,0:T(8,128)S(1)}, u32[]{:S(2)}, u32[]{:S(2)}) collective-permute-start(f32[21,2048]{1,0:T(8,128)S(1)} %add.89), channel_id=1, source_target_pairs={{0,6},{1,7},{2,4},{3,5},{4,2},{5,3},{6,0},{7,1},{8,14},{9,15},{10,... | collective-permute-start | bytes 516104 | tf_op jit(solution)/shard_map/ppermute | solution.py:16
  81.3 4.2 %collective-permute-done.14 = f32[21,2048]{1,0:T(8,128)S(1)} collective-permute-done((f32[21,2048]{1,0:T(8,128)S(1)}, f32[21,2048]{1,0:T(8,128)S(1)}, u32[]{:S(2)}, u32[]{:S(2)}) %collective-permute-start.14) | collective-permute-done | bytes 172064 | tf_op jit(solution)/shard_map/ppermute | solution.py:16
  85.5 0.0 copy-done.3
  85.5 2.2 %collective-permute-start.15 = (f32[21,2048]{1,0:T(8,128)S(1)}, f32[21,2048]{1,0:T(8,128)S(1)}, u32[]{:S(2)}, u32[]{:S(2)}) collective-permute-start(f32[21,2048]{1,0:T(8,128)S(1)} %add_subtract_fusion), channel_id=1, source_target_pairs={{0,1},{1,0},{2,3},{3,2},{4,5},{5,4},{6,7},{7,6},{8,9},{9,8},{10,11... | collective-permute-start | bytes 516104 | tf_op jit(solution)/shard_map/ppermute | solution.py:16
  87.7 1.1 %collective-permute-done.15 = f32[21,2048]{1,0:T(8,128)S(1)} collective-permute-done((f32[21,2048]{1,0:T(8,128)S(1)}, f32[21,2048]{1,0:T(8,128)S(1)}, u32[]{:S(2)}, u32[]{:S(2)}) %collective-permute-start.15) | collective-permute-done | bytes 172064 | tf_op jit(solution)/shard_map/ppermute | solution.py:16
  88.8 0.8 maximum_select_fusion.1
  89.5 0.0 copy-done.2
  (17 shorter events, 0.3 us)
Async XLA Ops:
  0.6 5.4 %copy-start = (f32[21,128]{1,0:T(8,128)S(1)}, f32[21,128]{1,0:T(8,128)}, u32[]{:S(2)}) copy-start(f32[21,128]{1,0:T(8,128)} %param.8) | copy-start | bytes 32260
  0.6 17.0 %copy-start.1 = (f32[2,128,1024]{2,1,0:T(8,128)S(1)}, f32[2,128,1024]{2,1,0:T(8,128)}, u32[]{:S(2)}) copy-start(f32[2,128,1024]{2,1,0:T(8,128)} %param.10) | copy-start | bytes 3145732
  2.7 11.3 %collective-permute-start.3 = (f32[128,4,128]{2,1,0:T(4,128)S(1)}, f32[128,4,128]{2,1,0:T(4,128)S(1)}, u32[]{:S(2)}, u32[]{:S(2)}) collective-permute-start(f32[128,4,128]{2,1,0:T(4,128)S(1)} %bitcast.51), channel_id=1, source_target_pairs={{0,1},{1,0},{2,3},{3,2},{4,5},{5,4},{6,7},{7,6},{8,9},{9,8},{10,11... | collective-permute-start | bytes 786440 | tf_op jit(solution)/shard_map/ppermute | solution.py:16
  7.4 1.4 %collective-permute-start = (f32[21,1024]{1,0:T(8,128)S(1)}, f32[21,1024]{1,0:T(8,128)S(1)}, u32[]{:S(2)}, u32[]{:S(2)}) collective-permute-start(f32[21,1024]{1,0:T(8,128)S(1)} %fusion.5), channel_id=1, source_target_pairs={{0,1},{1,0},{2,3},{3,2},{4,5},{5,4},{6,7},{7,6},{8,9},{9,8},{10,11... | collective-permute-start | bytes 258056 | tf_op jit(solution)/shard_map/ppermute | solution.py:16
  8.8 4.1 %collective-permute-start.1 = (f32[21,1024]{1,0:T(8,128)S(1)}, f32[21,1024]{1,0:T(8,128)S(1)}, u32[]{:S(2)}, u32[]{:S(2)}) collective-permute-start(f32[21,1024]{1,0:T(8,128)S(1)} %add.71), channel_id=1, source_target_pairs={{0,2},{1,3},{2,0},{3,1},{4,6},{5,7},{6,4},{7,5},{8,10},{9,11},{10,... | collective-permute-start | bytes 258056 | tf_op jit(solution)/shard_map/ppermute | solution.py:16
  12.9 4.8 %collective-permute-start.2 = (f32[21,1024]{1,0:T(8,128)S(1)}, f32[21,1024]{1,0:T(8,128)S(1)}, u32[]{:S(2)}, u32[]{:S(2)}) collective-permute-start(f32[21,1024]{1,0:T(8,128)S(1)} %add.72), channel_id=1, source_target_pairs={{0,6},{1,7},{2,4},{3,5},{4,2},{5,3},{6,0},{7,1},{8,14},{9,15},{10,... | collective-permute-start | bytes 258056 | tf_op jit(solution)/shard_map/ppermute | solution.py:16
  14.7 4.9 %collective-permute-start.4 = (f32[256,128]{1,0:T(8,128)S(1)}, f32[256,128]{1,0:T(8,128)S(1)}, u32[]{:S(2)}, u32[]{:S(2)}) collective-permute-start(f32[256,128]{1,0:T(8,128)S(1)} %bitcast.54), channel_id=1, source_target_pairs={{0,2},{1,3},{2,0},{3,1},{4,6},{5,7},{6,4},{7,5},{8,10},{9,11},{10,... | collective-permute-start | bytes 393224 | tf_op jit(solution)/shard_map/ppermute | solution.py:16
  18.0 5.5 %collective-permute-start.5 = (f32[256,128]{1,0:T(8,128)S(1)}, f32[256,128]{1,0:T(8,128)S(1)}, u32[]{:S(2)}, u32[]{:S(2)}) collective-permute-start(f32[256,128]{1,0:T(8,128)S(1)} %bitcast.53), channel_id=1, source_target_pairs={{0,4},{1,5},{2,6},{3,7},{4,0},{5,1},{6,2},{7,3},{8,12},{9,13},{10,... | collective-permute-start | bytes 393224 | tf_op jit(solution)/shard_map/ppermute | solution.py:16
  18.0 6.5 %collective-permute-start.6 = (f32[256,128]{1,0:T(8,128)S(1)}, f32[256,128]{1,0:T(8,128)S(1)}, u32[]{:S(2)}, u32[]{:S(2)}) collective-permute-start(f32[256,128]{1,0:T(8,128)S(1)} %bitcast.52), channel_id=1, source_target_pairs={{0,6},{1,7},{2,4},{3,5},{4,2},{5,3},{6,0},{7,1},{8,14},{9,15},{10,... | collective-permute-start | bytes 393224 | tf_op jit(solution)/shard_map/ppermute | solution.py:16
  24.9 60.5 %copy-start.3 = (f32[21,4096]{1,0:T(8,128)S(1)}, f32[21,4096]{1,0:T(8,128)}, u32[]{:S(2)}) copy-start(f32[21,4096]{1,0:T(8,128)} %param.13) | copy-start | bytes 1032196
  24.9 4.7 %collective-permute-start.7 = (f32[21,1024]{1,0:T(8,128)S(1)}, f32[21,1024]{1,0:T(8,128)S(1)}, u32[]{:S(2)}, u32[]{:S(2)}) collective-permute-start(f32[21,1024]{1,0:T(8,128)S(1)} %convolution_subtract_fusion), channel_id=1, source_target_pairs={{0,1},{1,0},{2,3},{3,2},{4,5},{5,4},{6,7},{7,6},{8,9},{9,8},{10,11... | collective-permute-start | bytes 258056 | tf_op jit(solution)/shard_map/ppermute | solution.py:16
  29.6 4.1 %collective-permute-start.8 = (f32[21,1024]{1,0:T(8,128)S(1)}, f32[21,1024]{1,0:T(8,128)S(1)}, u32[]{:S(2)}, u32[]{:S(2)}) collective-permute-start(f32[21,1024]{1,0:T(8,128)S(1)} %add.81), channel_id=1, source_target_pairs={{0,2},{1,3},{2,0},{3,1},{4,6},{5,7},{6,4},{7,5},{8,10},{9,11},{10,... | collective-permute-start | bytes 258056 | tf_op jit(solution)/shard_map/ppermute | solution.py:16
  33.8 4.8 %collective-permute-start.9 = (f32[21,1024]{1,0:T(8,128)S(1)}, f32[21,1024]{1,0:T(8,128)S(1)}, u32[]{:S(2)}, u32[]{:S(2)}) collective-permute-start(f32[21,1024]{1,0:T(8,128)S(1)} %add.82), channel_id=1, source_target_pairs={{0,6},{1,7},{2,4},{3,5},{4,2},{5,3},{6,0},{7,1},{8,14},{9,15},{10,... | collective-permute-start | bytes 258056 | tf_op jit(solution)/shard_map/ppermute | solution.py:16
  38.9 2.8 %collective-permute-start.10 = (f32[2,21,128]{2,1,0:T(8,128)S(1)}, f32[2,21,128]{2,1,0:T(8,128)S(1)}, u32[]{:S(2)}, u32[]{:S(2)}) collective-permute-start(f32[2,21,128]{2,1,0:T(8,128)S(1)} %pad_maximum_fusion), channel_id=1, source_target_pairs={{0,64},{8,72},{16,80},{24,88},{32,96},{40,104},{48,112},{56,120},{... | collective-permute-start | bytes 64520 | tf_op jit(solution)/shard_map/ppermute | solution.py:16
  41.7 3.9 %collective-permute-start.11 = (f32[2,21,128]{2,1,0:T(8,128)S(1)}, f32[2,21,128]{2,1,0:T(8,128)S(1)}, u32[]{:S(2)}, u32[]{:S(2)}) collective-permute-start(f32[2,21,128]{2,1,0:T(8,128)S(1)} %fusion.21), channel_id=1, source_target_pairs={{0,192},{8,200},{16,208},{24,216},{32,224},{40,232},{48,240},{56,2... | collective-permute-start | bytes 64520 | tf_op jit(solution)/shard_map/ppermute | solution.py:16
  46.3 15.2 %all-to-all-start = ((f32[8,2,21,128]{3,1,2,0:T(2,128)}), f32[8,2,21,128]{3,1,2,0:T(2,128)S(1)}, u32[]{:S(2)}, u32[]{:S(2)}) async-start(f32[8,2,21,128]{3,1,2,0:T(2,128)} %broadcast_in_dim.33), calls=%async_computation | async-start | bytes 344064 | tf_op jit(solution)/shard_map/all_to_all | solution.py:49
  61.5 28.0 %copy-start.2 = (f32[2,21,128]{2,0,1:T(2,128)}, f32[2,21,128]{2,0,1:T(2,128)S(1)}, u32[]{:S(2)}) copy-start(f32[2,21,128]{2,0,1:T(2,128)S(1)} %reduce_sum.9) | copy-start | bytes 64516
  65.5 7.2 %collective-permute-start.12 = (f32[21,2048]{1,0:T(8,128)S(1)}, f32[21,2048]{1,0:T(8,128)S(1)}, u32[]{:S(2)}, u32[]{:S(2)}) collective-permute-start(f32[21,2048]{1,0:T(8,128)S(1)} %constant_dynamic-slice_fusion), channel_id=1, source_target_pairs={{0,1},{1,0},{2,3},{3,2},{4,5},{5,4},{6,7},{7,6},{8,9},{9,8},{10,11... | collective-permute-start | bytes 516104 | tf_op jit(solution)/shard_map/ppermute | solution.py:16
  72.7 6.2 %collective-permute-start.13 = (f32[21,2048]{1,0:T(8,128)S(1)}, f32[21,2048]{1,0:T(8,128)S(1)}, u32[]{:S(2)}, u32[]{:S(2)}) collective-permute-start(f32[21,2048]{1,0:T(8,128)S(1)} %dynamic-slice_add_fusion), channel_id=1, source_target_pairs={{0,2},{1,3},{2,0},{3,1},{4,6},{5,7},{6,4},{7,5},{8,10},{9,11},{10,... | collective-permute-start | bytes 516104 | tf_op jit(solution)/shard_map/ppermute | solution.py:16
  79.0 6.5 %collective-permute-start.14 = (f32[21,2048]{1,0:T(8,128)S(1)}, f32[21,2048]{1,0:T(8,128)S(1)}, u32[]{:S(2)}, u32[]{:S(2)}) collective-permute-start(f32[21,2048]{1,0:T(8,128)S(1)} %add.89), channel_id=1, source_target_pairs={{0,6},{1,7},{2,4},{3,5},{4,2},{5,3},{6,0},{7,1},{8,14},{9,15},{10,... | collective-permute-start | bytes 516104 | tf_op jit(solution)/shard_map/ppermute | solution.py:16
  85.5 3.3 %collective-permute-start.15 = (f32[21,2048]{1,0:T(8,128)S(1)}, f32[21,2048]{1,0:T(8,128)S(1)}, u32[]{:S(2)}, u32[]{:S(2)}) collective-permute-start(f32[21,2048]{1,0:T(8,128)S(1)} %add_subtract_fusion), channel_id=1, source_target_pairs={{0,1},{1,0},{2,3},{3,2},{4,5},{5,4},{6,7},{7,6},{8,9},{9,8},{10,11... | collective-permute-start | bytes 516104 | tf_op jit(solution)/shard_map/ppermute | solution.py:16

commit v2 on v0

v2 whole, which is shorter than its diff:
```python
import jax
import jax.numpy as jnp
from jax import lax
from jax.experimental import pallas as pl
from jax.experimental.pallas import tpu as pltpu
from jax.sharding import PartitionSpec as P

HIGH = lax.Precision.HIGH
CHUNKS = 2
NT = (((1,), (1,)), ((), ()))


def head_and_tail(value):
    head = value.astype(jnp.bfloat16)
    return head, (value - head.astype(jnp.float32)).astype(jnp.bfloat16)


def trailing_kernel(core_ref, solved_ref, factor_ref, other_ref, mine_ref):
    solved = solved_ref[...]
    rhs, count = mine_ref.shape
    pad = -rhs % 8
    solved = jnp.concatenate([solved[:rhs], solved[rhs:]], 1)
    solved = jnp.concatenate([solved, jnp.zeros((pad, solved.shape[1]), jnp.float32)], 0)
    head = solved.astype(jnp.bfloat16).astype(jnp.float32)
    both = jnp.concatenate([head, solved - head], 0).astype(jnp.bfloat16)
    head = head.astype(jnp.bfloat16)
    size = count // CHUNKS
    for out_ref, half in ((other_ref, 1 - core_ref[0]), (mine_ref, core_ref[0])):
        start = pl.multiple_of(2 * count * half, 2 * count)
        for i in range(CHUNKS):
            block = [factor_ref[pl.ds(start + 2 * size * i + k, size, 2), :] for k in range(2)]
            heads, tails = head_and_tail(jnp.concatenate(block, 1))
            main = lax.dot_general(both, heads, NT, preferred_element_type=jnp.float32)
            side = lax.dot_general(head, tails, NT, preferred_element_type=jnp.float32)
            out_ref[:, size * i : size * (i + 1)] = main[:rhs] + (main[rhs + pad : 2 * rhs + pad] + side[:rhs])


def trailing_products(factor, solved, core):
    count, rhs, width = factor.shape[0] // 4, solved.shape[0] // 2, factor.shape[1]
    vmem = pl.BlockSpec(memory_space=pltpu.VMEM)
    return pl.pallas_call(
        trailing_kernel,
        in_specs=[pl.BlockSpec(memory_space=pltpu.SMEM), vmem, vmem],
        out_specs=[vmem] * 2,
        out_shape=[jax.ShapeDtypeStruct((rhs, count), jnp.float32)] * 2,
        cost_estimate=pl.CostEstimate(flops=24 * count * width * rhs, bytes_accessed=16 * count * width, transcendentals=0),
        compiler_params=pltpu.CompilerParams(vmem_limit_bytes=8 * 2**20),
    )(core.reshape(1), solved, pltpu.with_memory_space_constraint(factor, pltpu.VMEM))


def local(prev_factor, prev_solved, rhs, inverses, coupling, trailing_factor, trailing_rhs):
    width = inverses.shape[1]
    row, col = lax.axis_index("row"), lax.axis_index("col")
    core, y = col % 2, col // 2
    both = ("row", "col")

    def swap(value, mask0, mask1=None):
        masks = (mask0, mask0 if mask1 is None else mask1)
        return lax.ppermute(value, both, [(i, i ^ masks[i % 2]) for i in range(256)])

    def y_sum(value):
        value = value + swap(value, 2, 6)
        return value + swap(value, 6, 2)

    def lanes(value, start, size):
        return lax.dynamic_slice_in_dim(value, start, size, value.ndim - 1)

    def by_core(mine, other):
        return jnp.where(core == 0, mine, other), jnp.where(core == 0, other, mine)

    def dot(matrix, value):
        return jnp.einsum("ij,rj->ri", matrix, value, precision=HIGH)

    def among_leaders(value, step):
        return [swap(value, mask, step * i) for i, mask in ((1, 2), (2, 64), (3, 8))]

    def quad_sum(value, step):
        one, two, three = among_leaders(value, step)
        return (value + one) + (two + three)

    def here(value):
        return lax.optimization_barrier(jnp.where(core >= 0, value, 0.0))

    def both_rows(other, mine, value):
        return jnp.concatenate([dot(other, value), dot(mine, value)], 1)

    def gathered(value):
        one, two, three = among_leaders(value, 2)
        return jnp.concatenate(
            [
                jnp.where(y == i, value, jnp.where(y == i ^ 1, one, jnp.where(y == i ^ 2, two, three)))
                for i in range(4)
            ],
            1,
        )

    given = dot(lax.dynamic_index_in_dim(prev_factor, core, 0, keepdims=False), prev_solved)
    taken = swap(given, 1)
    kept = dot(lax.dynamic_index_in_dim(prev_factor, 1 - core, 0, keepdims=False), prev_solved)
    kept = lax.optimization_barrier(kept)
    sums, inverses, coupling, rhs = lax.optimization_barrier((kept + taken, inverses, coupling, rhs))
    other_inverses, other_coupling = swap(inverses, 1), here(swap(coupling, 1))
    other_inverses = here(other_inverses[0]), here(other_inverses[1])
    start = jnp.where(row == 0, lax.dynamic_index_in_dim(rhs, 1 - core, 0, keepdims=False), 0.0)
    reduced = start - y_sum(sums)
    own1 = swap(lanes(reduced, 2 * width * y, 2 * width), 1)
    block0 = both_rows(other_inverses[0], here(inverses[0]), reduced)
    second = own1 - both_rows(other_coupling, coupling, gathered(block0))
    block1 = both_rows(other_inverses[1], inverses[1], gathered(second))

    solved = quad_sum(quad_sum(jnp.concatenate([block0, block1]), 64), 8)
    solved = solved + swap(solved, 2, 56)
    other = swap(solved[:, :width], 1)
    solved = jnp.where(core == 0, other, solved[:, width:])
    other, mine = trailing_products(trailing_factor.reshape(-1, width), solved, core)
    mine = y_sum(mine + swap(other, 1))
    half = mine.shape[1]
    mine = lanes(trailing_rhs, core * half, half) - mine
    return (solved.reshape(2, -1, width), jnp.concatenate(by_core(mine, swap(mine, 1)), 1))


def solution(mesh):
    in_specs = (
        P(None, None, ("row", "col")),
        P(None, ("row", "col")),
        P(),
        P(None, "col", None),
        P("col", None),
        P("row", None, "col"),
        P(None, "row"),
    )
    out_specs = (P(None, None, "col"), P(None, "row"))
    return jax.shard_map(local, mesh=mesh, in_specs=in_specs, out_specs=out_specs, check_vma=False)
```

time: 373 us -> 75.1 us (0.20)
  waiting for transfers between devices: 312 us -> 30 us
  starting transfers between devices: 0.08 us -> 31.2 us
  blocking collectives: 26.3 us -> 0 us
  between operations: 14.1 us -> 0.89 us
  matrix products: 15.4 us -> 3.95 us
    psum x2 -> x0, waiting for transfers between devices: 312 us -> none  [the longest x1 252 us: local(): first_sum = lax.psum(first_part, ('row', 'col'))]
    ppermute x0 -> x24, starting transfers between devices: none -> 31.2 us  [swap(): lax.ppermute(value, both, [(i, i ^ masks[i % 2]) for i in range(256)])]
    ppermute x0 -> x24, waiting for transfers between devices: none -> 30 us  [swap(): lax.ppermute(value, both, [(i, i ^ masks[i % 2]) for i in range(256)])]
    all_gather x2 -> x0, blocking collectives: 26.3 us -> none  [the longest x1 13.6 us: local(): whole_block0 = lax.all_gather(block0, 'col', axis=1, tiled=True)]
    dot_general x6 -> x8, matrix products: 15.4 us -> 3.95 us  [dot(): return jnp.einsum('ij,rj->ri', matrix, value, precision=HIGH)]
  transfers between devices with their start and end apart: 2 -> 24, of which waited for: 2 -> 16; matrix products, arithmetic and copies ran while one was open for 0% -> 7% of each run, Pallas kernels for 0% -> 0%
where the time goes in v2:
time: 75.1 us; the launch traced here: 74.8 us
  starting transfers between devices  31.2 us (42%)
  waiting for transfers between devices  30 us (40%)
  local copies, waits for them, and re-layouts  5.03 us (7%)
  matrix products  3.95 us (5%)
  other arithmetic  2.24 us (3%)
  Pallas kernels  1.4 us (2%)
  between operations  0.89 us (1%)
    ppermute x24, starting transfers between devices, swap(): lax.ppermute(value, both, [(i, i ^ masks[i % 2]) for i in range(256)])  31.2 us
    ppermute x24, waiting for transfers between devices, swap(): lax.ppermute(value, both, [(i, i ^ masks[i % 2]) for i in range(256)])  30 us
    unnamed x11, local copies, waits for them, and re-layouts  4.03 us
    dot_general x8, matrix products, dot(): return jnp.einsum('ij,rj->ri', matrix, value, precision=HIGH)  3.95 us
  transfers between devices with their start and end apart: 24, of which 16 were waited for; matrix products, arithmetic and copies ran while one was open for 7% of the time, Pallas kernels for 0%

profile of v2, /device:TPU:1, one launch (start us, length us, event | category | flops | bytes accessed | tf_op | source)
XLA Modules:
  0.0 74.8 jit_solution(9634074497738181371)
XLA Ops:
  0.6 0.0 copy-start
  0.7 1.2 %copy-done = f32[2,1024,128]{2,1,0:T(8,128)S(1)} copy-done((f32[2,1024,128]{2,1,0:T(8,128)S(1)}, f32[2,1024,128]{2,1,0:T(8,128)}, u32[]{:S(2)}) %copy-start) | copy-done | bytes 1048600
  1.9 1.0 %convolution_bitcast_fusion = f32[21,1024]{1,0:T(8,128)S(1)} fusion(f32[21,128]{1,0:T(8,128)} %param.8, f32[2,1024,128]{2,1,0:T(8,128)S(1)} %copy-done, s32[]{:T(128)S(6)} %select_n.198), kind=kOutput, calls=%fused_computation | convolution fusion | flops 16515072 | bytes 621060 | tf_op jit(solution)/shard_map/ij,rj->ri/dot_general | solution.py:72
  2.9 3.3 %collective-permute-start = (f32[21,1024]{1,0:T(8,128)S(1)}, f32[21,1024]{1,0:T(8,128)S(1)}, u32[]{:S(2)}, u32[]{:S(2)}) collective-permute-start(f32[21,1024]{1,0:T(8,128)S(1)} %convolution_bitcast_fusion), channel_id=1, source_target_pairs={{0,1},{1,0},{2,3},{3,2},{4,5},{5,4},{6,7},{7,6},{8,9},{9,8},{10,11... | collective-permute-start | bytes 258056 | tf_op jit(solution)/shard_map/ppermute | solution.py:59
  6.2 1.0 %convolution_bitcast_fusion.1 = f32[21,1024]{1,0:T(8,128)S(1)} fusion(f32[21,128]{1,0:T(8,128)} %param.8, f32[2,1024,128]{2,1,0:T(8,128)S(1)} %copy-done, s32[]{:T(128)S(6)} %select_n.197), kind=kOutput, calls=%fused_computation.1 | convolution fusion | flops 16515072 | bytes 621060 | tf_op jit(solution)/shard_map/ij,rj->ri/dot_general | solution.py:72
  7.2 0.0 collective-permute-done
  7.3 0.3 collective-permute-start.3
  7.6 1.0 %collective-permute-start.1 = (f32[21,1024]{1,0:T(8,128)S(1)}, f32[21,1024]{1,0:T(8,128)S(1)}, u32[]{:S(2)}, u32[]{:S(2)}) collective-permute-start(f32[21,1024]{1,0:T(8,128)S(1)} %add.63), channel_id=1, source_target_pairs={{0,2},{1,7},{2,0},{3,5},{4,6},{5,3},{6,4},{7,1},{8,10},{9,15},{10,... | collective-permute-start | bytes 258056 | tf_op jit(solution)/shard_map/ppermute | solution.py:59
  8.6 3.7 %collective-permute-done.1 = f32[21,1024]{1,0:T(8,128)S(1)} collective-permute-done((f32[21,1024]{1,0:T(8,128)S(1)}, f32[21,1024]{1,0:T(8,128)S(1)}, u32[]{:S(2)}, u32[]{:S(2)}) %collective-permute-start.1) | collective-permute-done | bytes 86048 | tf_op jit(solution)/shard_map/ppermute | solution.py:59
  12.3 0.1 collective-permute-start.2
  12.4 1.1 %select_bitcast_fusion = f32[128,1024]{1,0:T(8,128)S(1)} fusion(f32[2,128,1024]{2,1,0:T(8,128)} %param.10, pred[]{:T(512)S(6)} %ge.2), kind=kLoop, calls=%fused_computation.11 | loop fusion | flops 131072 | bytes 1048577 | tf_op jit(solution)/shard_map/jit(_where)/select_n | solution.py:82
  13.5 1.0 %copy.11 = f32[2,21,1024]{2,1,0:T(8,128)S(1)} copy(f32[2,21,1024]{2,0,1:T(2,128)} %param.9) | data formatting | bytes 344064 | tf_op jit(solution)/shard_map/optimization_barrier | solution.py:101
  14.5 1.5 %collective-permute-start.8 = (f32[128,1024]{1,0:T(8,128)}, f32[128,1024]{1,0:T(8,128)S(1)}, u32[]{:S(2)}, u32[]{:S(2)}) collective-permute-start(f32[128,1024]{1,0:T(8,128)} %param.11), channel_id=1, source_target_pairs={{0,1},{1,0},{2,3},{3,2},{4,5},{5,4},{6,7},{7,6},{8,9},{9,8},{10,11... | collective-permute-start | bytes 1572872 | tf_op jit(solution)/shard_map/ppermute | solution.py:59
  16.0 0.0 collective-permute-done.2
  16.1 2.5 %collective-permute-start.4 = (f32[21,256]{1,0:T(8,128)S(1)}, f32[21,256]{1,0:T(8,128)S(1)}, u32[]{:S(2)}, u32[]{:S(2)}) collective-permute-start(f32[21,256]{1,0:T(8,128)S(1)} %constant_dynamic-slice_fusion), channel_id=1, source_target_pairs={{0,1},{1,0},{2,3},{3,2},{4,5},{5,4},{6,7},{7,6},{8,9},{9,8},{10,11... | collective-permute-start | bytes 64520 | tf_op jit(solution)/shard_map/ppermute | solution.py:59
  18.6 0.3 fusion.19
  18.9 0.0 collective-permute-done.3
  18.9 0.1 fusion
  19.0 0.3 fusion.18
  19.3 0.1 collective-permute-start.5
  19.4 2.2 %collective-permute-start.6 = (f32[21,256]{1,0:T(8,128)S(1)}, f32[21,256]{1,0:T(8,128)S(1)}, u32[]{:S(2)}, u32[]{:S(2)}) collective-permute-start(f32[21,256]{1,0:T(8,128)S(1)} %pad_maximum_fusion.7), channel_id=1, source_target_pairs={{0,64},{1,5},{2,66},{3,7},{4,68},{5,1},{6,70},{7,3},{8,72},{9,13},... | collective-permute-start | bytes 64520 | tf_op jit(solution)/shard_map/ppermute | solution.py:59
  21.6 1.7 %collective-permute-start.7 = (f32[21,256]{1,0:T(8,128)S(1)}, f32[21,256]{1,0:T(8,128)S(1)}, u32[]{:S(2)}, u32[]{:S(2)}) collective-permute-start(f32[21,256]{1,0:T(8,128)S(1)} %pad_maximum_fusion.7), channel_id=1, source_target_pairs={{0,8},{1,7},{2,10},{3,5},{4,12},{5,3},{6,14},{7,1},{8,0},{9,15},{1... | collective-permute-start | bytes 64520 | tf_op jit(solution)/shard_map/ppermute | solution.py:59
  23.3 0.0 collective-permute-done.8
  23.3 0.0 collective-permute-done.5
  23.3 0.4 collective-permute-done.6
  23.7 1.8 %collective-permute-done.7 = f32[21,256]{1,0:T(8,128)S(1)} collective-permute-done((f32[21,256]{1,0:T(8,128)S(1)}, f32[21,256]{1,0:T(8,128)S(1)}, u32[]{:S(2)}, u32[]{:S(2)}) %collective-permute-start.7) | collective-permute-done | bytes 21536 | tf_op jit(solution)/shard_map/ppermute | solution.py:59
  25.5 0.3 fusion.10
  25.8 0.0 copy-start.4
  25.8 0.3 fusion.11
  26.1 0.0 collective-permute-done.4
  26.2 0.4 collective-permute-start.10
  26.6 1.7 %collective-permute-start.11 = (f32[21,256]{1,0:T(8,128)S(1)}, f32[21,256]{1,0:T(8,128)S(1)}, u32[]{:S(2)}, u32[]{:S(2)}) collective-permute-start(f32[21,256]{1,0:T(8,128)S(1)} %maximum_subtract_fusion), channel_id=1, source_target_pairs={{0,8},{1,7},{2,10},{3,5},{4,12},{5,3},{6,14},{7,1},{8,0},{9,15},{1... | collective-permute-start | bytes 64520 | tf_op jit(solution)/shard_map/ppermute | solution.py:59
  28.2 0.7 collective-permute-start.9
  28.9 1.6 %collective-permute-done.10 = f32[21,256]{1,0:T(8,128)S(1)} collective-permute-done((f32[21,256]{1,0:T(8,128)S(1)}, f32[21,256]{1,0:T(8,128)S(1)}, u32[]{:S(2)}, u32[]{:S(2)}) %collective-permute-start.10) | collective-permute-done | bytes 21536 | tf_op jit(solution)/shard_map/ppermute | solution.py:59
  30.5 0.2 collective-permute-done.11
  30.7 0.2 collective-permute-done.9
  31.0 0.3 fusion.2
  31.3 0.3 fusion.9
  31.6 1.1 %collective-permute-start.12 = (f32[42,256]{1,0:T(8,128)S(1)}, f32[42,256]{1,0:T(8,128)S(1)}, u32[]{:S(2)}, u32[]{:S(2)}) collective-permute-start(f32[42,256]{1,0:T(8,128)S(1)} %maximum_maximum_fusion), channel_id=1, source_target_pairs={{0,2},{1,65},{2,0},{3,67},{4,6},{5,69},{6,4},{7,71},{8,10},{9,73},... | collective-permute-start | bytes 129032 | tf_op jit(solution)/shard_map/ppermute | solution.py:59
  32.7 2.5 %collective-permute-start.13 = (f32[42,256]{1,0:T(8,128)S(1)}, f32[42,256]{1,0:T(8,128)S(1)}, u32[]{:S(2)}, u32[]{:S(2)}) collective-permute-start(f32[42,256]{1,0:T(8,128)S(1)} %maximum_maximum_fusion), channel_id=1, source_target_pairs={{0,64},{1,129},{2,66},{3,131},{4,68},{5,133},{6,70},{7,135},{8,72}... | collective-permute-start | bytes 129032 | tf_op jit(solution)/shard_map/ppermute | solution.py:59
  35.2 0.4 collective-permute-start.14
  35.6 0.0 collective-permute-done.12
  35.6 1.6 %collective-permute-done.13 = f32[42,256]{1,0:T(8,128)S(1)} collective-permute-done((f32[42,256]{1,0:T(8,128)S(1)}, f32[42,256]{1,0:T(8,128)S(1)}, u32[]{:S(2)}, u32[]{:S(2)}) %collective-permute-start.13) | collective-permute-done | bytes 43040 | tf_op jit(solution)/shard_map/ppermute | solution.py:59
  37.2 2.1 %collective-permute-done.14 = f32[42,256]{1,0:T(8,128)S(1)} collective-permute-done((f32[42,256]{1,0:T(8,128)S(1)}, f32[42,256]{1,0:T(8,128)S(1)}, u32[]{:S(2)}, u32[]{:S(2)}) %collective-permute-start.14) | collective-permute-done | bytes 43040 | tf_op jit(solution)/shard_map/ppermute | solution.py:59
  39.3 1.7 %collective-permute-start.15 = (f32[42,256]{1,0:T(8,128)S(1)}, f32[42,256]{1,0:T(8,128)S(1)}, u32[]{:S(2)}, u32[]{:S(2)}) collective-permute-start(f32[42,256]{1,0:T(8,128)S(1)} %add_add_fusion.1), channel_id=1, source_target_pairs={{0,2},{1,9},{2,0},{3,11},{4,6},{5,13},{6,4},{7,15},{8,10},{9,1},{1... | collective-permute-start | bytes 129032 | tf_op jit(solution)/shard_map/ppermute | solution.py:59
  41.1 3.0 %collective-permute-start.16 = (f32[42,256]{1,0:T(8,128)S(1)}, f32[42,256]{1,0:T(8,128)S(1)}, u32[]{:S(2)}, u32[]{:S(2)}) collective-permute-start(f32[42,256]{1,0:T(8,128)S(1)} %add_add_fusion.1), channel_id=1, source_target_pairs={{0,64},{1,17},{2,66},{3,19},{4,68},{5,21},{6,70},{7,23},{8,72},{9,... | collective-permute-start | bytes 129032 | tf_op jit(solution)/shard_map/ppermute | solution.py:59
  44.1 1.6 %collective-permute-done.16 = f32[42,256]{1,0:T(8,128)S(1)} collective-permute-done((f32[42,256]{1,0:T(8,128)S(1)}, f32[42,256]{1,0:T(8,128)S(1)}, u32[]{:S(2)}, u32[]{:S(2)}) %collective-permute-start.16) | collective-permute-done | bytes 43040 | tf_op jit(solution)/shard_map/ppermute | solution.py:59
  45.6 3.2 %collective-permute-done.17 = f32[42,256]{1,0:T(8,128)S(1)} collective-permute-done((f32[42,256]{1,0:T(8,128)S(1)}, f32[42,256]{1,0:T(8,128)S(1)}, u32[]{:S(2)}, u32[]{:S(2)}) %collective-permute-start.17) | collective-permute-done | bytes 43040 | tf_op jit(solution)/shard_map/ppermute | solution.py:59
  48.8 3.1 %collective-permute-start.18 = (f32[42,256]{1,0:T(8,128)S(1)}, f32[42,256]{1,0:T(8,128)S(1)}, u32[]{:S(2)}, u32[]{:S(2)}) collective-permute-start(f32[42,256]{1,0:T(8,128)S(1)} %add_add_fusion), channel_id=1, source_target_pairs={{0,2},{1,57},{2,0},{3,59},{4,6},{5,61},{6,4},{7,63},{8,10},{9,49},... | collective-permute-start | bytes 129032 | tf_op jit(solution)/shard_map/ppermute | solution.py:59
  51.9 1.5 %collective-permute-done.18 = f32[42,256]{1,0:T(8,128)S(1)} collective-permute-done((f32[42,256]{1,0:T(8,128)S(1)}, f32[42,256]{1,0:T(8,128)S(1)}, u32[]{:S(2)}, u32[]{:S(2)}) %collective-permute-start.18) | collective-permute-done | bytes 43040 | tf_op jit(solution)/shard_map/ppermute | solution.py:59
  53.4 0.1 collective-permute-start.19
  53.5 1.2 %collective-permute-done.19 = f32[42,128]{1,0:T(8,128)S(1)} collective-permute-done((f32[42,128]{1,0:T(8,128)S(1)}, f32[42,128]{1,0:T(8,128)S(1)}, u32[]{:S(2)}, u32[]{:S(2)}) %collective-permute-start.19) | collective-permute-done | bytes 21536 | tf_op jit(solution)/shard_map/ppermute | solution.py:59
  54.7 2.2 %copy-done.1 = f32[4096,2,128]{2,1,0:T(2,128)S(1)} copy-done((f32[4096,2,128]{2,1,0:T(2,128)S(1)}, f32[4096,2,128]{2,1,0:T(2,128)}, u32[]{:S(2)}) %copy-start.1) | copy-done | bytes 4194328
  56.9 1.4 %shard_map.86 = (f32[21,2048]{1,0:T(8,128)S(1)}, f32[21,2048]{1,0:T(8,128)S(1)}) custom-call(s32[1]{0:T(128)} %bitcast.9.core_ref, f32[42,128]{1,0:T(8,128)S(1)} %slice_select_fusion.2.solved_ref, f32[8192,128]{1,0:T(8,128)S(1)} %bitcast.32), custom_call_target="tpu_custom_call" | custom-call | flops 132120576 | bytes 4194304 | tf_op jit(solution)/shard_map/pallas_call | solution.py:41
  58.3 0.2 collective-permute-start.20
  58.5 1.3 %collective-permute-done.20 = f32[21,2048]{1,0:T(8,128)S(1)} collective-permute-done((f32[21,2048]{1,0:T(8,128)S(1)}, f32[21,2048]{1,0:T(8,128)S(1)}, u32[]{:S(2)}, u32[]{:S(2)}) %collective-permute-start.20) | collective-permute-done | bytes 172064 | tf_op jit(solution)/shard_map/ppermute | solution.py:59
  59.8 1.3 %collective-permute-start.21 = (f32[21,2048]{1,0:T(8,128)S(1)}, f32[21,2048]{1,0:T(8,128)S(1)}, u32[]{:S(2)}, u32[]{:S(2)}) collective-permute-start(f32[21,2048]{1,0:T(8,128)S(1)} %add.75), channel_id=1, source_target_pairs={{0,2},{1,7},{2,0},{3,5},{4,6},{5,3},{6,4},{7,1},{8,10},{9,15},{10,... | collective-permute-start | bytes 516104 | tf_op jit(solution)/shard_map/ppermute | solution.py:59
  61.1 4.5 %collective-permute-done.21 = f32[21,2048]{1,0:T(8,128)S(1)} collective-permute-done((f32[21,2048]{1,0:T(8,128)S(1)}, f32[21,2048]{1,0:T(8,128)S(1)}, u32[]{:S(2)}, u32[]{:S(2)}) %collective-permute-start.21) | collective-permute-done | bytes 172064 | tf_op jit(solution)/shard_map/ppermute | solution.py:59
  65.7 0.1 collective-permute-start.22
  65.8 4.8 %collective-permute-done.22 = f32[21,2048]{1,0:T(8,128)S(1)} collective-permute-done((f32[21,2048]{1,0:T(8,128)S(1)}, f32[21,2048]{1,0:T(8,128)S(1)}, u32[]{:S(2)}, u32[]{:S(2)}) %collective-permute-start.22) | collective-permute-done | bytes 172064 | tf_op jit(solution)/shard_map/ppermute | solution.py:59
  70.6 2.3 %collective-permute-start.23 = (f32[21,2048]{1,0:T(8,128)S(1)}, f32[21,2048]{1,0:T(8,128)S(1)}, u32[]{:S(2)}, u32[]{:S(2)}) collective-permute-start(f32[21,2048]{1,0:T(8,128)S(1)} %add_subtract_fusion), channel_id=1, source_target_pairs={{0,1},{1,0},{2,3},{3,2},{4,5},{5,4},{6,7},{7,6},{8,9},{9,8},{10,11... | collective-permute-start | bytes 516104 | tf_op jit(solution)/shard_map/ppermute | solution.py:59
  72.9 0.6 copy.12
  73.5 0.4 collective-permute-done.23
  74.0 0.8 %pad_maximum_fusion = f32[21,4096]{1,0:T(8,128)} fusion(f32[21,2048]{1,0:T(8,128)S(1)} %get-tuple-element.21, f32[21,2048]{1,0:T(8,128)S(1)} %get-tuple-element.20), kind=kLoop, calls=%fused_computation.14 | loop fusion | flops 86016 | bytes 688128 | tf_op jit(solution)/shard_map/concatenate | solution.py:119
  (28 shorter events, 0.3 us)
Async XLA Ops:
  0.6 1.2 %copy-start = (f32[2,1024,128]{2,1,0:T(8,128)S(1)}, f32[2,1024,128]{2,1,0:T(8,128)}, u32[]{:S(2)}) copy-start(f32[2,1024,128]{2,1,0:T(8,128)} %param.7) | copy-start | bytes 3145732
  2.9 4.4 %collective-permute-start = (f32[21,1024]{1,0:T(8,128)S(1)}, f32[21,1024]{1,0:T(8,128)S(1)}, u32[]{:S(2)}, u32[]{:S(2)}) collective-permute-start(f32[21,1024]{1,0:T(8,128)S(1)} %convolution_bitcast_fusion), channel_id=1, source_target_pairs={{0,1},{1,0},{2,3},{3,2},{4,5},{5,4},{6,7},{7,6},{8,9},{9,8},{10,11... | collective-permute-start | bytes 258056 | tf_op jit(solution)/shard_map/ppermute | solution.py:59
  7.3 11.6 %collective-permute-start.3 = (f32[2,128,1024]{2,1,0:T(8,128)}, f32[2,128,1024]{2,1,0:T(8,128)S(1)}, u32[]{:S(2)}, u32[]{:S(2)}) collective-permute-start(f32[2,128,1024]{2,1,0:T(8,128)} %param.10), channel_id=1, source_target_pairs={{0,1},{1,0},{2,3},{3,2},{4,5},{5,4},{6,7},{7,6},{8,9},{9,8},{10,11... | collective-permute-start | bytes 3145736 | tf_op jit(solution)/shard_map/ppermute | solution.py:59
  7.6 4.7 %collective-permute-start.1 = (f32[21,1024]{1,0:T(8,128)S(1)}, f32[21,1024]{1,0:T(8,128)S(1)}, u32[]{:S(2)}, u32[]{:S(2)}) collective-permute-start(f32[21,1024]{1,0:T(8,128)S(1)} %add.63), channel_id=1, source_target_pairs={{0,2},{1,7},{2,0},{3,5},{4,6},{5,3},{6,4},{7,1},{8,10},{9,15},{10,... | collective-permute-start | bytes 258056 | tf_op jit(solution)/shard_map/ppermute | solution.py:59
  8.6 22.3 %copy-start.2 = (f32[2,128,1024]{2,1,0:T(8,128)S(1)}, f32[2,128,1024]{2,1,0:T(8,128)}, u32[]{:S(2)}) copy-start(f32[2,128,1024]{2,1,0:T(8,128)} %param.10) | copy-start | bytes 3145732
  8.6 16.9 %copy-start.3 = (f32[128,1024]{1,0:T(8,128)S(1)}, f32[128,1024]{1,0:T(8,128)}, u32[]{:S(2)}) copy-start(f32[128,1024]{1,0:T(8,128)} %param.11) | copy-start | bytes 1572868
  12.3 3.7 %collective-permute-start.2 = (f32[21,1024]{1,0:T(8,128)S(1)}, f32[21,1024]{1,0:T(8,128)S(1)}, u32[]{:S(2)}, u32[]{:S(2)}) collective-permute-start(f32[21,1024]{1,0:T(8,128)S(1)} %add.64), channel_id=1, source_target_pairs={{0,6},{1,3},{2,4},{3,1},{4,2},{5,7},{6,0},{7,5},{8,14},{9,11},{10,... | collective-permute-start | bytes 258056 | tf_op jit(solution)/shard_map/ppermute | solution.py:59
  14.5 8.8 %collective-permute-start.8 = (f32[128,1024]{1,0:T(8,128)}, f32[128,1024]{1,0:T(8,128)S(1)}, u32[]{:S(2)}, u32[]{:S(2)}) collective-permute-start(f32[128,1024]{1,0:T(8,128)} %param.11), channel_id=1, source_target_pairs={{0,1},{1,0},{2,3},{3,2},{4,5},{5,4},{6,7},{7,6},{8,9},{9,8},{10,11... | collective-permute-start | bytes 1572872 | tf_op jit(solution)/shard_map/ppermute | solution.py:59
  16.1 10.1 %collective-permute-start.4 = (f32[21,256]{1,0:T(8,128)S(1)}, f32[21,256]{1,0:T(8,128)S(1)}, u32[]{:S(2)}, u32[]{:S(2)}) collective-permute-start(f32[21,256]{1,0:T(8,128)S(1)} %constant_dynamic-slice_fusion), channel_id=1, source_target_pairs={{0,1},{1,0},{2,3},{3,2},{4,5},{5,4},{6,7},{7,6},{8,9},{9,8},{10,11... | collective-permute-start | bytes 64520 | tf_op jit(solution)/shard_map/ppermute | solution.py:59
  19.3 4.0 %collective-permute-start.5 = (f32[21,256]{1,0:T(8,128)S(1)}, f32[21,256]{1,0:T(8,128)S(1)}, u32[]{:S(2)}, u32[]{:S(2)}) collective-permute-start(f32[21,256]{1,0:T(8,128)S(1)} %pad_maximum_fusion.7), channel_id=1, source_target_pairs={{0,2},{1,3},{2,0},{3,1},{4,6},{5,7},{6,4},{7,5},{8,10},{9,11},{10,... | collective-permute-start | bytes 64520 | tf_op jit(solution)/shard_map/ppermute | solution.py:59
  19.4 4.3 %collective-permute-start.6 = (f32[21,256]{1,0:T(8,128)S(1)}, f32[21,256]{1,0:T(8,128)S(1)}, u32[]{:S(2)}, u32[]{:S(2)}) collective-permute-start(f32[21,256]{1,0:T(8,128)S(1)} %pad_maximum_fusion.7), channel_id=1, source_target_pairs={{0,64},{1,5},{2,66},{3,7},{4,68},{5,1},{6,70},{7,3},{8,72},{9,13},... | collective-permute-start | bytes 64520 | tf_op jit(solution)/shard_map/ppermute | solution.py:59
  21.6 3.9 %collective-permute-start.7 = (f32[21,256]{1,0:T(8,128)S(1)}, f32[21,256]{1,0:T(8,128)S(1)}, u32[]{:S(2)}, u32[]{:S(2)}) collective-permute-start(f32[21,256]{1,0:T(8,128)S(1)} %pad_maximum_fusion.7), channel_id=1, source_target_pairs={{0,8},{1,7},{2,10},{3,5},{4,12},{5,3},{6,14},{7,1},{8,0},{9,15},{1... | collective-permute-start | bytes 64520 | tf_op jit(solution)/shard_map/ppermute | solution.py:59
  25.8 44.8 %copy-start.4 = (f32[21,4096]{1,0:T(8,128)S(1)}, f32[21,4096]{1,0:T(8,128)}, u32[]{:S(2)}) copy-start(f32[21,4096]{1,0:T(8,128)} %param.13) | copy-start | bytes 1032196
  26.2 4.3 %collective-permute-start.10 = (f32[21,256]{1,0:T(8,128)S(1)}, f32[21,256]{1,0:T(8,128)S(1)}, u32[]{:S(2)}, u32[]{:S(2)}) collective-permute-start(f32[21,256]{1,0:T(8,128)S(1)} %maximum_subtract_fusion), channel_id=1, source_target_pairs={{0,64},{1,5},{2,66},{3,7},{4,68},{5,1},{6,70},{7,3},{8,72},{9,13},... | collective-permute-start | bytes 64520 | tf_op jit(solution)/shard_map/ppermute | solution.py:59
  26.6 4.1 %collective-permute-start.11 = (f32[21,256]{1,0:T(8,128)S(1)}, f32[21,256]{1,0:T(8,128)S(1)}, u32[]{:S(2)}, u32[]{:S(2)}) collective-permute-start(f32[21,256]{1,0:T(8,128)S(1)} %maximum_subtract_fusion), channel_id=1, source_target_pairs={{0,8},{1,7},{2,10},{3,5},{4,12},{5,3},{6,14},{7,1},{8,0},{9,15},{1... | collective-permute-start | bytes 64520 | tf_op jit(solution)/shard_map/ppermute | solution.py:59
  28.2 2.7 %collective-permute-start.9 = (f32[21,256]{1,0:T(8,128)S(1)}, f32[21,256]{1,0:T(8,128)S(1)}, u32[]{:S(2)}, u32[]{:S(2)}) collective-permute-start(f32[21,256]{1,0:T(8,128)S(1)} %maximum_subtract_fusion), channel_id=1, source_target_pairs={{0,2},{1,3},{2,0},{3,1},{4,6},{5,7},{6,4},{7,5},{8,10},{9,11},{10,... | collective-permute-start | bytes 64520 | tf_op jit(solution)/shard_map/ppermute | solution.py:59
  31.6 3.9 %collective-permute-start.12 = (f32[42,256]{1,0:T(8,128)S(1)}, f32[42,256]{1,0:T(8,128)S(1)}, u32[]{:S(2)}, u32[]{:S(2)}) collective-permute-start(f32[42,256]{1,0:T(8,128)S(1)} %maximum_maximum_fusion), channel_id=1, source_target_pairs={{0,2},{1,65},{2,0},{3,67},{4,6},{5,69},{6,4},{7,71},{8,10},{9,73},... | collective-permute-start | bytes 129032 | tf_op jit(solution)/shard_map/ppermute | solution.py:59
  32.7 4.5 %collective-permute-start.13 = (f32[42,256]{1,0:T(8,128)S(1)}, f32[42,256]{1,0:T(8,128)S(1)}, u32[]{:S(2)}, u32[]{:S(2)}) collective-permute-start(f32[42,256]{1,0:T(8,128)S(1)} %maximum_maximum_fusion), channel_id=1, source_target_pairs={{0,64},{1,129},{2,66},{3,131},{4,68},{5,133},{6,70},{7,135},{8,72}... | collective-permute-start | bytes 129032 | tf_op jit(solution)/shard_map/ppermute | solution.py:59
  35.2 4.2 %collective-permute-start.14 = (f32[42,256]{1,0:T(8,128)S(1)}, f32[42,256]{1,0:T(8,128)S(1)}, u32[]{:S(2)}, u32[]{:S(2)}) collective-permute-start(f32[42,256]{1,0:T(8,128)S(1)} %maximum_maximum_fusion), channel_id=1, source_target_pairs={{0,8},{1,193},{2,10},{3,195},{4,12},{5,197},{6,14},{7,199},{8,0},{... | collective-permute-start | bytes 129032 | tf_op jit(solution)/shard_map/ppermute | solution.py:59
  39.3 4.7 %collective-permute-start.15 = (f32[42,256]{1,0:T(8,128)S(1)}, f32[42,256]{1,0:T(8,128)S(1)}, u32[]{:S(2)}, u32[]{:S(2)}) collective-permute-start(f32[42,256]{1,0:T(8,128)S(1)} %add_add_fusion.1), channel_id=1, source_target_pairs={{0,2},{1,9},{2,0},{3,11},{4,6},{5,13},{6,4},{7,15},{8,10},{9,1},{1... | collective-permute-start | bytes 129032 | tf_op jit(solution)/shard_map/ppermute | solution.py:59
  41.1 4.6 %collective-permute-start.16 = (f32[42,256]{1,0:T(8,128)S(1)}, f32[42,256]{1,0:T(8,128)S(1)}, u32[]{:S(2)}, u32[]{:S(2)}) collective-permute-start(f32[42,256]{1,0:T(8,128)S(1)} %add_add_fusion.1), channel_id=1, source_target_pairs={{0,64},{1,17},{2,66},{3,19},{4,68},{5,21},{6,70},{7,23},{8,72},{9,... | collective-permute-start | bytes 129032 | tf_op jit(solution)/shard_map/ppermute | solution.py:59
  44.1 4.7 %collective-permute-start.17 = (f32[42,256]{1,0:T(8,128)S(1)}, f32[42,256]{1,0:T(8,128)S(1)}, u32[]{:S(2)}, u32[]{:S(2)}) collective-permute-start(f32[42,256]{1,0:T(8,128)S(1)} %add_add_fusion.1), channel_id=1, source_target_pairs={{0,8},{1,25},{2,10},{3,27},{4,12},{5,29},{6,14},{7,31},{8,0},{9,17... | collective-permute-start | bytes 129032 | tf_op jit(solution)/shard_map/ppermute | solution.py:59
  48.8 4.6 %collective-permute-start.18 = (f32[42,256]{1,0:T(8,128)S(1)}, f32[42,256]{1,0:T(8,128)S(1)}, u32[]{:S(2)}, u32[]{:S(2)}) collective-permute-start(f32[42,256]{1,0:T(8,128)S(1)} %add_add_fusion), channel_id=1, source_target_pairs={{0,2},{1,57},{2,0},{3,59},{4,6},{5,61},{6,4},{7,63},{8,10},{9,49},... | collective-permute-start | bytes 129032 | tf_op jit(solution)/shard_map/ppermute | solution.py:59
  53.4 1.3 %collective-permute-start.19 = (f32[42,128]{1,0:T(8,128)S(1)}, f32[42,128]{1,0:T(8,128)S(1)}, u32[]{:S(2)}, u32[]{:S(2)}) collective-permute-start(f32[42,128]{1,0:T(8,128)S(1)} %slice.26), channel_id=1, source_target_pairs={{0,1},{1,0},{2,3},{3,2},{4,5},{5,4},{6,7},{7,6},{8,9},{9,8},{10,11... | collective-permute-start | bytes 64520 | tf_op jit(solution)/shard_map/ppermute | solution.py:59
  54.7 2.2 %copy-start.1 = (f32[4096,2,128]{2,1,0:T(2,128)S(1)}, f32[4096,2,128]{2,1,0:T(2,128)}, u32[]{:S(2)}) copy-start(f32[4096,2,128]{2,1,0:T(2,128)} %param.12) | copy-start | bytes 12582916
  58.3 1.5 %collective-permute-start.20 = (f32[21,2048]{1,0:T(8,128)S(1)}, f32[21,2048]{1,0:T(8,128)S(1)}, u32[]{:S(2)}, u32[]{:S(2)}) collective-permute-start(f32[21,2048]{1,0:T(8,128)S(1)} %get-tuple-element.13), channel_id=1, source_target_pairs={{0,1},{1,0},{2,3},{3,2},{4,5},{5,4},{6,7},{7,6},{8,9},{9,8},{10,11... | collective-permute-start | bytes 516104 | tf_op jit(solution)/shard_map/ppermute | solution.py:59
  59.8 5.8 %collective-permute-start.21 = (f32[21,2048]{1,0:T(8,128)S(1)}, f32[21,2048]{1,0:T(8,128)S(1)}, u32[]{:S(2)}, u32[]{:S(2)}) collective-permute-start(f32[21,2048]{1,0:T(8,128)S(1)} %add.75), channel_id=1, source_target_pairs={{0,2},{1,7},{2,0},{3,5},{4,6},{5,3},{6,4},{7,1},{8,10},{9,15},{10,... | collective-permute-start | bytes 516104 | tf_op jit(solution)/shard_map/ppermute | solution.py:59
  65.7 4.9 %collective-permute-start.22 = (f32[21,2048]{1,0:T(8,128)S(1)}, f32[21,2048]{1,0:T(8,128)S(1)}, u32[]{:S(2)}, u32[]{:S(2)}) collective-permute-start(f32[21,2048]{1,0:T(8,128)S(1)} %add.76), channel_id=1, source_target_pairs={{0,6},{1,3},{2,4},{3,1},{4,2},{5,7},{6,0},{7,5},{8,14},{9,11},{10,... | collective-permute-start | bytes 516104 | tf_op jit(solution)/shard_map/ppermute | solution.py:59
  70.6 3.3 %collective-permute-start.23 = (f32[21,2048]{1,0:T(8,128)S(1)}, f32[21,2048]{1,0:T(8,128)S(1)}, u32[]{:S(2)}, u32[]{:S(2)}) collective-permute-start(f32[21,2048]{1,0:T(8,128)S(1)} %add_subtract_fusion), channel_id=1, source_target_pairs={{0,1},{1,0},{2,3},{3,2},{4,5},{5,4},{6,7},{7,6},{8,9},{9,8},{10,11... | collective-permute-start | bytes 516104 | tf_op jit(solution)/shard_map/ppermute | solution.py:59

commit v3 on v2

v3 whole, which is shorter than its diff:
```python
import jax
import jax.numpy as jnp
from jax import lax
from jax.experimental import pallas as pl
from jax.experimental.pallas import tpu as pltpu
from jax.sharding import PartitionSpec as P

HIGH = lax.Precision.HIGH
CHUNKS = 2
NT = (((1,), (1,)), ((), ()))


def head_and_tail(value):
    head = value.astype(jnp.bfloat16)
    return head, (value - head.astype(jnp.float32)).astype(jnp.bfloat16)


def product(left, right):
    rows, pad = left.shape[0], -left.shape[0] % 8
    left = jnp.concatenate([left, jnp.zeros((pad, left.shape[1]), jnp.float32)], 0)
    head = left.astype(jnp.bfloat16).astype(jnp.float32)
    both = jnp.concatenate([head, left - head], 0).astype(jnp.bfloat16)
    heads, tails = head_and_tail(right)
    main = lax.dot_general(both, heads, NT, preferred_element_type=jnp.float32)
    side = lax.dot_general(head.astype(jnp.bfloat16), tails, NT, preferred_element_type=jnp.float32)
    return main[:rows] + (main[rows + pad : 2 * rows + pad] + side[:rows])


def local_call(kernel, out_shape, scalar, *arrays, pinned=(), work=(0, 0)):
    vmem = pl.BlockSpec(memory_space=pltpu.VMEM)
    pinned = [pltpu.with_memory_space_constraint(array, pltpu.VMEM) for array in pinned]
    return pl.pallas_call(
        kernel,
        in_specs=[pl.BlockSpec(memory_space=pltpu.SMEM)] + [vmem] * (len(arrays) + len(pinned)),
        out_specs=[vmem] * len(out_shape),
        out_shape=[jax.ShapeDtypeStruct(shape, jnp.float32) for shape in out_shape],
        cost_estimate=pl.CostEstimate(flops=work[0], bytes_accessed=work[1], transcendentals=0),
        compiler_params=pltpu.CompilerParams(vmem_limit_bytes=8 * 2**20),
    )(scalar.reshape(1), *arrays, *pinned)


def rows_of_both(other_ref, own_ref):
    return jnp.concatenate([other_ref[...], own_ref[...]], 0)


def in_order(y, refs):
    own, one, two, three = [ref[...] for ref in refs]
    blocks = [jnp.where(y == i, own, jnp.where(y == i ^ 1, one, jnp.where(y == i ^ 2, two, three))) for i in range(4)]
    return jnp.concatenate(blocks, 1)


def first_kernel(y_ref, reduced_ref, other_ref, own_ref, out_ref):
    out_ref[...] = product(reduced_ref[...], rows_of_both(other_ref, own_ref))


def second_kernel(y_ref, base_ref, own0, one0, two0, three0, other_ref, own_ref, out_ref):
    known = in_order(y_ref[0], (own0, one0, two0, three0))
    out_ref[...] = base_ref[...] - product(known, rows_of_both(other_ref, own_ref))


def third_kernel(y_ref, block0_ref, own1, one1, two1, three1, other_ref, own_ref, out_ref):
    known = in_order(y_ref[0], (own1, one1, two1, three1))
    rows = block0_ref.shape[0]
    out_ref[:rows, :] = block0_ref[...]
    out_ref[rows:, :] = product(known, rows_of_both(other_ref, own_ref))


def unknowns(core_ref, leader_ref, taken_ref):
    return jnp.where(core_ref[0] == 0, taken_ref[...], leader_ref[:, taken_ref.shape[1] :])


def trailing_kernel(own, core_ref, leader_ref, taken_ref, factor_ref, out_ref, *solved_ref):
    solved = unknowns(core_ref, leader_ref, taken_ref)
    if own:
        solved_ref[0][...] = solved
    rhs, count = out_ref.shape
    pad = -rhs % 8
    solved = jnp.concatenate([solved[:rhs], solved[rhs:]], 1)
    solved = jnp.concatenate([solved, jnp.zeros((pad, solved.shape[1]), jnp.float32)], 0)
    head = solved.astype(jnp.bfloat16).astype(jnp.float32)
    both = jnp.concatenate([head, solved - head], 0).astype(jnp.bfloat16)
    head = head.astype(jnp.bfloat16)
    size = count // CHUNKS
    start = pl.multiple_of(2 * count * (core_ref[0] if own else 1 - core_ref[0]), 2 * count)
    for i in range(CHUNKS):
        block = [factor_ref[pl.ds(start + 2 * size * i + k, size, 2), :] for k in range(2)]
        heads, tails = head_and_tail(jnp.concatenate(block, 1))
        main = lax.dot_general(both, heads, NT, preferred_element_type=jnp.float32)
        side = lax.dot_general(head, tails, NT, preferred_element_type=jnp.float32)
        out_ref[:, size * i : size * (i + 1)] = main[:rhs] + (main[rhs + pad : 2 * rhs + pad] + side[:rhs])


def trailing_products(own, factor, leader, taken, core):
    count, rhs, width = factor.shape[0] // 4, taken.shape[0] // 2, factor.shape[1]
    vmem = pl.BlockSpec(memory_space=pltpu.VMEM)
    out_shape = [jax.ShapeDtypeStruct((rhs, count), jnp.float32)]
    if own:
        out_shape.append(jax.ShapeDtypeStruct(taken.shape, jnp.float32))
    return pl.pallas_call(
        lambda *refs: trailing_kernel(own, *refs),
        in_specs=[pl.BlockSpec(memory_space=pltpu.SMEM), vmem, vmem, vmem],
        out_specs=[vmem] * len(out_shape),
        out_shape=out_shape,
        cost_estimate=pl.CostEstimate(flops=12 * count * width * rhs, bytes_accessed=8 * count * width, transcendentals=0),
        compiler_params=pltpu.CompilerParams(vmem_limit_bytes=8 * 2**20),
    )(core.reshape(1), leader, taken, pltpu.with_memory_space_constraint(factor, pltpu.VMEM))


def place_kernel(half_ref, value_ref, *rest):
    out_ref, sem = rest[-2:]
    count = value_ref.shape[1]
    start = pl.multiple_of(half_ref[0] * count, count)
    copy = pltpu.make_async_copy(value_ref, out_ref.at[:, pl.ds(start, count)], sem)
    copy.start()
    copy.wait()


def place(half, value, *target):
    vmem, anywhere = pl.BlockSpec(memory_space=pltpu.VMEM), pl.BlockSpec(memory_space=pl.ANY)
    return pl.pallas_call(
        place_kernel,
        in_specs=[pl.BlockSpec(memory_space=pltpu.SMEM), vmem] + [anywhere] * len(target),
        out_specs=anywhere,
        out_shape=jax.ShapeDtypeStruct((value.shape[0], 2 * value.shape[1]), jnp.float32),
        scratch_shapes=[pltpu.SemaphoreType.DMA],
        input_output_aliases={2: 0} if target else {},
    )(half.reshape(1), pltpu.with_memory_space_constraint(value, pltpu.VMEM), *target)


def local(prev_factor, prev_solved, rhs, inverses, coupling, trailing_factor, trailing_rhs):
    width = inverses.shape[1]
    row, col = lax.axis_index("row"), lax.axis_index("col")
    core, y = col & 1, col >> 1
    both = ("row", "col")

    def swap(value, mask0, mask1=None):
        masks = (mask0, mask0 if mask1 is None else mask1)
        return lax.ppermute(value, both, [(i, i ^ masks[i % 2]) for i in range(256)])

    def y_sum(value):
        value = value + swap(value, 2, 6)
        return value + swap(value, 6, 2)

    def lanes(value, start, size):
        return lax.dynamic_slice_in_dim(value, start, size, value.ndim - 1)

    def by_core(mine, other):
        return jnp.where(core == 0, mine, other), jnp.where(core == 0, other, mine)

    def dot(matrix, value):
        return jnp.einsum("ij,rj->ri", matrix, value, precision=HIGH)

    def among_leaders(value, step):
        return [swap(value, mask, step * i) for i, mask in ((1, 2), (2, 64), (3, 8))]

    def quad_sum(value, step):
        one, two, three = among_leaders(value, step)
        return (value + one) + (two + three)

    def here(value):
        return lax.optimization_barrier(jnp.where(core >= 0, value, 0.0))

    given = dot(lax.dynamic_index_in_dim(prev_factor, core, 0, keepdims=False), prev_solved)
    taken = swap(given, 1)
    kept = dot(lax.dynamic_index_in_dim(prev_factor, 1 - core, 0, keepdims=False), prev_solved)
    kept = lax.optimization_barrier(kept)
    sums, inverses, coupling, rhs = lax.optimization_barrier((kept + taken, inverses, coupling, rhs))
    other_inverses = swap(inverses, 1)
    inverses0 = here(other_inverses[0]), here(inverses[0])
    inverses1 = here(other_inverses[1]), here(inverses[1])
    one, two, three = swap(sums, 2, 6), swap(sums, 6, 2), swap(sums, 4)
    one, coupling = lax.optimization_barrier((one, coupling))
    couplings = here(swap(coupling, 1)), here(coupling)
    start = jnp.where(row == 0, lax.dynamic_index_in_dim(rhs, 1 - core, 0, keepdims=False), 0.0)
    reduced = start - ((sums + one) + (two + three))
    rows, work = reduced.shape[0], (12 * 21 * width * 8 * width, 16 * width * 8 * width)
    shape = (rows, 2 * width)
    (block0,) = local_call(first_kernel, [shape], y, reduced, pinned=inverses0, work=work)
    block0, own1 = lax.optimization_barrier((block0, lanes(reduced, 2 * width * y, 2 * width)))
    others = among_leaders(block0, 2)
    (second,) = local_call(second_kernel, [shape], y, swap(own1, 1), block0, *others, pinned=couplings, work=work)
    others = among_leaders(second, 2)
    (solved,) = local_call(third_kernel, [(2 * rows, 2 * width)], y, block0, second, *others, pinned=inverses1, work=work)
    solved = quad_sum(solved, 64)
    solved, trailing_factor = lax.optimization_barrier((solved, trailing_factor))
    solved = quad_sum(solved, 8)
    solved = solved + swap(solved, 2, 48)
    taken = swap(solved[:, :width], 1)

    factor = trailing_factor.reshape(-1, width)
    (other,) = trailing_products(False, factor, solved, taken, core)
    mine, solved = trailing_products(True, factor, solved, taken, core)
    mine = y_sum(mine + swap(other, 1))
    half = mine.shape[1]
    mine = lanes(trailing_rhs, core * half, half) - mine
    updated = place(1 - core, swap(mine, 1), place(core, mine))
    return (solved.reshape(2, -1, width), updated)


def solution(mesh):
    in_specs = (
        P(None, None, ("row", "col")),
        P(None, ("row", "col")),
        P(),
        P(None, "col", None),
        P("col", None),
        P("row", None, "col"),
        P(None, "row"),
    )
    out_specs = (P(None, None, "col"), P(None, "row"))
    return jax.shard_map(local, mesh=mesh, in_specs=in_specs, out_specs=out_specs, check_vma=False)
```

time: 75.1 us -> 70.4 us (0.937)
  waiting for transfers between devices: 30 us -> 25.8 us
  Pallas kernels: 1.4 us -> 4.1 us
  local copies, waits for them, and re-layouts: 5.03 us -> 2.84 us
  matrix products: 3.95 us -> 2.06 us
  starting transfers between devices: 31.2 us -> 32.7 us
    ppermute x24 -> x25, waiting for transfers between devices: 30 us -> 25.8 us  [swap(): lax.ppermute(value, both, [(i, i ^ masks[i % 2]) for i in range(256)])]
    pallas_call x1 -> x7, Pallas kernels: 1.4 us -> 4.1 us  [the longest x2 1.46 us: trailing_products(): pl.pallas_call(lambda *refs: trailing_kernel(own, *refs), in_specs=[pl.Bl...]
    unnamed x11 -> x9, local copies, waits for them, and re-layouts: 4.03 us -> 1.84 us
    dot_general x8 -> x2, matrix products: 3.95 us -> 2.06 us  [dot(): return jnp.einsum('ij,rj->ri', matrix, value, precision=HIGH)]
    ppermute x24 -> x25, starting transfers between devices: 31.2 us -> 32.7 us  [swap(): lax.ppermute(value, both, [(i, i ^ masks[i % 2]) for i in range(256)])]
    concatenate x3 -> x0, other arithmetic: 0.81 us -> none  [the longest x1 0.77 us: local(): jnp.concatenate(by_core(mine, swap(mine, 1)), 1)]
  transfers between devices with their start and end apart: 24 -> 25, of which waited for: 16 -> 14; matrix products, arithmetic and copies ran while one was open for 7% -> 6% of each run, Pallas kernels for 0% -> 3%
where the time goes in v3:
time: 70.4 us; the launch traced here: 70.2 us
  starting transfers between devices  32.7 us (46%)
  waiting for transfers between devices  25.8 us (37%)
  Pallas kernels  4.1 us (6%)
  local copies, waits for them, and re-layouts  2.84 us (4%)
  matrix products  2.06 us (3%)
  other arithmetic  1.62 us (2%)
  between operations  1.02 us (1%)
    ppermute x25, starting transfers between devices, swap(): lax.ppermute(value, both, [(i, i ^ masks[i % 2]) for i in range(256)])  32.7 us
    ppermute x25, waiting for transfers between devices, swap(): lax.ppermute(value, both, [(i, i ^ masks[i % 2]) for i in range(256)])  25.8 us
    dot_general x2, matrix products, dot(): return jnp.einsum('ij,rj->ri', matrix, value, precision=HIGH)  2.06 us
    unnamed x9, local copies, waits for them, and re-layouts  1.84 us
    select_n x4, other arithmetic, here(): return lax.optimization_barrier(jnp.where(core >= 0, value, 0.0))  1.46 us
    pallas_call x2, Pallas kernels, trailing_products(): pl.pallas_call(lambda *refs: trailing_kernel(own, *refs), in_specs=[pl.Bl...  1.46 us
  transfers between devices with their start and end apart: 25, of which 14 were waited for; matrix products, arithmetic and copies ran while one was open for 6% of the time, Pallas kernels for 3%

profile of v3, /device:TPU:1, one launch (start us, length us, event | category | flops | bytes accessed | tf_op | source)
XLA Modules:
  0.0 70.2 jit_solution(11828630800812757698)
XLA Ops:
  0.6 0.0 copy-start
  0.6 0.0 copy-start.2
  0.7 1.2 %copy-done = f32[2,1024,128]{2,1,0:T(8,128)S(1)} copy-done((f32[2,1024,128]{2,1,0:T(8,128)S(1)}, f32[2,1024,128]{2,1,0:T(8,128)}, u32[]{:S(2)}) %copy-start) | copy-done | bytes 1048600
  1.9 1.0 %convolution_bitcast_fusion = f32[21,1024]{1,0:T(8,128)S(1)} fusion(f32[21,128]{1,0:T(8,128)} %param.8, f32[2,1024,128]{2,1,0:T(8,128)S(1)} %copy-done, s32[]{:T(128)S(6)} %select_n.70), kind=kOutput, calls=%fused_computation | convolution fusion | flops 16515072 | bytes 621060 | tf_op jit(solution)/shard_map/ij,rj->ri/dot_general | solution.py:151
  2.9 3.3 %collective-permute-start = (f32[21,1024]{1,0:T(8,128)S(1)}, f32[21,1024]{1,0:T(8,128)S(1)}, u32[]{:S(2)}, u32[]{:S(2)}) collective-permute-start(f32[21,1024]{1,0:T(8,128)S(1)} %convolution_bitcast_fusion), channel_id=1, source_target_pairs={{0,1},{1,0},{2,3},{3,2},{4,5},{5,4},{6,7},{7,6},{8,9},{9,8},{10,11... | collective-permute-start | bytes 258056 | tf_op jit(solution)/shard_map/ppermute | solution.py:138
  6.2 1.0 %convolution_bitcast_fusion.1 = f32[21,1024]{1,0:T(8,128)S(1)} fusion(f32[21,128]{1,0:T(8,128)} %param.8, f32[2,1024,128]{2,1,0:T(8,128)S(1)} %copy-done, s32[]{:T(128)S(6)} %select_n.69), kind=kOutput, calls=%fused_computation.1 | convolution fusion | flops 16515072 | bytes 621060 | tf_op jit(solution)/shard_map/ij,rj->ri/dot_general | solution.py:151
  7.2 0.0 collective-permute-done
  7.3 0.3 collective-permute-start.4
  7.6 1.0 %collective-permute-start.1 = (f32[21,1024]{1,0:T(8,128)S(1)}, f32[21,1024]{1,0:T(8,128)S(1)}, u32[]{:S(2)}, u32[]{:S(2)}) collective-permute-start(f32[21,1024]{1,0:T(8,128)S(1)} %add.60), channel_id=1, source_target_pairs={{0,2},{1,7},{2,0},{3,5},{4,6},{5,3},{6,4},{7,1},{8,10},{9,15},{10,... | collective-permute-start | bytes 258056 | tf_op jit(solution)/shard_map/ppermute | solution.py:138
  8.6 0.0 collective-permute-start.2
  8.6 2.9 %collective-permute-start.3 = (f32[21,1024]{1,0:T(8,128)S(1)}, f32[21,1024]{1,0:T(8,128)S(1)}, u32[]{:S(2)}, u32[]{:S(2)}) collective-permute-start(f32[21,1024]{1,0:T(8,128)S(1)} %add.60), channel_id=1, source_target_pairs={{0,4},{1,5},{2,6},{3,7},{4,0},{5,1},{6,2},{7,3},{8,12},{9,13},{10,... | collective-permute-start | bytes 258056 | tf_op jit(solution)/shard_map/ppermute | solution.py:138
  11.5 1.3 %select_bitcast_fusion = (f32[128,1024]{1,0:T(8,128)S(1)}, f32[128,1024]{1,0:T(8,128)S(1)}) fusion(f32[2,128,1024]{2,1,0:T(8,128)} %param.10, pred[]{:T(512)S(6)} %ge.2), kind=kLoop, calls=%fused_computation.8 | loop fusion | flops 262144 | bytes 2097153 | tf_op jit(solution)/shard_map/jit(_where)/select_n | solution.py:161
  12.8 1.0 %copy.12 = f32[2,21,1024]{2,1,0:T(8,128)S(1)} copy(f32[2,21,1024]{2,0,1:T(2,128)} %param.9) | data formatting | bytes 344064 | tf_op jit(solution)/shard_map/optimization_barrier | solution.py:167
  13.8 0.0 collective-permute-done.1
  13.8 0.6 collective-permute-start.9
  14.4 0.0 copy-start.1
  14.4 0.0 collective-permute-done.2
  14.4 0.8 %collective-permute-done.3 = f32[21,1024]{1,0:T(8,128)S(1)} collective-permute-done((f32[21,1024]{1,0:T(8,128)S(1)}, f32[21,1024]{1,0:T(8,128)S(1)}, u32[]{:S(2)}, u32[]{:S(2)}) %collective-permute-start.3) | collective-permute-done | bytes 86048 | tf_op jit(solution)/shard_map/ppermute | solution.py:138
  15.3 0.0 collective-permute-done.4
  15.3 0.1 fusion
  15.3 0.4 shard_map.86.own0.block0_ref
  15.8 0.7 collective-permute-start.6
  16.4 3.0 %collective-permute-start.7 = (f32[21,256]{1,0:T(8,128)S(1)}, f32[21,256]{1,0:T(8,128)S(1)}, u32[]{:S(2)}, u32[]{:S(2)}) collective-permute-start(f32[21,256]{1,0:T(8,128)S(1)} %shard_map.86.own0.block0_ref), channel_id=1, source_target_pairs={{0,64},{1,5},{2,66},{3,7},{4,68},{5,1},{6,70},{7,3},{8,72},{9,13},... | collective-permute-start | bytes 64520 | tf_op jit(solution)/shard_map/ppermute | solution.py:138
  19.5 0.3 collective-permute-start.8
  19.7 1.4 %collective-permute-start.5 = (f32[21,256]{1,0:T(8,128)S(1)}, f32[21,256]{1,0:T(8,128)S(1)}, u32[]{:S(2)}, u32[]{:S(2)}) collective-permute-start(f32[21,256]{1,0:T(8,128)S(1)} %constant_dynamic-slice_fusion), channel_id=1, source_target_pairs={{0,1},{1,0},{2,3},{3,2},{4,5},{5,4},{6,7},{7,6},{8,9},{9,8},{10,11... | collective-permute-start | bytes 64520 | tf_op jit(solution)/shard_map/ppermute | solution.py:138
  21.1 0.0 collective-permute-done.9
  21.2 0.8 %collective-permute-done.5.base_ref = f32[21,256]{1,0:T(8,128)S(1)} collective-permute-done((f32[21,256]{1,0:T(8,128)S(1)}, f32[21,256]{1,0:T(8,128)S(1)}, u32[]{:S(2)}, u32[]{:S(2)}) %collective-permute-start.5) | collective-permute-done | bytes 21536 | tf_op jit(solution)/shard_map/ppermute | solution.py:138
  22.0 1.3 %collective-permute-done.8.three0 = f32[21,256]{1,0:T(8,128)S(1)} collective-permute-done((f32[21,256]{1,0:T(8,128)S(1)}, f32[21,256]{1,0:T(8,128)S(1)}, u32[]{:S(2)}, u32[]{:S(2)}) %collective-permute-start.8) | collective-permute-done | bytes 21536 | tf_op jit(solution)/shard_map/ppermute | solution.py:138
  23.4 0.4 shard_map.87.own1
  23.8 0.1 collective-permute-start.10
  23.9 1.4 %collective-permute-start.11 = (f32[21,256]{1,0:T(8,128)S(1)}, f32[21,256]{1,0:T(8,128)S(1)}, u32[]{:S(2)}, u32[]{:S(2)}) collective-permute-start(f32[21,256]{1,0:T(8,128)S(1)} %shard_map.87.own1), channel_id=1, source_target_pairs={{0,64},{1,5},{2,66},{3,7},{4,68},{5,1},{6,70},{7,3},{8,72},{9,13},... | collective-permute-start | bytes 64520 | tf_op jit(solution)/shard_map/ppermute | solution.py:138
  25.3 2.4 %collective-permute-start.12 = (f32[21,256]{1,0:T(8,128)S(1)}, f32[21,256]{1,0:T(8,128)S(1)}, u32[]{:S(2)}, u32[]{:S(2)}) collective-permute-start(f32[21,256]{1,0:T(8,128)S(1)} %shard_map.87.own1), channel_id=1, source_target_pairs={{0,8},{1,7},{2,10},{3,5},{4,12},{5,3},{6,14},{7,1},{8,0},{9,15},{1... | collective-permute-start | bytes 64520 | tf_op jit(solution)/shard_map/ppermute | solution.py:138
  27.7 0.0 collective-permute-done.10.one1
  27.7 0.4 collective-permute-done.11.two1
  28.2 1.0 %collective-permute-done.12.three1 = f32[21,256]{1,0:T(8,128)S(1)} collective-permute-done((f32[21,256]{1,0:T(8,128)S(1)}, f32[21,256]{1,0:T(8,128)S(1)}, u32[]{:S(2)}, u32[]{:S(2)}) %collective-permute-start.12) | collective-permute-done | bytes 21536 | tf_op jit(solution)/shard_map/ppermute | solution.py:138
  29.2 0.4 shard_map.88
  29.6 0.5 collective-permute-start.13
  30.1 2.5 %collective-permute-start.14 = (f32[42,256]{1,0:T(8,128)S(1)}, f32[42,256]{1,0:T(8,128)S(1)}, u32[]{:S(2)}, u32[]{:S(2)}) collective-permute-start(f32[42,256]{1,0:T(8,128)S(1)} %shard_map.88), channel_id=1, source_target_pairs={{0,64},{1,129},{2,66},{3,131},{4,68},{5,133},{6,70},{7,135},{8,72}... | collective-permute-start | bytes 129032 | tf_op jit(solution)/shard_map/ppermute | solution.py:138
  32.6 1.0 %collective-permute-start.15 = (f32[42,256]{1,0:T(8,128)S(1)}, f32[42,256]{1,0:T(8,128)S(1)}, u32[]{:S(2)}, u32[]{:S(2)}) collective-permute-start(f32[42,256]{1,0:T(8,128)S(1)} %shard_map.88), channel_id=1, source_target_pairs={{0,8},{1,193},{2,10},{3,195},{4,12},{5,197},{6,14},{7,199},{8,0},{... | collective-permute-start | bytes 129032 | tf_op jit(solution)/shard_map/ppermute | solution.py:138
  33.6 1.0 %collective-permute-done.14 = f32[42,256]{1,0:T(8,128)S(1)} collective-permute-done((f32[42,256]{1,0:T(8,128)S(1)}, f32[42,256]{1,0:T(8,128)S(1)}, u32[]{:S(2)}, u32[]{:S(2)}) %collective-permute-start.14) | collective-permute-done | bytes 43040 | tf_op jit(solution)/shard_map/ppermute | solution.py:138
  34.6 2.1 %collective-permute-done.15 = f32[42,256]{1,0:T(8,128)S(1)} collective-permute-done((f32[42,256]{1,0:T(8,128)S(1)}, f32[42,256]{1,0:T(8,128)S(1)}, u32[]{:S(2)}, u32[]{:S(2)}) %collective-permute-start.15) | collective-permute-done | bytes 43040 | tf_op jit(solution)/shard_map/ppermute | solution.py:138
  36.8 1.7 %collective-permute-start.16 = (f32[42,256]{1,0:T(8,128)S(1)}, f32[42,256]{1,0:T(8,128)S(1)}, u32[]{:S(2)}, u32[]{:S(2)}) collective-permute-start(f32[42,256]{1,0:T(8,128)S(1)} %add_add_fusion.1), channel_id=1, source_target_pairs={{0,2},{1,9},{2,0},{3,11},{4,6},{5,13},{6,4},{7,15},{8,10},{9,1},{1... | collective-permute-start | bytes 129032 | tf_op jit(solution)/shard_map/ppermute | solution.py:138
  38.5 3.0 %collective-permute-start.17 = (f32[42,256]{1,0:T(8,128)S(1)}, f32[42,256]{1,0:T(8,128)S(1)}, u32[]{:S(2)}, u32[]{:S(2)}) collective-permute-start(f32[42,256]{1,0:T(8,128)S(1)} %add_add_fusion.1), channel_id=1, source_target_pairs={{0,64},{1,17},{2,66},{3,19},{4,68},{5,21},{6,70},{7,23},{8,72},{9,... | collective-permute-start | bytes 129032 | tf_op jit(solution)/shard_map/ppermute | solution.py:138
  41.5 0.1 collective-permute-start.18
  41.6 0.0 collective-permute-done.16
  41.6 1.9 %collective-permute-done.17 = f32[42,256]{1,0:T(8,128)S(1)} collective-permute-done((f32[42,256]{1,0:T(8,128)S(1)}, f32[42,256]{1,0:T(8,128)S(1)}, u32[]{:S(2)}, u32[]{:S(2)}) %collective-permute-start.17) | collective-permute-done | bytes 43040 | tf_op jit(solution)/shard_map/ppermute | solution.py:138
  43.5 2.7 %collective-permute-done.18 = f32[42,256]{1,0:T(8,128)S(1)} collective-permute-done((f32[42,256]{1,0:T(8,128)S(1)}, f32[42,256]{1,0:T(8,128)S(1)}, u32[]{:S(2)}, u32[]{:S(2)}) %collective-permute-start.18) | collective-permute-done | bytes 43040 | tf_op jit(solution)/shard_map/ppermute | solution.py:138
  46.2 1.9 %collective-permute-start.19 = (f32[42,256]{1,0:T(8,128)S(1)}, f32[42,256]{1,0:T(8,128)S(1)}, u32[]{:S(2)}, u32[]{:S(2)}) collective-permute-start(f32[42,256]{1,0:T(8,128)S(1)} %add_add_fusion), channel_id=1, source_target_pairs={{0,2},{1,49},{2,0},{3,51},{4,6},{5,53},{6,4},{7,55},{8,10},{9,57},... | collective-permute-start | bytes 129032 | tf_op jit(solution)/shard_map/ppermute | solution.py:138
  48.2 3.2 %collective-permute-done.19 = f32[42,256]{1,0:T(8,128)S(1)} collective-permute-done((f32[42,256]{1,0:T(8,128)S(1)}, f32[42,256]{1,0:T(8,128)S(1)}, u32[]{:S(2)}, u32[]{:S(2)}) %collective-permute-start.19) | collective-permute-done | bytes 43040 | tf_op jit(solution)/shard_map/ppermute | solution.py:138
  51.4 0.1 collective-permute-start.20
  51.5 1.2 %collective-permute-done.20.refs_2_ = f32[42,128]{1,0:T(8,128)S(1)} collective-permute-done((f32[42,128]{1,0:T(8,128)S(1)}, f32[42,128]{1,0:T(8,128)S(1)}, u32[]{:S(2)}, u32[]{:S(2)}) %collective-permute-start.20) | collective-permute-done | bytes 21536 | tf_op jit(solution)/shard_map/ppermute | solution.py:138
  52.7 0.7 %shard_map.90 = f32[21,2048]{1,0:T(8,128)S(1)} custom-call(s32[1]{0:T(128)} %bitcast.refs_0_.half_ref, f32[42,256]{1,0:T(8,128)S(1)} %add.71.refs_1_, f32[42,128]{1,0:T(8,128)S(1)} %collective-permute-done.20.refs_2_, f32[8192,128]{1,0:T(8,128)S(1)} %bitcast.26), custom_call_target="tpu_custom_call" | custom-call | flops 66060288 | bytes 2097152 | tf_op jit(solution)/shard_map/pallas_call | solution.py:99
  53.4 0.2 collective-permute-start.21
  53.6 0.7 %shard_map.89 = (f32[21,2048]{1,0:T(8,128)S(1)}, f32[42,128]{1,0:T(8,128)S(1)}) custom-call(s32[1]{0:T(128)} %bitcast.refs_0_.half_ref, f32[42,256]{1,0:T(8,128)S(1)} %add.71.refs_1_, f32[42,128]{1,0:T(8,128)S(1)} %collective-permute-done.20.refs_2_, f32[8192,128]{1,0:T(8,128)S(1)} %bitcast.27), custom_call_target="tpu_custom_call" | custom-call | flops 66060288 | bytes 2097152 | tf_op jit(solution)/shard_map/pallas_call | solution.py:99
  54.4 0.5 collective-permute-done.21
  54.9 2.0 %collective-permute-start.22 = (f32[21,2048]{1,0:T(8,128)S(1)}, f32[21,2048]{1,0:T(8,128)S(1)}, u32[]{:S(2)}, u32[]{:S(2)}) collective-permute-start(f32[21,2048]{1,0:T(8,128)S(1)} %add.73), channel_id=1, source_target_pairs={{0,2},{1,7},{2,0},{3,5},{4,6},{5,3},{6,4},{7,1},{8,10},{9,15},{10,... | collective-permute-start | bytes 516104 | tf_op jit(solution)/shard_map/ppermute | solution.py:138
  56.9 3.9 %collective-permute-done.22 = f32[21,2048]{1,0:T(8,128)S(1)} collective-permute-done((f32[21,2048]{1,0:T(8,128)S(1)}, f32[21,2048]{1,0:T(8,128)S(1)}, u32[]{:S(2)}, u32[]{:S(2)}) %collective-permute-start.22) | collective-permute-done | bytes 172064 | tf_op jit(solution)/shard_map/ppermute | solution.py:138
  60.8 0.1 collective-permute-start.23
  60.9 4.8 %collective-permute-done.23 = f32[21,2048]{1,0:T(8,128)S(1)} collective-permute-done((f32[21,2048]{1,0:T(8,128)S(1)}, f32[21,2048]{1,0:T(8,128)S(1)}, u32[]{:S(2)}, u32[]{:S(2)}) %collective-permute-start.23) | collective-permute-done | bytes 172064 | tf_op jit(solution)/shard_map/ppermute | solution.py:138
  65.7 2.3 %collective-permute-start.24 = (f32[21,2048]{1,0:T(8,128)S(1)}, f32[21,2048]{1,0:T(8,128)S(1)}, u32[]{:S(2)}, u32[]{:S(2)}) collective-permute-start(f32[21,2048]{1,0:T(8,128)S(1)} %add_subtract_fusion.value_ref), channel_id=1, source_target_pairs={{0,1},{1,0},{2,3},{3,2},{4,5},{5,4},{6,7},{7,6},{8,9},{9,8},{10,11... | collective-permute-start | bytes 516104 | tf_op jit(solution)/shard_map/ppermute | solution.py:138
  68.0 0.6 copy.13
  68.6 0.7 shard_map.91.rest_0_
  69.3 0.0 collective-permute-done.24.value_ref
  69.3 0.7 shard_map.92
  (20 shorter events, 0.3 us)
Async XLA Ops:
  0.6 1.2 %copy-start = (f32[2,1024,128]{2,1,0:T(8,128)S(1)}, f32[2,1024,128]{2,1,0:T(8,128)}, u32[]{:S(2)}) copy-start(f32[2,1024,128]{2,1,0:T(8,128)} %param.7) | copy-start | bytes 3145732
  0.6 13.7 %copy-start.2 = (f32[128,1024]{1,0:T(8,128)S(1)}, f32[128,1024]{1,0:T(8,128)}, u32[]{:S(2)}) copy-start(f32[128,1024]{1,0:T(8,128)} %param.11) | copy-start | bytes 1572868
  2.9 4.4 %collective-permute-start = (f32[21,1024]{1,0:T(8,128)S(1)}, f32[21,1024]{1,0:T(8,128)S(1)}, u32[]{:S(2)}, u32[]{:S(2)}) collective-permute-start(f32[21,1024]{1,0:T(8,128)S(1)} %convolution_bitcast_fusion), channel_id=1, source_target_pairs={{0,1},{1,0},{2,3},{3,2},{4,5},{5,4},{6,7},{7,6},{8,9},{9,8},{10,11... | collective-permute-start | bytes 258056 | tf_op jit(solution)/shard_map/ppermute | solution.py:138
  7.3 8.0 %collective-permute-start.4 = (f32[2,128,1024]{2,1,0:T(8,128)}, f32[2,128,1024]{2,1,0:T(8,128)S(1)}, u32[]{:S(2)}, u32[]{:S(2)}) collective-permute-start(f32[2,128,1024]{2,1,0:T(8,128)} %param.10), channel_id=1, source_target_pairs={{0,1},{1,0},{2,3},{3,2},{4,5},{5,4},{6,7},{7,6},{8,9},{9,8},{10,11... | collective-permute-start | bytes 3145736 | tf_op jit(solution)/shard_map/ppermute | solution.py:138
  7.6 6.2 %collective-permute-start.1 = (f32[21,1024]{1,0:T(8,128)S(1)}, f32[21,1024]{1,0:T(8,128)S(1)}, u32[]{:S(2)}, u32[]{:S(2)}) collective-permute-start(f32[21,1024]{1,0:T(8,128)S(1)} %add.60), channel_id=1, source_target_pairs={{0,2},{1,7},{2,0},{3,5},{4,6},{5,3},{6,4},{7,1},{8,10},{9,15},{10,... | collective-permute-start | bytes 258056 | tf_op jit(solution)/shard_map/ppermute | solution.py:138
  8.6 5.8 %collective-permute-start.2 = (f32[21,1024]{1,0:T(8,128)S(1)}, f32[21,1024]{1,0:T(8,128)S(1)}, u32[]{:S(2)}, u32[]{:S(2)}) collective-permute-start(f32[21,1024]{1,0:T(8,128)S(1)} %add.60), channel_id=1, source_target_pairs={{0,6},{1,3},{2,4},{3,1},{4,2},{5,7},{6,0},{7,5},{8,14},{9,11},{10,... | collective-permute-start | bytes 258056 | tf_op jit(solution)/shard_map/ppermute | solution.py:138
  8.6 6.6 %collective-permute-start.3 = (f32[21,1024]{1,0:T(8,128)S(1)}, f32[21,1024]{1,0:T(8,128)S(1)}, u32[]{:S(2)}, u32[]{:S(2)}) collective-permute-start(f32[21,1024]{1,0:T(8,128)S(1)} %add.60), channel_id=1, source_target_pairs={{0,4},{1,5},{2,6},{3,7},{4,0},{5,1},{6,2},{7,3},{8,12},{9,13},{10,... | collective-permute-start | bytes 258056 | tf_op jit(solution)/shard_map/ppermute | solution.py:138
  13.8 7.4 %collective-permute-start.9 = (f32[128,1024]{1,0:T(8,128)}, f32[128,1024]{1,0:T(8,128)S(1)}, u32[]{:S(2)}, u32[]{:S(2)}) collective-permute-start(f32[128,1024]{1,0:T(8,128)} %param.11), channel_id=1, source_target_pairs={{0,1},{1,0},{2,3},{3,2},{4,5},{5,4},{6,7},{7,6},{8,9},{9,8},{10,11... | collective-permute-start | bytes 1572872 | tf_op jit(solution)/shard_map/ppermute | solution.py:138
  14.4 38.3 %copy-start.1 = (f32[4096,2,128]{2,1,0:T(2,128)S(1)}, f32[4096,2,128]{2,1,0:T(2,128)}, u32[]{:S(2)}) copy-start(f32[4096,2,128]{2,1,0:T(2,128)} %param.12) | copy-start | bytes 12582916
  15.8 6.2 %collective-permute-start.6 = (f32[21,256]{1,0:T(8,128)S(1)}, f32[21,256]{1,0:T(8,128)S(1)}, u32[]{:S(2)}, u32[]{:S(2)}) collective-permute-start(f32[21,256]{1,0:T(8,128)S(1)} %shard_map.86.own0.block0_ref), channel_id=1, source_target_pairs={{0,2},{1,3},{2,0},{3,1},{4,6},{5,7},{6,4},{7,5},{8,10},{9,11},{10,... | collective-permute-start | bytes 64520 | tf_op jit(solution)/shard_map/ppermute | solution.py:138
  16.4 5.6 %collective-permute-start.7 = (f32[21,256]{1,0:T(8,128)S(1)}, f32[21,256]{1,0:T(8,128)S(1)}, u32[]{:S(2)}, u32[]{:S(2)}) collective-permute-start(f32[21,256]{1,0:T(8,128)S(1)} %shard_map.86.own0.block0_ref), channel_id=1, source_target_pairs={{0,64},{1,5},{2,66},{3,7},{4,68},{5,1},{6,70},{7,3},{8,72},{9,13},... | collective-permute-start | bytes 64520 | tf_op jit(solution)/shard_map/ppermute | solution.py:138
  19.5 3.9 %collective-permute-start.8 = (f32[21,256]{1,0:T(8,128)S(1)}, f32[21,256]{1,0:T(8,128)S(1)}, u32[]{:S(2)}, u32[]{:S(2)}) collective-permute-start(f32[21,256]{1,0:T(8,128)S(1)} %shard_map.86.own0.block0_ref), channel_id=1, source_target_pairs={{0,8},{1,7},{2,10},{3,5},{4,12},{5,3},{6,14},{7,1},{8,0},{9,15},{1... | collective-permute-start | bytes 64520 | tf_op jit(solution)/shard_map/ppermute | solution.py:138
  19.7 2.3 %collective-permute-start.5 = (f32[21,256]{1,0:T(8,128)S(1)}, f32[21,256]{1,0:T(8,128)S(1)}, u32[]{:S(2)}, u32[]{:S(2)}) collective-permute-start(f32[21,256]{1,0:T(8,128)S(1)} %constant_dynamic-slice_fusion), channel_id=1, source_target_pairs={{0,1},{1,0},{2,3},{3,2},{4,5},{5,4},{6,7},{7,6},{8,9},{9,8},{10,11... | collective-permute-start | bytes 64520 | tf_op jit(solution)/shard_map/ppermute | solution.py:138
  23.8 3.9 %collective-permute-start.10 = (f32[21,256]{1,0:T(8,128)S(1)}, f32[21,256]{1,0:T(8,128)S(1)}, u32[]{:S(2)}, u32[]{:S(2)}) collective-permute-start(f32[21,256]{1,0:T(8,128)S(1)} %shard_map.87.own1), channel_id=1, source_target_pairs={{0,2},{1,3},{2,0},{3,1},{4,6},{5,7},{6,4},{7,5},{8,10},{9,11},{10,... | collective-permute-start | bytes 64520 | tf_op jit(solution)/shard_map/ppermute | solution.py:138
  23.9 4.3 %collective-permute-start.11 = (f32[21,256]{1,0:T(8,128)S(1)}, f32[21,256]{1,0:T(8,128)S(1)}, u32[]{:S(2)}, u32[]{:S(2)}) collective-permute-start(f32[21,256]{1,0:T(8,128)S(1)} %shard_map.87.own1), channel_id=1, source_target_pairs={{0,64},{1,5},{2,66},{3,7},{4,68},{5,1},{6,70},{7,3},{8,72},{9,13},... | collective-permute-start | bytes 64520 | tf_op jit(solution)/shard_map/ppermute | solution.py:138
  25.3 3.9 %collective-permute-start.12 = (f32[21,256]{1,0:T(8,128)S(1)}, f32[21,256]{1,0:T(8,128)S(1)}, u32[]{:S(2)}, u32[]{:S(2)}) collective-permute-start(f32[21,256]{1,0:T(8,128)S(1)} %shard_map.87.own1), channel_id=1, source_target_pairs={{0,8},{1,7},{2,10},{3,5},{4,12},{5,3},{6,14},{7,1},{8,0},{9,15},{1... | collective-permute-start | bytes 64520 | tf_op jit(solution)/shard_map/ppermute | solution.py:138
  29.6 3.9 %collective-permute-start.13 = (f32[42,256]{1,0:T(8,128)S(1)}, f32[42,256]{1,0:T(8,128)S(1)}, u32[]{:S(2)}, u32[]{:S(2)}) collective-permute-start(f32[42,256]{1,0:T(8,128)S(1)} %shard_map.88), channel_id=1, source_target_pairs={{0,2},{1,65},{2,0},{3,67},{4,6},{5,69},{6,4},{7,71},{8,10},{9,73},... | collective-permute-start | bytes 129032 | tf_op jit(solution)/shard_map/ppermute | solution.py:138
  30.1 4.5 %collective-permute-start.14 = (f32[42,256]{1,0:T(8,128)S(1)}, f32[42,256]{1,0:T(8,128)S(1)}, u32[]{:S(2)}, u32[]{:S(2)}) collective-permute-start(f32[42,256]{1,0:T(8,128)S(1)} %shard_map.88), channel_id=1, source_target_pairs={{0,64},{1,129},{2,66},{3,131},{4,68},{5,133},{6,70},{7,135},{8,72}... | collective-permute-start | bytes 129032 | tf_op jit(solution)/shard_map/ppermute | solution.py:138
  32.6 4.2 %collective-permute-start.15 = (f32[42,256]{1,0:T(8,128)S(1)}, f32[42,256]{1,0:T(8,128)S(1)}, u32[]{:S(2)}, u32[]{:S(2)}) collective-permute-start(f32[42,256]{1,0:T(8,128)S(1)} %shard_map.88), channel_id=1, source_target_pairs={{0,8},{1,193},{2,10},{3,195},{4,12},{5,197},{6,14},{7,199},{8,0},{... | collective-permute-start | bytes 129032 | tf_op jit(solution)/shard_map/ppermute | solution.py:138
  36.8 4.8 %collective-permute-start.16 = (f32[42,256]{1,0:T(8,128)S(1)}, f32[42,256]{1,0:T(8,128)S(1)}, u32[]{:S(2)}, u32[]{:S(2)}) collective-permute-start(f32[42,256]{1,0:T(8,128)S(1)} %add_add_fusion.1), channel_id=1, source_target_pairs={{0,2},{1,9},{2,0},{3,11},{4,6},{5,13},{6,4},{7,15},{8,10},{9,1},{1... | collective-permute-start | bytes 129032 | tf_op jit(solution)/shard_map/ppermute | solution.py:138
  38.5 5.0 %collective-permute-start.17 = (f32[42,256]{1,0:T(8,128)S(1)}, f32[42,256]{1,0:T(8,128)S(1)}, u32[]{:S(2)}, u32[]{:S(2)}) collective-permute-start(f32[42,256]{1,0:T(8,128)S(1)} %add_add_fusion.1), channel_id=1, source_target_pairs={{0,64},{1,17},{2,66},{3,19},{4,68},{5,21},{6,70},{7,23},{8,72},{9,... | collective-permute-start | bytes 129032 | tf_op jit(solution)/shard_map/ppermute | solution.py:138
  41.5 4.7 %collective-permute-start.18 = (f32[42,256]{1,0:T(8,128)S(1)}, f32[42,256]{1,0:T(8,128)S(1)}, u32[]{:S(2)}, u32[]{:S(2)}) collective-permute-start(f32[42,256]{1,0:T(8,128)S(1)} %add_add_fusion.1), channel_id=1, source_target_pairs={{0,8},{1,25},{2,10},{3,27},{4,12},{5,29},{6,14},{7,31},{8,0},{9,17... | collective-permute-start | bytes 129032 | tf_op jit(solution)/shard_map/ppermute | solution.py:138
  46.2 5.1 %collective-permute-start.19 = (f32[42,256]{1,0:T(8,128)S(1)}, f32[42,256]{1,0:T(8,128)S(1)}, u32[]{:S(2)}, u32[]{:S(2)}) collective-permute-start(f32[42,256]{1,0:T(8,128)S(1)} %add_add_fusion), channel_id=1, source_target_pairs={{0,2},{1,49},{2,0},{3,51},{4,6},{5,53},{6,4},{7,55},{8,10},{9,57},... | collective-permute-start | bytes 129032 | tf_op jit(solution)/shard_map/ppermute | solution.py:138
  51.4 1.3 %collective-permute-start.20 = (f32[42,128]{1,0:T(8,128)S(1)}, f32[42,128]{1,0:T(8,128)S(1)}, u32[]{:S(2)}, u32[]{:S(2)}) collective-permute-start(f32[42,128]{1,0:T(8,128)S(1)} %slice.22), channel_id=1, source_target_pairs={{0,1},{1,0},{2,3},{3,2},{4,5},{5,4},{6,7},{7,6},{8,9},{9,8},{10,11... | collective-permute-start | bytes 64520 | tf_op jit(solution)/shard_map/ppermute | solution.py:138
  52.7 13.0 %copy-start.3 = (f32[21,4096]{1,0:T(8,128)S(1)}, f32[21,4096]{1,0:T(8,128)}, u32[]{:S(2)}) copy-start(f32[21,4096]{1,0:T(8,128)} %param.13) | copy-start | bytes 1032196
  53.4 1.5 %collective-permute-start.21 = (f32[21,2048]{1,0:T(8,128)S(1)}, f32[21,2048]{1,0:T(8,128)S(1)}, u32[]{:S(2)}, u32[]{:S(2)}) collective-permute-start(f32[21,2048]{1,0:T(8,128)S(1)} %shard_map.90), channel_id=1, source_target_pairs={{0,1},{1,0},{2,3},{3,2},{4,5},{5,4},{6,7},{7,6},{8,9},{9,8},{10,11... | collective-permute-start | bytes 516104 | tf_op jit(solution)/shard_map/ppermute | solution.py:138
  54.9 5.8 %collective-permute-start.22 = (f32[21,2048]{1,0:T(8,128)S(1)}, f32[21,2048]{1,0:T(8,128)S(1)}, u32[]{:S(2)}, u32[]{:S(2)}) collective-permute-start(f32[21,2048]{1,0:T(8,128)S(1)} %add.73), channel_id=1, source_target_pairs={{0,2},{1,7},{2,0},{3,5},{4,6},{5,3},{6,4},{7,1},{8,10},{9,15},{10,... | collective-permute-start | bytes 516104 | tf_op jit(solution)/shard_map/ppermute | solution.py:138
  60.8 4.9 %collective-permute-start.23 = (f32[21,2048]{1,0:T(8,128)S(1)}, f32[21,2048]{1,0:T(8,128)S(1)}, u32[]{:S(2)}, u32[]{:S(2)}) collective-permute-start(f32[21,2048]{1,0:T(8,128)S(1)} %add.74), channel_id=1, source_target_pairs={{0,6},{1,3},{2,4},{3,1},{4,2},{5,7},{6,0},{7,5},{8,14},{9,11},{10,... | collective-permute-start | bytes 516104 | tf_op jit(solution)/shard_map/ppermute | solution.py:138
  65.7 3.6 %collective-permute-start.24 = (f32[21,2048]{1,0:T(8,128)S(1)}, f32[21,2048]{1,0:T(8,128)S(1)}, u32[]{:S(2)}, u32[]{:S(2)}) collective-permute-start(f32[21,2048]{1,0:T(8,128)S(1)} %add_subtract_fusion.value_ref), channel_id=1, source_target_pairs={{0,1},{1,0},{2,3},{3,2},{4,5},{5,4},{6,7},{7,6},{8,9},{9,8},{10,11... | collective-permute-start | bytes 516104 | tf_op jit(solution)/shard_map/ppermute | solution.py:138

commit v4 on v3

--- a/solution.py
+++ b/solution.py
@@ -44,7 +44,7 @@
 
 
 def in_order(y, refs):
-    own, one, two, three = [ref[...] for ref in refs]
+    own, two, three, one = [ref[...] for ref in refs]
     blocks = [jnp.where(y == i, own, jnp.where(y == i ^ 1, one, jnp.where(y == i ^ 2, two, three))) for i in range(4)]
     return jnp.concatenate(blocks, 1)
 
@@ -53,13 +53,13 @@
     out_ref[...] = product(reduced_ref[...], rows_of_both(other_ref, own_ref))
 
 
-def second_kernel(y_ref, base_ref, own0, one0, two0, three0, other_ref, own_ref, out_ref):
-    known = in_order(y_ref[0], (own0, one0, two0, three0))
+def second_kernel(y_ref, base_ref, own0, two0, three0, one0, other_ref, own_ref, out_ref):
+    known = in_order(y_ref[0], (own0, two0, three0, one0))
     out_ref[...] = base_ref[...] - product(known, rows_of_both(other_ref, own_ref))
 
 
-def third_kernel(y_ref, block0_ref, own1, one1, two1, three1, other_ref, own_ref, out_ref):
-    known = in_order(y_ref[0], (own1, one1, two1, three1))
+def third_kernel(y_ref, block0_ref, own1, two1, three1, one1, other_ref, own_ref, out_ref):
+    known = in_order(y_ref[0], (own1, two1, three1, one1))
     rows = block0_ref.shape[0]
     out_ref[:rows, :] = block0_ref[...]
     out_ref[rows:, :] = product(known, rows_of_both(other_ref, own_ref))
@@ -150,12 +150,20 @@
     def dot(matrix, value):
         return jnp.einsum("ij,rj->ri", matrix, value, precision=HIGH)
 
-    def among_leaders(value, step):
-        return [swap(value, mask, step * i) for i, mask in ((1, 2), (2, 64), (3, 8))]
-
-    def quad_sum(value, step):
-        one, two, three = among_leaders(value, step)
-        return (value + one) + (two + three)
+    def among_leaders(value, step, mask):
+        return [swap(value, mask, step * i) for i in (2, 3, 1)]
+
+    def from_z(value, source):
+        pairs = [(i, i ^ 2) for i in range(0, 256, 2)]
+        pairs += [((i & ~56) | source(i >> 3 & 7) << 3, i) for i in range(1, 256, 2)]
+        return lax.ppermute(value, both, pairs)
+
+    def z_sum(value):
+        value = value + swap(value, 2, 8)
+        beside = from_z(value, lambda z: (z + 1 if z & 1 else z - 1) & 7)
+        beyond = from_z(value, lambda z: (z - 2 if z & 1 else z + 2) & 7)
+        opposite = from_z(value, lambda z: z ^ 5)
+        return (value + opposite) + (beyond + beside)
 
     def here(value):
         return lax.optimization_barrier(jnp.where(core >= 0, value, 0.0))
@@ -172,19 +180,19 @@
     one, coupling = lax.optimization_barrier((one, coupling))
     couplings = here(swap(coupling, 1)), here(coupling)
     start = jnp.where(row == 0, lax.dynamic_index_in_dim(rhs, 1 - core, 0, keepdims=False), 0.0)
-    reduced = start - ((sums + one) + (two + three))
+    reduced = start - ((three + two) + (one + sums))
     rows, work = reduced.shape[0], (12 * 21 * width * 8 * width, 16 * width * 8 * width)
     shape = (rows, 2 * width)
     (block0,) = local_call(first_kernel, [shape], y, reduced, pinned=inverses0, work=work)
     block0, own1 = lax.optimization_barrier((block0, lanes(reduced, 2 * width * y, 2 * width)))
-    others = among_leaders(block0, 2)
+    others = among_leaders(block0, 2, 64)
     (second,) = local_call(second_kernel, [shape], y, swap(own1, 1), block0, *others, pinned=couplings, work=work)
-    others = among_leaders(second, 2)
+    others = among_leaders(second, 2, 64)
     (solved,) = local_call(third_kernel, [(2 * rows, 2 * width)], y, block0, second, *others, pinned=inverses1, work=work)
-    solved = quad_sum(solved, 64)
+    two, three, one = among_leaders(solved, 64, 2)
+    solved = (two + three) + (one + solved)
     solved, trailing_factor = lax.optimization_barrier((solved, trailing_factor))
-    solved = quad_sum(solved, 8)
-    solved = solved + swap(solved, 2, 48)
+    solved = z_sum(solved)
     taken = swap(solved[:, :width], 1)
 
     factor = trailing_factor.reshape(-1, width)

time: 70.4 us -> 68.1 us (0.967)
  waiting for transfers between devices: 25.8 us -> 21.7 us
  starting transfers between devices: 32.7 us -> 34.5 us
    ppermute x0 -> x3, starting transfers between devices: none -> 9.5 us  [from_z(): return lax.ppermute(value, both, pairs)]
    ppermute x25 -> x22, starting transfers between devices: 32.7 us -> 25 us  [swap(): lax.ppermute(value, both, [(i, i ^ masks[i % 2]) for i in range(256)])]
    ppermute x25 -> x22, waiting for transfers between devices: 25.8 us -> 19.7 us  [swap(): lax.ppermute(value, both, [(i, i ^ masks[i % 2]) for i in range(256)])]
    ppermute x0 -> x3, waiting for transfers between devices: none -> 2 us  [from_z(): return lax.ppermute(value, both, pairs)]
where the time goes in v4:
time: 68.1 us; the launch traced here: 67.8 us
  starting transfers between devices  34.5 us (51%)
  waiting for transfers between devices  21.7 us (32%)
  Pallas kernels  4.1 us (6%)
  local copies, waits for them, and re-layouts  2.84 us (4%)
  matrix products  2.06 us (3%)
  other arithmetic  1.62 us (2%)
  between operations  1.02 us (1%)
    ppermute x22, starting transfers between devices, swap(): lax.ppermute(value, both, [(i, i ^ masks[i % 2]) for i in range(256)])  25 us
    ppermute x22, waiting for transfers between devices, swap(): lax.ppermute(value, both, [(i, i ^ masks[i % 2]) for i in range(256)])  19.7 us
    ppermute x3, starting transfers between devices, from_z(): return lax.ppermute(value, both, pairs)  9.5 us
    dot_general x2, matrix products, dot(): return jnp.einsum('ij,rj->ri', matrix, value, precision=HIGH)  2.06 us
    ppermute x3, waiting for transfers between devices, from_z(): return lax.ppermute(value, both, pairs)  2 us
    unnamed x9, local copies, waits for them, and re-layouts  1.84 us
    select_n x4, other arithmetic, here(): return lax.optimization_barrier(jnp.where(core >= 0, value, 0.0))  1.46 us
    pallas_call x2, Pallas kernels, trailing_products(): pl.pallas_call(lambda *refs: trailing_kernel(own, *refs), in_specs=[pl.Bl...  1.46 us
  transfers between devices with their start and end apart: 25, of which 14 were waited for; matrix products, arithmetic and copies ran while one was open for 6% of the time, Pallas kernels for 3%

profile of v4, /device:TPU:1, one launch (start us, length us, event | category | flops | bytes accessed | tf_op | source)
XLA Modules:
  0.0 67.8 jit_solution(13336242028186481114)
XLA Ops:
  0.6 0.0 copy-start
  0.6 0.0 copy-start.2
  0.7 1.2 %copy-done = f32[2,1024,128]{2,1,0:T(8,128)S(1)} copy-done((f32[2,1024,128]{2,1,0:T(8,128)S(1)}, f32[2,1024,128]{2,1,0:T(8,128)}, u32[]{:S(2)}) %copy-start) | copy-done | bytes 1048600
  1.9 1.0 %convolution_bitcast_fusion = f32[21,1024]{1,0:T(8,128)S(1)} fusion(f32[21,128]{1,0:T(8,128)} %param.8, f32[2,1024,128]{2,1,0:T(8,128)S(1)} %copy-done, s32[]{:T(128)S(6)} %select_n.70), kind=kOutput, calls=%fused_computation | convolution fusion | flops 16515072 | bytes 621060 | tf_op jit(solution)/shard_map/ij,rj->ri/dot_general | solution.py:151
  2.9 3.3 %collective-permute-start = (f32[21,1024]{1,0:T(8,128)S(1)}, f32[21,1024]{1,0:T(8,128)S(1)}, u32[]{:S(2)}, u32[]{:S(2)}) collective-permute-start(f32[21,1024]{1,0:T(8,128)S(1)} %convolution_bitcast_fusion), channel_id=1, source_target_pairs={{0,1},{1,0},{2,3},{3,2},{4,5},{5,4},{6,7},{7,6},{8,9},{9,8},{10,11... | collective-permute-start | bytes 258056 | tf_op jit(solution)/shard_map/ppermute | solution.py:138
  6.2 1.0 %convolution_bitcast_fusion.1 = f32[21,1024]{1,0:T(8,128)S(1)} fusion(f32[21,128]{1,0:T(8,128)} %param.8, f32[2,1024,128]{2,1,0:T(8,128)S(1)} %copy-done, s32[]{:T(128)S(6)} %select_n.69), kind=kOutput, calls=%fused_computation.1 | convolution fusion | flops 16515072 | bytes 621060 | tf_op jit(solution)/shard_map/ij,rj->ri/dot_general | solution.py:151
  7.2 0.0 collective-permute-done
  7.3 0.3 collective-permute-start.4
  7.6 1.0 %collective-permute-start.3 = (f32[21,1024]{1,0:T(8,128)S(1)}, f32[21,1024]{1,0:T(8,128)S(1)}, u32[]{:S(2)}, u32[]{:S(2)}) collective-permute-start(f32[21,1024]{1,0:T(8,128)S(1)} %add.60), channel_id=1, source_target_pairs={{0,2},{1,7},{2,0},{3,5},{4,6},{5,3},{6,4},{7,1},{8,10},{9,15},{10,... | collective-permute-start | bytes 258056 | tf_op jit(solution)/shard_map/ppermute | solution.py:138
  8.6 0.3 collective-permute-start.1
  9.0 1.9 %collective-permute-start.2 = (f32[21,1024]{1,0:T(8,128)S(1)}, f32[21,1024]{1,0:T(8,128)S(1)}, u32[]{:S(2)}, u32[]{:S(2)}) collective-permute-start(f32[21,1024]{1,0:T(8,128)S(1)} %add.60), channel_id=1, source_target_pairs={{0,6},{1,3},{2,4},{3,1},{4,2},{5,7},{6,0},{7,5},{8,14},{9,11},{10,... | collective-permute-start | bytes 258056 | tf_op jit(solution)/shard_map/ppermute | solution.py:138
  10.9 1.3 %select_bitcast_fusion = (f32[128,1024]{1,0:T(8,128)S(1)}, f32[128,1024]{1,0:T(8,128)S(1)}) fusion(f32[2,128,1024]{2,1,0:T(8,128)} %param.10, pred[]{:T(512)S(6)} %ge.2), kind=kLoop, calls=%fused_computation.8 | loop fusion | flops 262144 | bytes 2097153 | tf_op jit(solution)/shard_map/jit(_where)/select_n | solution.py:169
  12.2 1.0 %copy.12 = f32[2,21,1024]{2,1,0:T(8,128)S(1)} copy(f32[2,21,1024]{2,0,1:T(2,128)} %param.9) | data formatting | bytes 344064 | tf_op jit(solution)/shard_map/optimization_barrier | solution.py:175
  13.2 0.0 collective-permute-done.3
  13.2 1.8 %collective-permute-start.9 = (f32[128,1024]{1,0:T(8,128)}, f32[128,1024]{1,0:T(8,128)S(1)}, u32[]{:S(2)}, u32[]{:S(2)}) collective-permute-start(f32[128,1024]{1,0:T(8,128)} %param.11), channel_id=1, source_target_pairs={{0,1},{1,0},{2,3},{3,2},{4,5},{5,4},{6,7},{7,6},{8,9},{9,8},{10,11... | collective-permute-start | bytes 1572872 | tf_op jit(solution)/shard_map/ppermute | solution.py:138
  15.0 0.0 copy-start.1
  15.0 0.2 collective-permute-done.2
  15.3 0.0 collective-permute-done.4
  15.3 0.1 fusion
  15.4 0.4 shard_map.86.own0.block0_ref
  15.8 0.7 collective-permute-start.6
  16.5 2.2 %collective-permute-start.7 = (f32[21,256]{1,0:T(8,128)S(1)}, f32[21,256]{1,0:T(8,128)S(1)}, u32[]{:S(2)}, u32[]{:S(2)}) collective-permute-start(f32[21,256]{1,0:T(8,128)S(1)} %shard_map.86.own0.block0_ref), channel_id=1, source_target_pairs={{0,64},{1,7},{2,66},{3,5},{4,68},{5,3},{6,70},{7,1},{8,72},{9,15},... | collective-permute-start | bytes 64520 | tf_op jit(solution)/shard_map/ppermute | solution.py:138
  18.7 0.0 collective-permute-start.8
  18.7 2.0 %collective-permute-start.5 = (f32[21,256]{1,0:T(8,128)S(1)}, f32[21,256]{1,0:T(8,128)S(1)}, u32[]{:S(2)}, u32[]{:S(2)}) collective-permute-start(f32[21,256]{1,0:T(8,128)S(1)} %constant_dynamic-slice_fusion), channel_id=1, source_target_pairs={{0,1},{1,0},{2,3},{3,2},{4,5},{5,4},{6,7},{7,6},{8,9},{9,8},{10,11... | collective-permute-start | bytes 64520 | tf_op jit(solution)/shard_map/ppermute | solution.py:138
  20.6 0.0 collective-permute-done.9
  20.7 0.8 %collective-permute-done.5.base_ref = f32[21,256]{1,0:T(8,128)S(1)} collective-permute-done((f32[21,256]{1,0:T(8,128)S(1)}, f32[21,256]{1,0:T(8,128)S(1)}, u32[]{:S(2)}, u32[]{:S(2)}) %collective-permute-start.5) | collective-permute-done | bytes 21536 | tf_op jit(solution)/shard_map/ppermute | solution.py:138
  21.5 0.0 collective-permute-done.6.two0
  21.5 0.0 collective-permute-done.7.three0
  21.5 0.0 collective-permute-done.8.one0
  21.5 0.4 shard_map.87.own1
  21.9 0.9 %collective-permute-start.10 = (f32[21,256]{1,0:T(8,128)S(1)}, f32[21,256]{1,0:T(8,128)S(1)}, u32[]{:S(2)}, u32[]{:S(2)}) collective-permute-start(f32[21,256]{1,0:T(8,128)S(1)} %shard_map.87.own1), channel_id=1, source_target_pairs={{0,64},{1,5},{2,66},{3,7},{4,68},{5,1},{6,70},{7,3},{8,72},{9,13},... | collective-permute-start | bytes 64520 | tf_op jit(solution)/shard_map/ppermute | solution.py:138
  22.8 1.7 %collective-permute-start.11 = (f32[21,256]{1,0:T(8,128)S(1)}, f32[21,256]{1,0:T(8,128)S(1)}, u32[]{:S(2)}, u32[]{:S(2)}) collective-permute-start(f32[21,256]{1,0:T(8,128)S(1)} %shard_map.87.own1), channel_id=1, source_target_pairs={{0,64},{1,7},{2,66},{3,5},{4,68},{5,3},{6,70},{7,1},{8,72},{9,15},... | collective-permute-start | bytes 64520 | tf_op jit(solution)/shard_map/ppermute | solution.py:138
  24.6 0.1 collective-permute-start.12
  24.7 1.5 %collective-permute-done.10.two1 = f32[21,256]{1,0:T(8,128)S(1)} collective-permute-done((f32[21,256]{1,0:T(8,128)S(1)}, f32[21,256]{1,0:T(8,128)S(1)}, u32[]{:S(2)}, u32[]{:S(2)}) %collective-permute-start.10) | collective-permute-done | bytes 21536 | tf_op jit(solution)/shard_map/ppermute | solution.py:138
  26.2 0.5 collective-permute-done.11.three1
  26.7 0.5 collective-permute-done.12.one1
  27.2 0.4 shard_map.88
  27.7 2.5 %collective-permute-start.13 = (f32[42,256]{1,0:T(8,128)S(1)}, f32[42,256]{1,0:T(8,128)S(1)}, u32[]{:S(2)}, u32[]{:S(2)}) collective-permute-start(f32[42,256]{1,0:T(8,128)S(1)} %shard_map.88), channel_id=1, source_target_pairs={{0,2},{1,129},{2,0},{3,131},{4,6},{5,133},{6,4},{7,135},{8,10},{9,... | collective-permute-start | bytes 129032 | tf_op jit(solution)/shard_map/ppermute | solution.py:138
  30.1 0.8 %collective-permute-start.14 = (f32[42,256]{1,0:T(8,128)S(1)}, f32[42,256]{1,0:T(8,128)S(1)}, u32[]{:S(2)}, u32[]{:S(2)}) collective-permute-start(f32[42,256]{1,0:T(8,128)S(1)} %shard_map.88), channel_id=1, source_target_pairs={{0,2},{1,193},{2,0},{3,195},{4,6},{5,197},{6,4},{7,199},{8,10},{9,... | collective-permute-start | bytes 129032 | tf_op jit(solution)/shard_map/ppermute | solution.py:138
  30.9 1.3 %collective-permute-done.13 = f32[42,256]{1,0:T(8,128)S(1)} collective-permute-done((f32[42,256]{1,0:T(8,128)S(1)}, f32[42,256]{1,0:T(8,128)S(1)}, u32[]{:S(2)}, u32[]{:S(2)}) %collective-permute-start.13) | collective-permute-done | bytes 43040 | tf_op jit(solution)/shard_map/ppermute | solution.py:138
  32.2 2.1 %collective-permute-done.14 = f32[42,256]{1,0:T(8,128)S(1)} collective-permute-done((f32[42,256]{1,0:T(8,128)S(1)}, f32[42,256]{1,0:T(8,128)S(1)}, u32[]{:S(2)}, u32[]{:S(2)}) %collective-permute-start.14) | collective-permute-done | bytes 43040 | tf_op jit(solution)/shard_map/ppermute | solution.py:138
  34.3 0.0 collective-permute-done.15
  34.3 1.7 %collective-permute-start.16 = (f32[42,256]{1,0:T(8,128)S(1)}, f32[42,256]{1,0:T(8,128)S(1)}, u32[]{:S(2)}, u32[]{:S(2)}) collective-permute-start(f32[42,256]{1,0:T(8,128)S(1)} %add_add_fusion.1), channel_id=1, source_target_pairs={{0,2},{1,9},{2,0},{3,11},{4,6},{5,13},{6,4},{7,15},{8,10},{9,1},{1... | collective-permute-start | bytes 129032 | tf_op jit(solution)/shard_map/ppermute | solution.py:138
  36.0 1.5 %collective-permute-done.16 = f32[42,256]{1,0:T(8,128)S(1)} collective-permute-done((f32[42,256]{1,0:T(8,128)S(1)}, f32[42,256]{1,0:T(8,128)S(1)}, u32[]{:S(2)}, u32[]{:S(2)}) %collective-permute-start.16) | collective-permute-done | bytes 43040 | tf_op jit(solution)/shard_map/ppermute | solution.py:138
  37.5 6.4 %collective-permute-start.17 = (f32[42,256]{1,0:T(8,128)S(1)}, f32[42,256]{1,0:T(8,128)S(1)}, u32[]{:S(2)}, u32[]{:S(2)}) collective-permute-start(f32[42,256]{1,0:T(8,128)S(1)} %add.68), channel_id=1, source_target_pairs={{0,2},{2,0},{4,6},{6,4},{8,10},{10,8},{12,14},{14,12},{16,18},{18,... | collective-permute-start | bytes 129032 | tf_op jit(solution)/shard_map/ppermute | solution.py:159
  43.9 0.3 collective-permute-start.18
  44.2 2.9 %collective-permute-start.19 = (f32[42,256]{1,0:T(8,128)S(1)}, f32[42,256]{1,0:T(8,128)S(1)}, u32[]{:S(2)}, u32[]{:S(2)}) collective-permute-start(f32[42,256]{1,0:T(8,128)S(1)} %add.68), channel_id=1, source_target_pairs={{0,2},{2,0},{4,6},{6,4},{8,10},{10,8},{12,14},{14,12},{16,18},{18,... | collective-permute-start | bytes 129032 | tf_op jit(solution)/shard_map/ppermute | solution.py:159
  47.0 0.0 collective-permute-done.17
  47.0 0.7 %collective-permute-done.18 = f32[42,256]{1,0:T(8,128)S(1)} collective-permute-done((f32[42,256]{1,0:T(8,128)S(1)}, f32[42,256]{1,0:T(8,128)S(1)}, u32[]{:S(2)}, u32[]{:S(2)}) %collective-permute-start.18) | collective-permute-done | bytes 43040 | tf_op jit(solution)/shard_map/ppermute | solution.py:159
  47.7 1.3 %collective-permute-done.19 = f32[42,256]{1,0:T(8,128)S(1)} collective-permute-done((f32[42,256]{1,0:T(8,128)S(1)}, f32[42,256]{1,0:T(8,128)S(1)}, u32[]{:S(2)}, u32[]{:S(2)}) %collective-permute-start.19) | collective-permute-done | bytes 43040 | tf_op jit(solution)/shard_map/ppermute | solution.py:159
  49.0 0.1 collective-permute-start.20
  49.1 1.2 %collective-permute-done.20.refs_2_ = f32[42,128]{1,0:T(8,128)S(1)} collective-permute-done((f32[42,128]{1,0:T(8,128)S(1)}, f32[42,128]{1,0:T(8,128)S(1)}, u32[]{:S(2)}, u32[]{:S(2)}) %collective-permute-start.20) | collective-permute-done | bytes 21536 | tf_op jit(solution)/shard_map/ppermute | solution.py:138
  50.3 0.7 %shard_map.90 = f32[21,2048]{1,0:T(8,128)S(1)} custom-call(s32[1]{0:T(128)} %bitcast.refs_0_.half_ref, f32[42,256]{1,0:T(8,128)S(1)} %add_add_fusion.refs_1_, f32[42,128]{1,0:T(8,128)S(1)} %collective-permute-done.20.refs_2_, f32[8192,128]{1,0:T(8,128)S(1)} %bitcast.26), custom_call_target="tpu_custom_call" | custom-call | flops 66060288 | bytes 2097152 | tf_op jit(solution)/shard_map/pallas_call | solution.py:99
  51.1 0.2 collective-permute-start.21
  51.3 0.7 %shard_map.89 = (f32[21,2048]{1,0:T(8,128)S(1)}, f32[42,128]{1,0:T(8,128)S(1)}) custom-call(s32[1]{0:T(128)} %bitcast.refs_0_.half_ref, f32[42,256]{1,0:T(8,128)S(1)} %add_add_fusion.refs_1_, f32[42,128]{1,0:T(8,128)S(1)} %collective-permute-done.20.refs_2_, f32[8192,128]{1,0:T(8,128)S(1)} %bitcast.27), custom_call_target="tpu_custom_call" | custom-call | flops 66060288 | bytes 2097152 | tf_op jit(solution)/shard_map/pallas_call | solution.py:99
  52.0 0.6 collective-permute-done.21
  52.6 1.2 %collective-permute-start.22 = (f32[21,2048]{1,0:T(8,128)S(1)}, f32[21,2048]{1,0:T(8,128)S(1)}, u32[]{:S(2)}, u32[]{:S(2)}) collective-permute-start(f32[21,2048]{1,0:T(8,128)S(1)} %add.73), channel_id=1, source_target_pairs={{0,2},{1,7},{2,0},{3,5},{4,6},{5,3},{6,4},{7,1},{8,10},{9,15},{10,... | collective-permute-start | bytes 516104 | tf_op jit(solution)/shard_map/ppermute | solution.py:138
  53.8 4.6 %collective-permute-done.22 = f32[21,2048]{1,0:T(8,128)S(1)} collective-permute-done((f32[21,2048]{1,0:T(8,128)S(1)}, f32[21,2048]{1,0:T(8,128)S(1)}, u32[]{:S(2)}, u32[]{:S(2)}) %collective-permute-start.22) | collective-permute-done | bytes 172064 | tf_op jit(solution)/shard_map/ppermute | solution.py:138
  58.4 0.1 collective-permute-start.23
  58.5 4.8 %collective-permute-done.23 = f32[21,2048]{1,0:T(8,128)S(1)} collective-permute-done((f32[21,2048]{1,0:T(8,128)S(1)}, f32[21,2048]{1,0:T(8,128)S(1)}, u32[]{:S(2)}, u32[]{:S(2)}) %collective-permute-start.23) | collective-permute-done | bytes 172064 | tf_op jit(solution)/shard_map/ppermute | solution.py:138
  63.4 2.3 %collective-permute-start.24 = (f32[21,2048]{1,0:T(8,128)S(1)}, f32[21,2048]{1,0:T(8,128)S(1)}, u32[]{:S(2)}, u32[]{:S(2)}) collective-permute-start(f32[21,2048]{1,0:T(8,128)S(1)} %add_subtract_fusion.value_ref), channel_id=1, source_target_pairs={{0,1},{1,0},{2,3},{3,2},{4,5},{5,4},{6,7},{7,6},{8,9},{9,8},{10,11... | collective-permute-start | bytes 516104 | tf_op jit(solution)/shard_map/ppermute | solution.py:138
  65.6 0.6 copy.13
  66.3 0.7 %shard_map.91.rest_0_ = f32[21,4096]{1,0:T(8,128)} custom-call(s32[1]{0:T(128)} %bitcast.refs_0_.half_ref, f32[21,2048]{1,0:T(8,128)S(1)} %add_subtract_fusion.value_ref), custom_call_target="tpu_custom_call" | custom-call | tf_op jit(solution)/shard_map/pallas_call | solution.py:120
  67.0 0.7 %shard_map.92 = f32[21,4096]{1,0:T(8,128)} custom-call(s32[1]{0:T(128)} %bitcast.12.half_ref, f32[21,2048]{1,0:T(8,128)S(1)} %collective-permute-done.24.value_ref, f32[21,4096]{1,0:T(8,128)} %shard_map.91.rest_0_), custom_call_target="tpu_custom_call", output_to_operand_aliasing={{}: (2, {})} | custom-call | tf_op jit(solution)/shard_map/pallas_call | solution.py:120
  (20 shorter events, 0.3 us)
Async XLA Ops:
  0.6 1.2 %copy-start = (f32[2,1024,128]{2,1,0:T(8,128)S(1)}, f32[2,1024,128]{2,1,0:T(8,128)}, u32[]{:S(2)}) copy-start(f32[2,1024,128]{2,1,0:T(8,128)} %param.7) | copy-start | bytes 3145732
  0.6 14.3 %copy-start.2 = (f32[128,1024]{1,0:T(8,128)S(1)}, f32[128,1024]{1,0:T(8,128)}, u32[]{:S(2)}) copy-start(f32[128,1024]{1,0:T(8,128)} %param.11) | copy-start | bytes 1572868
  2.9 4.4 %collective-permute-start = (f32[21,1024]{1,0:T(8,128)S(1)}, f32[21,1024]{1,0:T(8,128)S(1)}, u32[]{:S(2)}, u32[]{:S(2)}) collective-permute-start(f32[21,1024]{1,0:T(8,128)S(1)} %convolution_bitcast_fusion), channel_id=1, source_target_pairs={{0,1},{1,0},{2,3},{3,2},{4,5},{5,4},{6,7},{7,6},{8,9},{9,8},{10,11... | collective-permute-start | bytes 258056 | tf_op jit(solution)/shard_map/ppermute | solution.py:138
  7.3 8.0 %collective-permute-start.4 = (f32[2,128,1024]{2,1,0:T(8,128)}, f32[2,128,1024]{2,1,0:T(8,128)S(1)}, u32[]{:S(2)}, u32[]{:S(2)}) collective-permute-start(f32[2,128,1024]{2,1,0:T(8,128)} %param.10), channel_id=1, source_target_pairs={{0,1},{1,0},{2,3},{3,2},{4,5},{5,4},{6,7},{7,6},{8,9},{9,8},{10,11... | collective-permute-start | bytes 3145736 | tf_op jit(solution)/shard_map/ppermute | solution.py:138
  7.6 5.6 %collective-permute-start.3 = (f32[21,1024]{1,0:T(8,128)S(1)}, f32[21,1024]{1,0:T(8,128)S(1)}, u32[]{:S(2)}, u32[]{:S(2)}) collective-permute-start(f32[21,1024]{1,0:T(8,128)S(1)} %add.60), channel_id=1, source_target_pairs={{0,2},{1,7},{2,0},{3,5},{4,6},{5,3},{6,4},{7,1},{8,10},{9,15},{10,... | collective-permute-start | bytes 258056 | tf_op jit(solution)/shard_map/ppermute | solution.py:138
  8.6 6.4 %collective-permute-start.1 = (f32[21,1024]{1,0:T(8,128)S(1)}, f32[21,1024]{1,0:T(8,128)S(1)}, u32[]{:S(2)}, u32[]{:S(2)}) collective-permute-start(f32[21,1024]{1,0:T(8,128)S(1)} %add.60), channel_id=1, source_target_pairs={{0,4},{1,5},{2,6},{3,7},{4,0},{5,1},{6,2},{7,3},{8,12},{9,13},{10,... | collective-permute-start | bytes 258056 | tf_op jit(solution)/shard_map/ppermute | solution.py:138
  9.0 6.3 %collective-permute-start.2 = (f32[21,1024]{1,0:T(8,128)S(1)}, f32[21,1024]{1,0:T(8,128)S(1)}, u32[]{:S(2)}, u32[]{:S(2)}) collective-permute-start(f32[21,1024]{1,0:T(8,128)S(1)} %add.60), channel_id=1, source_target_pairs={{0,6},{1,3},{2,4},{3,1},{4,2},{5,7},{6,0},{7,5},{8,14},{9,11},{10,... | collective-permute-start | bytes 258056 | tf_op jit(solution)/shard_map/ppermute | solution.py:138
  13.2 7.5 %collective-permute-start.9 = (f32[128,1024]{1,0:T(8,128)}, f32[128,1024]{1,0:T(8,128)S(1)}, u32[]{:S(2)}, u32[]{:S(2)}) collective-permute-start(f32[128,1024]{1,0:T(8,128)} %param.11), channel_id=1, source_target_pairs={{0,1},{1,0},{2,3},{3,2},{4,5},{5,4},{6,7},{7,6},{8,9},{9,8},{10,11... | collective-permute-start | bytes 1572872 | tf_op jit(solution)/shard_map/ppermute | solution.py:138
  15.0 35.3 %copy-start.1 = (f32[4096,2,128]{2,1,0:T(2,128)S(1)}, f32[4096,2,128]{2,1,0:T(2,128)}, u32[]{:S(2)}) copy-start(f32[4096,2,128]{2,1,0:T(2,128)} %param.12) | copy-start | bytes 12582916
  15.8 5.6 %collective-permute-start.6 = (f32[21,256]{1,0:T(8,128)S(1)}, f32[21,256]{1,0:T(8,128)S(1)}, u32[]{:S(2)}, u32[]{:S(2)}) collective-permute-start(f32[21,256]{1,0:T(8,128)S(1)} %shard_map.86.own0.block0_ref), channel_id=1, source_target_pairs={{0,64},{1,5},{2,66},{3,7},{4,68},{5,1},{6,70},{7,3},{8,72},{9,13},... | collective-permute-start | bytes 64520 | tf_op jit(solution)/shard_map/ppermute | solution.py:138
  16.5 5.0 %collective-permute-start.7 = (f32[21,256]{1,0:T(8,128)S(1)}, f32[21,256]{1,0:T(8,128)S(1)}, u32[]{:S(2)}, u32[]{:S(2)}) collective-permute-start(f32[21,256]{1,0:T(8,128)S(1)} %shard_map.86.own0.block0_ref), channel_id=1, source_target_pairs={{0,64},{1,7},{2,66},{3,5},{4,68},{5,3},{6,70},{7,1},{8,72},{9,15},... | collective-permute-start | bytes 64520 | tf_op jit(solution)/shard_map/ppermute | solution.py:138
  18.7 2.8 %collective-permute-start.8 = (f32[21,256]{1,0:T(8,128)S(1)}, f32[21,256]{1,0:T(8,128)S(1)}, u32[]{:S(2)}, u32[]{:S(2)}) collective-permute-start(f32[21,256]{1,0:T(8,128)S(1)} %shard_map.86.own0.block0_ref), channel_id=1, source_target_pairs={{0,64},{1,3},{2,66},{3,1},{4,68},{5,7},{6,70},{7,5},{8,72},{9,11},... | collective-permute-start | bytes 64520 | tf_op jit(solution)/shard_map/ppermute | solution.py:138
  18.7 2.8 %collective-permute-start.5 = (f32[21,256]{1,0:T(8,128)S(1)}, f32[21,256]{1,0:T(8,128)S(1)}, u32[]{:S(2)}, u32[]{:S(2)}) collective-permute-start(f32[21,256]{1,0:T(8,128)S(1)} %constant_dynamic-slice_fusion), channel_id=1, source_target_pairs={{0,1},{1,0},{2,3},{3,2},{4,5},{5,4},{6,7},{7,6},{8,9},{9,8},{10,11... | collective-permute-start | bytes 64520 | tf_op jit(solution)/shard_map/ppermute | solution.py:138
  21.9 4.3 %collective-permute-start.10 = (f32[21,256]{1,0:T(8,128)S(1)}, f32[21,256]{1,0:T(8,128)S(1)}, u32[]{:S(2)}, u32[]{:S(2)}) collective-permute-start(f32[21,256]{1,0:T(8,128)S(1)} %shard_map.87.own1), channel_id=1, source_target_pairs={{0,64},{1,5},{2,66},{3,7},{4,68},{5,1},{6,70},{7,3},{8,72},{9,13},... | collective-permute-start | bytes 64520 | tf_op jit(solution)/shard_map/ppermute | solution.py:138
  22.8 3.9 %collective-permute-start.11 = (f32[21,256]{1,0:T(8,128)S(1)}, f32[21,256]{1,0:T(8,128)S(1)}, u32[]{:S(2)}, u32[]{:S(2)}) collective-permute-start(f32[21,256]{1,0:T(8,128)S(1)} %shard_map.87.own1), channel_id=1, source_target_pairs={{0,64},{1,7},{2,66},{3,5},{4,68},{5,3},{6,70},{7,1},{8,72},{9,15},... | collective-permute-start | bytes 64520 | tf_op jit(solution)/shard_map/ppermute | solution.py:138
  24.6 2.7 %collective-permute-start.12 = (f32[21,256]{1,0:T(8,128)S(1)}, f32[21,256]{1,0:T(8,128)S(1)}, u32[]{:S(2)}, u32[]{:S(2)}) collective-permute-start(f32[21,256]{1,0:T(8,128)S(1)} %shard_map.87.own1), channel_id=1, source_target_pairs={{0,64},{1,3},{2,66},{3,1},{4,68},{5,7},{6,70},{7,5},{8,72},{9,11},... | collective-permute-start | bytes 64520 | tf_op jit(solution)/shard_map/ppermute | solution.py:138
  27.7 4.5 %collective-permute-start.13 = (f32[42,256]{1,0:T(8,128)S(1)}, f32[42,256]{1,0:T(8,128)S(1)}, u32[]{:S(2)}, u32[]{:S(2)}) collective-permute-start(f32[42,256]{1,0:T(8,128)S(1)} %shard_map.88), channel_id=1, source_target_pairs={{0,2},{1,129},{2,0},{3,131},{4,6},{5,133},{6,4},{7,135},{8,10},{9,... | collective-permute-start | bytes 129032 | tf_op jit(solution)/shard_map/ppermute | solution.py:138
  30.1 4.2 %collective-permute-start.14 = (f32[42,256]{1,0:T(8,128)S(1)}, f32[42,256]{1,0:T(8,128)S(1)}, u32[]{:S(2)}, u32[]{:S(2)}) collective-permute-start(f32[42,256]{1,0:T(8,128)S(1)} %shard_map.88), channel_id=1, source_target_pairs={{0,2},{1,193},{2,0},{3,195},{4,6},{5,197},{6,4},{7,199},{8,10},{9,... | collective-permute-start | bytes 129032 | tf_op jit(solution)/shard_map/ppermute | solution.py:138
  30.9 3.4 %collective-permute-start.15 = (f32[42,256]{1,0:T(8,128)S(1)}, f32[42,256]{1,0:T(8,128)S(1)}, u32[]{:S(2)}, u32[]{:S(2)}) collective-permute-start(f32[42,256]{1,0:T(8,128)S(1)} %shard_map.88), channel_id=1, source_target_pairs={{0,2},{1,65},{2,0},{3,67},{4,6},{5,69},{6,4},{7,71},{8,10},{9,73},... | collective-permute-start | bytes 129032 | tf_op jit(solution)/shard_map/ppermute | solution.py:138
  34.3 3.2 %collective-permute-start.16 = (f32[42,256]{1,0:T(8,128)S(1)}, f32[42,256]{1,0:T(8,128)S(1)}, u32[]{:S(2)}, u32[]{:S(2)}) collective-permute-start(f32[42,256]{1,0:T(8,128)S(1)} %add_add_fusion.1), channel_id=1, source_target_pairs={{0,2},{1,9},{2,0},{3,11},{4,6},{5,13},{6,4},{7,15},{8,10},{9,1},{1... | collective-permute-start | bytes 129032 | tf_op jit(solution)/shard_map/ppermute | solution.py:138
  37.5 9.5 %collective-permute-start.17 = (f32[42,256]{1,0:T(8,128)S(1)}, f32[42,256]{1,0:T(8,128)S(1)}, u32[]{:S(2)}, u32[]{:S(2)}) collective-permute-start(f32[42,256]{1,0:T(8,128)S(1)} %add.68), channel_id=1, source_target_pairs={{0,2},{2,0},{4,6},{6,4},{8,10},{10,8},{12,14},{14,12},{16,18},{18,... | collective-permute-start | bytes 129032 | tf_op jit(solution)/shard_map/ppermute | solution.py:159
  43.9 3.8 %collective-permute-start.18 = (f32[42,256]{1,0:T(8,128)S(1)}, f32[42,256]{1,0:T(8,128)S(1)}, u32[]{:S(2)}, u32[]{:S(2)}) collective-permute-start(f32[42,256]{1,0:T(8,128)S(1)} %add.68), channel_id=1, source_target_pairs={{0,2},{2,0},{4,6},{6,4},{8,10},{10,8},{12,14},{14,12},{16,18},{18,... | collective-permute-start | bytes 129032 | tf_op jit(solution)/shard_map/ppermute | solution.py:159
  44.2 4.9 %collective-permute-start.19 = (f32[42,256]{1,0:T(8,128)S(1)}, f32[42,256]{1,0:T(8,128)S(1)}, u32[]{:S(2)}, u32[]{:S(2)}) collective-permute-start(f32[42,256]{1,0:T(8,128)S(1)} %add.68), channel_id=1, source_target_pairs={{0,2},{2,0},{4,6},{6,4},{8,10},{10,8},{12,14},{14,12},{16,18},{18,... | collective-permute-start | bytes 129032 | tf_op jit(solution)/shard_map/ppermute | solution.py:159
  49.0 1.3 %collective-permute-start.20 = (f32[42,128]{1,0:T(8,128)S(1)}, f32[42,128]{1,0:T(8,128)S(1)}, u32[]{:S(2)}, u32[]{:S(2)}) collective-permute-start(f32[42,128]{1,0:T(8,128)S(1)} %slice.22), channel_id=1, source_target_pairs={{0,1},{1,0},{2,3},{3,2},{4,5},{5,4},{6,7},{7,6},{8,9},{9,8},{10,11... | collective-permute-start | bytes 64520 | tf_op jit(solution)/shard_map/ppermute | solution.py:138
  50.3 13.0 %copy-start.3 = (f32[21,4096]{1,0:T(8,128)S(1)}, f32[21,4096]{1,0:T(8,128)}, u32[]{:S(2)}) copy-start(f32[21,4096]{1,0:T(8,128)} %param.13) | copy-start | bytes 1032196
  51.1 1.5 %collective-permute-start.21 = (f32[21,2048]{1,0:T(8,128)S(1)}, f32[21,2048]{1,0:T(8,128)S(1)}, u32[]{:S(2)}, u32[]{:S(2)}) collective-permute-start(f32[21,2048]{1,0:T(8,128)S(1)} %shard_map.90), channel_id=1, source_target_pairs={{0,1},{1,0},{2,3},{3,2},{4,5},{5,4},{6,7},{7,6},{8,9},{9,8},{10,11... | collective-permute-start | bytes 516104 | tf_op jit(solution)/shard_map/ppermute | solution.py:138
  52.6 5.8 %collective-permute-start.22 = (f32[21,2048]{1,0:T(8,128)S(1)}, f32[21,2048]{1,0:T(8,128)S(1)}, u32[]{:S(2)}, u32[]{:S(2)}) collective-permute-start(f32[21,2048]{1,0:T(8,128)S(1)} %add.73), channel_id=1, source_target_pairs={{0,2},{1,7},{2,0},{3,5},{4,6},{5,3},{6,4},{7,1},{8,10},{9,15},{10,... | collective-permute-start | bytes 516104 | tf_op jit(solution)/shard_map/ppermute | solution.py:138
  58.4 4.9 %collective-permute-start.23 = (f32[21,2048]{1,0:T(8,128)S(1)}, f32[21,2048]{1,0:T(8,128)S(1)}, u32[]{:S(2)}, u32[]{:S(2)}) collective-permute-start(f32[21,2048]{1,0:T(8,128)S(1)} %add.74), channel_id=1, source_target_pairs={{0,6},{1,3},{2,4},{3,1},{4,2},{5,7},{6,0},{7,5},{8,14},{9,11},{10,... | collective-permute-start | bytes 516104 | tf_op jit(solution)/shard_map/ppermute | solution.py:138
  63.4 3.6 %collective-permute-start.24 = (f32[21,2048]{1,0:T(8,128)S(1)}, f32[21,2048]{1,0:T(8,128)S(1)}, u32[]{:S(2)}, u32[]{:S(2)}) collective-permute-start(f32[21,2048]{1,0:T(8,128)S(1)} %add_subtract_fusion.value_ref), channel_id=1, source_target_pairs={{0,1},{1,0},{2,3},{3,2},{4,5},{5,4},{6,7},{7,6},{8,9},{9,8},{10,11... | collective-permute-start | bytes 516104 | tf_op jit(solution)/shard_map/ppermute | solution.py:138

commit v5 on v4

--- a/solution.py
+++ b/solution.py
@@ -49,8 +49,23 @@
     return jnp.concatenate(blocks, 1)
 
 
-def first_kernel(y_ref, reduced_ref, other_ref, own_ref, out_ref):
-    out_ref[...] = product(reduced_ref[...], rows_of_both(other_ref, own_ref))
+def pack_kernel(y_ref, kept_ref, taken_ref, out_ref):
+    rows, width = kept_ref.shape[0], out_ref.shape[1]
+    for i in range(kept_ref.shape[1] // width):
+        lanes = pl.ds(width * i, width)
+        out_ref[rows * i : rows * (i + 1), :] = kept_ref[:, lanes] + taken_ref[:, lanes]
+
+
+def first_kernel(y_ref, start_ref, sums_ref, other_ref, own_ref, out_ref, own1_ref):
+    rows, width = start_ref.shape[0], sums_ref.shape[1]
+    blocks = [sums_ref[rows * i : rows * (i + 1), :] for i in range(sums_ref.shape[0] // rows)]
+    reduced = start_ref[...] - jnp.concatenate(blocks, 1)
+    out_ref[...] = product(reduced, rows_of_both(other_ref, own_ref))
+    y, span = y_ref[0], own1_ref.shape[1]
+    own1 = reduced[:, :span]
+    for i in range(1, reduced.shape[1] // span):
+        own1 = jnp.where(y == i, reduced[:, span * i : span * (i + 1)], own1)
+    own1_ref[...] = own1
 
 
 def second_kernel(y_ref, base_ref, own0, two0, three0, one0, other_ref, own_ref, out_ref):
@@ -73,7 +88,8 @@
     solved = unknowns(core_ref, leader_ref, taken_ref)
     if own:
         solved_ref[0][...] = solved
-    rhs, count = out_ref.shape
+    rhs, width = solved.shape[0] // 2, solved.shape[1]
+    count = out_ref.shape[0] // rhs * width
     pad = -rhs % 8
     solved = jnp.concatenate([solved[:rhs], solved[rhs:]], 1)
     solved = jnp.concatenate([solved, jnp.zeros((pad, solved.shape[1]), jnp.float32)], 0)
@@ -87,13 +103,16 @@
         heads, tails = head_and_tail(jnp.concatenate(block, 1))
         main = lax.dot_general(both, heads, NT, preferred_element_type=jnp.float32)
         side = lax.dot_general(head, tails, NT, preferred_element_type=jnp.float32)
-        out_ref[:, size * i : size * (i + 1)] = main[:rhs] + (main[rhs + pad : 2 * rhs + pad] + side[:rhs])
+        sums = main[:rhs] + (main[rhs + pad : 2 * rhs + pad] + side[:rhs])
+        for j in range(size // width):
+            first = rhs * (size // width * i + j)
+            out_ref[first : first + rhs, :] = sums[:, width * j : width * (j + 1)]
 
 
 def trailing_products(own, factor, leader, taken, core):
     count, rhs, width = factor.shape[0] // 4, taken.shape[0] // 2, factor.shape[1]
     vmem = pl.BlockSpec(memory_space=pltpu.VMEM)
-    out_shape = [jax.ShapeDtypeStruct((rhs, count), jnp.float32)]
+    out_shape = [jax.ShapeDtypeStruct((count // width * rhs, width), jnp.float32)]
     if own:
         out_shape.append(jax.ShapeDtypeStruct(taken.shape, jnp.float32))
     return pl.pallas_call(
@@ -106,25 +125,31 @@
     )(core.reshape(1), leader, taken, pltpu.with_memory_space_constraint(factor, pltpu.VMEM))
 
 
-def place_kernel(half_ref, value_ref, *rest):
-    out_ref, sem = rest[-2:]
-    count = value_ref.shape[1]
+def place_kernel(half_ref, value_ref, base_ref, *rest):
+    out_ref, held, sem = rest[-3:]
+    rhs, count = held.shape
+    width = value_ref.shape[1]
     start = pl.multiple_of(half_ref[0] * count, count)
-    copy = pltpu.make_async_copy(value_ref, out_ref.at[:, pl.ds(start, count)], sem)
+    for j in range(count // width):
+        lanes = pl.ds(pl.multiple_of(start + width * j, width), width)
+        held[:, width * j : width * (j + 1)] = base_ref[:, lanes] - value_ref[rhs * j : rhs * (j + 1), :]
+    copy = pltpu.make_async_copy(held, out_ref.at[:, pl.ds(start, count)], sem)
     copy.start()
     copy.wait()
 
 
-def place(half, value, *target):
+def place(half, value, base, *target):
     vmem, anywhere = pl.BlockSpec(memory_space=pltpu.VMEM), pl.BlockSpec(memory_space=pl.ANY)
+    value, base = (pltpu.with_memory_space_constraint(array, pltpu.VMEM) for array in (value, base))
     return pl.pallas_call(
         place_kernel,
-        in_specs=[pl.BlockSpec(memory_space=pltpu.SMEM), vmem] + [anywhere] * len(target),
+        in_specs=[pl.BlockSpec(memory_space=pltpu.SMEM), vmem, vmem] + [anywhere] * len(target),
         out_specs=anywhere,
-        out_shape=jax.ShapeDtypeStruct((value.shape[0], 2 * value.shape[1]), jnp.float32),
-        scratch_shapes=[pltpu.SemaphoreType.DMA],
-        input_output_aliases={2: 0} if target else {},
-    )(half.reshape(1), pltpu.with_memory_space_constraint(value, pltpu.VMEM), *target)
+        out_shape=jax.ShapeDtypeStruct(base.shape, jnp.float32),
+        scratch_shapes=[pltpu.VMEM((base.shape[0], base.shape[1] // 2), jnp.float32), pltpu.SemaphoreType.DMA],
+        input_output_aliases={3: 0} if target else {},
+        compiler_params=pltpu.CompilerParams(vmem_limit_bytes=8 * 2**20),
+    )(half.reshape(1), value, base, *target)
 
 
 def local(prev_factor, prev_solved, rhs, inverses, coupling, trailing_factor, trailing_rhs):
@@ -138,8 +163,8 @@
         return lax.ppermute(value, both, [(i, i ^ masks[i % 2]) for i in range(256)])
 
     def y_sum(value):
-        value = value + swap(value, 2, 6)
-        return value + swap(value, 6, 2)
+        one, two, three = swap(value, 2, 6), swap(value, 6, 2), swap(value, 4)
+        return (three + two) + (one + value)
 
     def lanes(value, start, size):
         return lax.dynamic_slice_in_dim(value, start, size, value.ndim - 1)
@@ -172,7 +197,9 @@
     taken = swap(given, 1)
     kept = dot(lax.dynamic_index_in_dim(prev_factor, 1 - core, 0, keepdims=False), prev_solved)
     kept = lax.optimization_barrier(kept)
-    sums, inverses, coupling, rhs = lax.optimization_barrier((kept + taken, inverses, coupling, rhs))
+    rows = prev_solved.shape[0]
+    (sums,) = local_call(pack_kernel, [(8 * rows, width)], y, pinned=(kept, taken))
+    sums, inverses, coupling, rhs = lax.optimization_barrier((sums, inverses, coupling, rhs))
     other_inverses = swap(inverses, 1)
     inverses0 = here(other_inverses[0]), here(inverses[0])
     inverses1 = here(other_inverses[1]), here(inverses[1])
@@ -180,11 +207,11 @@
     one, coupling = lax.optimization_barrier((one, coupling))
     couplings = here(swap(coupling, 1)), here(coupling)
     start = jnp.where(row == 0, lax.dynamic_index_in_dim(rhs, 1 - core, 0, keepdims=False), 0.0)
-    reduced = start - ((three + two) + (one + sums))
-    rows, work = reduced.shape[0], (12 * 21 * width * 8 * width, 16 * width * 8 * width)
+    sums = (three + two) + (one + sums)
+    work = (12 * 21 * width * 8 * width, 16 * width * 8 * width)
     shape = (rows, 2 * width)
-    (block0,) = local_call(first_kernel, [shape], y, reduced, pinned=inverses0, work=work)
-    block0, own1 = lax.optimization_barrier((block0, lanes(reduced, 2 * width * y, 2 * width)))
+    block0, own1 = local_call(first_kernel, [shape, shape], y, start, sums, pinned=inverses0, work=work)
+    block0, own1 = lax.optimization_barrier((block0, own1))
     others = among_leaders(block0, 2, 64)
     (second,) = local_call(second_kernel, [shape], y, swap(own1, 1), block0, *others, pinned=couplings, work=work)
     others = among_leaders(second, 2, 64)
@@ -199,9 +226,7 @@
     (other,) = trailing_products(False, factor, solved, taken, core)
     mine, solved = trailing_products(True, factor, solved, taken, core)
     mine = y_sum(mine + swap(other, 1))
-    half = mine.shape[1]
-    mine = lanes(trailing_rhs, core * half, half) - mine
-    updated = place(1 - core, swap(mine, 1), place(core, mine))
+    updated = place(1 - core, swap(mine, 1), trailing_rhs, place(core, mine, trailing_rhs))
     return (solved.reshape(2, -1, width), updated)
 
 

time: 68.1 us -> 66.6 us (0.978)
  waiting for transfers between devices: 21.7 us -> 19.8 us
    ppermute x22 -> x23, waiting for transfers between devices: 19.7 us -> 17.8 us  [swap(): lax.ppermute(value, both, [(i, i ^ masks[i % 2]) for i in range(256)])]
    ppermute x22 -> x23, starting transfers between devices: 25 us -> 25.4 us  [swap(): lax.ppermute(value, both, [(i, i ^ masks[i % 2]) for i in range(256)])]
  transfers between devices with their start and end apart: 25 -> 26, of which waited for: 14 -> 14; matrix products, arithmetic and copies ran while one was open for 6% -> 6% of each run, Pallas kernels for 3% -> 3%
where the time goes in v5:
time: 66.6 us; the launch traced here: 66.3 us
  starting transfers between devices  34.9 us (52%)
  waiting for transfers between devices  19.8 us (30%)
  Pallas kernels  4.2 us (6%)
  local copies, waits for them, and re-layouts  2.83 us (4%)
  matrix products  2.06 us (3%)
  other arithmetic  1.63 us (2%)
  between operations  1.01 us (2%)
    ppermute x23, starting transfers between devices, swap(): lax.ppermute(value, both, [(i, i ^ masks[i % 2]) for i in range(256)])  25.4 us
    ppermute x23, waiting for transfers between devices, swap(): lax.ppermute(value, both, [(i, i ^ masks[i % 2]) for i in range(256)])  17.8 us
    ppermute x3, starting transfers between devices, from_z(): return lax.ppermute(value, both, pairs)  9.5 us
    dot_general x2, matrix products, dot(): return jnp.einsum('ij,rj->ri', matrix, value, precision=HIGH)  2.06 us
    ppermute x3, waiting for transfers between devices, from_z(): return lax.ppermute(value, both, pairs)  2 us
    unnamed x9, local copies, waits for them, and re-layouts  1.84 us
    select_n x4, other arithmetic, here(): return lax.optimization_barrier(jnp.where(core >= 0, value, 0.0))  1.48 us
    pallas_call x2, Pallas kernels, trailing_products(): pl.pallas_call(lambda *refs: trailing_kernel(own, *refs), in_specs=[pl.Bl...  1.46 us
  transfers between devices with their start and end apart: 26, of which 14 were waited for; matrix products, arithmetic and copies ran while one was open for 6% of the time, Pallas kernels for 3%

profile of v5, /device:TPU:1, one launch (start us, length us, event | category | flops | bytes accessed | tf_op | source)
XLA Modules:
  0.0 66.3 jit_solution(10677010667496181459)
XLA Ops:
  0.6 0.0 copy-start
  0.7 1.2 %copy-done = f32[2,1024,128]{2,1,0:T(8,128)S(1)} copy-done((f32[2,1024,128]{2,1,0:T(8,128)S(1)}, f32[2,1024,128]{2,1,0:T(8,128)}, u32[]{:S(2)}) %copy-start) | copy-done | bytes 1048600
  1.9 1.0 %convolution_bitcast_fusion = f32[21,1024]{1,0:T(8,128)S(1)} fusion(f32[21,128]{1,0:T(8,128)} %param.8, f32[2,1024,128]{2,1,0:T(8,128)S(1)} %copy-done, s32[]{:T(128)S(6)} %select_n.63), kind=kOutput, calls=%fused_computation | convolution fusion | flops 16515072 | bytes 621060 | tf_op jit(solution)/shard_map/ij,rj->ri/dot_general | solution.py:176
  2.9 3.3 %collective-permute-start = (f32[21,1024]{1,0:T(8,128)S(1)}, f32[21,1024]{1,0:T(8,128)S(1)}, u32[]{:S(2)}, u32[]{:S(2)}) collective-permute-start(f32[21,1024]{1,0:T(8,128)S(1)} %convolution_bitcast_fusion), channel_id=1, source_target_pairs={{0,1},{1,0},{2,3},{3,2},{4,5},{5,4},{6,7},{7,6},{8,9},{9,8},{10,11... | collective-permute-start | bytes 258056 | tf_op jit(solution)/shard_map/ppermute | solution.py:163
  6.2 1.0 %convolution_bitcast_fusion.1.kept_ref = f32[21,1024]{1,0:T(8,128)S(1)} fusion(f32[21,128]{1,0:T(8,128)} %param.8, f32[2,1024,128]{2,1,0:T(8,128)S(1)} %copy-done, s32[]{:T(128)S(6)} %select_n.62), kind=kOutput, calls=%fused_computation.1 | convolution fusion | flops 16515072 | bytes 621060 | tf_op jit(solution)/shard_map/ij,rj->ri/dot_general | solution.py:176
  7.2 0.0 collective-permute-done.taken_ref
  7.3 0.3 collective-permute-start.4
  7.6 1.0 %collective-permute-start.3 = (f32[168,128]{1,0:T(8,128)S(1)}, f32[168,128]{1,0:T(8,128)S(1)}, u32[]{:S(2)}, u32[]{:S(2)}) collective-permute-start(f32[168,128]{1,0:T(8,128)S(1)} %shard_map.86), channel_id=1, source_target_pairs={{0,2},{1,7},{2,0},{3,5},{4,6},{5,3},{6,4},{7,1},{8,10},{9,15},{10,... | collective-permute-start | bytes 258056 | tf_op jit(solution)/shard_map/ppermute | solution.py:163
  8.6 0.3 collective-permute-start.1
  9.0 1.9 %collective-permute-start.2 = (f32[168,128]{1,0:T(8,128)S(1)}, f32[168,128]{1,0:T(8,128)S(1)}, u32[]{:S(2)}, u32[]{:S(2)}) collective-permute-start(f32[168,128]{1,0:T(8,128)S(1)} %shard_map.86), channel_id=1, source_target_pairs={{0,6},{1,3},{2,4},{3,1},{4,2},{5,7},{6,0},{7,5},{8,14},{9,11},{10,... | collective-permute-start | bytes 258056 | tf_op jit(solution)/shard_map/ppermute | solution.py:163
  10.9 1.0 %copy.12 = f32[2,21,1024]{2,1,0:T(8,128)S(1)} copy(f32[2,21,1024]{2,0,1:T(2,128)} %param.9) | data formatting | bytes 344064 | tf_op jit(solution)/shard_map/optimization_barrier | solution.py:202
  11.9 1.3 %select_bitcast_fusion = (f32[128,1024]{1,0:T(8,128)S(1)}, f32[128,1024]{1,0:T(8,128)S(1)}) fusion(f32[2,128,1024]{2,1,0:T(8,128)} %param.10, pred[]{:T(512)S(6)} %ge.2), kind=kLoop, calls=%fused_computation.8 | loop fusion | flops 262144 | bytes 2097153 | tf_op jit(solution)/shard_map/jit(_where)/select_n | solution.py:194
  13.2 0.0 collective-permute-done.3
  13.2 1.8 %collective-permute-start.9 = (f32[128,1024]{1,0:T(8,128)S(1)}, f32[128,1024]{1,0:T(8,128)S(1)}, u32[]{:S(2)}, u32[]{:S(2)}) collective-permute-start(f32[128,1024]{1,0:T(8,128)S(1)} %copy-done.3), channel_id=1, source_target_pairs={{0,1},{1,0},{2,3},{3,2},{4,5},{5,4},{6,7},{7,6},{8,9},{9,8},{10,11... | collective-permute-start | bytes 1572872 | tf_op jit(solution)/shard_map/ppermute | solution.py:163
  15.0 0.0 copy-start.1
  15.1 0.0 collective-permute-done.1
  15.1 0.0 collective-permute-done.4
  15.1 0.1 fusion
  15.2 0.4 shard_map.87
  15.7 0.6 collective-permute-start.6
  16.2 2.2 %collective-permute-start.7 = (f32[21,256]{1,0:T(8,128)S(1)}, f32[21,256]{1,0:T(8,128)S(1)}, u32[]{:S(2)}, u32[]{:S(2)}) collective-permute-start(f32[21,256]{1,0:T(8,128)S(1)} %get-tuple-element.19.own0.block0_ref), channel_id=1, source_target_pairs={{0,64},{1,7},{2,66},{3,5},{4,68},{5,3},{6,70},{7,1},{8,72},{9,15},... | collective-permute-start | bytes 64520 | tf_op jit(solution)/shard_map/ppermute | solution.py:163
  18.4 2.1 %collective-permute-start.5 = (f32[21,256]{1,0:T(8,128)S(1)}, f32[21,256]{1,0:T(8,128)S(1)}, u32[]{:S(2)}, u32[]{:S(2)}) collective-permute-start(f32[21,256]{1,0:T(8,128)S(1)} %get-tuple-element.20), channel_id=1, source_target_pairs={{0,1},{1,0},{2,3},{3,2},{4,5},{5,4},{6,7},{7,6},{8,9},{9,8},{10,11... | collective-permute-start | bytes 64520 | tf_op jit(solution)/shard_map/ppermute | solution.py:163
  20.5 0.0 collective-permute-done.9
  20.5 0.8 %collective-permute-done.5.base_ref = f32[21,256]{1,0:T(8,128)S(1)} collective-permute-done((f32[21,256]{1,0:T(8,128)S(1)}, f32[21,256]{1,0:T(8,128)S(1)}, u32[]{:S(2)}, u32[]{:S(2)}) %collective-permute-start.5) | collective-permute-done | bytes 21536 | tf_op jit(solution)/shard_map/ppermute | solution.py:163
  21.3 0.0 collective-permute-done.6.two0
  21.3 0.0 collective-permute-done.7.three0
  21.3 0.0 collective-permute-done.8.one0
  21.4 0.4 shard_map.88.own1
  21.8 0.7 %collective-permute-start.10 = (f32[21,256]{1,0:T(8,128)S(1)}, f32[21,256]{1,0:T(8,128)S(1)}, u32[]{:S(2)}, u32[]{:S(2)}) collective-permute-start(f32[21,256]{1,0:T(8,128)S(1)} %shard_map.88.own1), channel_id=1, source_target_pairs={{0,64},{1,5},{2,66},{3,7},{4,68},{5,1},{6,70},{7,3},{8,72},{9,13},... | collective-permute-start | bytes 64520 | tf_op jit(solution)/shard_map/ppermute | solution.py:163
  22.5 1.7 %collective-permute-start.11 = (f32[21,256]{1,0:T(8,128)S(1)}, f32[21,256]{1,0:T(8,128)S(1)}, u32[]{:S(2)}, u32[]{:S(2)}) collective-permute-start(f32[21,256]{1,0:T(8,128)S(1)} %shard_map.88.own1), channel_id=1, source_target_pairs={{0,64},{1,7},{2,66},{3,5},{4,68},{5,3},{6,70},{7,1},{8,72},{9,15},... | collective-permute-start | bytes 64520 | tf_op jit(solution)/shard_map/ppermute | solution.py:163
  24.2 0.3 collective-permute-start.12
  24.5 1.5 %collective-permute-done.10.two1 = f32[21,256]{1,0:T(8,128)S(1)} collective-permute-done((f32[21,256]{1,0:T(8,128)S(1)}, f32[21,256]{1,0:T(8,128)S(1)}, u32[]{:S(2)}, u32[]{:S(2)}) %collective-permute-start.10) | collective-permute-done | bytes 21536 | tf_op jit(solution)/shard_map/ppermute | solution.py:163
  26.1 0.3 collective-permute-done.11.three1
  26.4 0.5 collective-permute-done.12.one1
  26.9 0.4 shard_map.89
  27.3 2.1 %collective-permute-start.13 = (f32[42,256]{1,0:T(8,128)S(1)}, f32[42,256]{1,0:T(8,128)S(1)}, u32[]{:S(2)}, u32[]{:S(2)}) collective-permute-start(f32[42,256]{1,0:T(8,128)S(1)} %shard_map.89), channel_id=1, source_target_pairs={{0,2},{1,129},{2,0},{3,131},{4,6},{5,133},{6,4},{7,135},{8,10},{9,... | collective-permute-start | bytes 129032 | tf_op jit(solution)/shard_map/ppermute | solution.py:163
  29.5 0.9 %collective-permute-start.14 = (f32[42,256]{1,0:T(8,128)S(1)}, f32[42,256]{1,0:T(8,128)S(1)}, u32[]{:S(2)}, u32[]{:S(2)}) collective-permute-start(f32[42,256]{1,0:T(8,128)S(1)} %shard_map.89), channel_id=1, source_target_pairs={{0,2},{1,193},{2,0},{3,195},{4,6},{5,197},{6,4},{7,199},{8,10},{9,... | collective-permute-start | bytes 129032 | tf_op jit(solution)/shard_map/ppermute | solution.py:163
  30.3 0.0 collective-permute-start.15
  30.3 1.5 %collective-permute-done.13 = f32[42,256]{1,0:T(8,128)S(1)} collective-permute-done((f32[42,256]{1,0:T(8,128)S(1)}, f32[42,256]{1,0:T(8,128)S(1)}, u32[]{:S(2)}, u32[]{:S(2)}) %collective-permute-start.13) | collective-permute-done | bytes 43040 | tf_op jit(solution)/shard_map/ppermute | solution.py:163
  31.9 1.8 %collective-permute-done.14 = f32[42,256]{1,0:T(8,128)S(1)} collective-permute-done((f32[42,256]{1,0:T(8,128)S(1)}, f32[42,256]{1,0:T(8,128)S(1)}, u32[]{:S(2)}, u32[]{:S(2)}) %collective-permute-start.14) | collective-permute-done | bytes 43040 | tf_op jit(solution)/shard_map/ppermute | solution.py:163
  33.6 1.7 %collective-permute-start.16 = (f32[42,256]{1,0:T(8,128)S(1)}, f32[42,256]{1,0:T(8,128)S(1)}, u32[]{:S(2)}, u32[]{:S(2)}) collective-permute-start(f32[42,256]{1,0:T(8,128)S(1)} %add_add_fusion.3), channel_id=1, source_target_pairs={{0,2},{1,9},{2,0},{3,11},{4,6},{5,13},{6,4},{7,15},{8,10},{9,1},{1... | collective-permute-start | bytes 129032 | tf_op jit(solution)/shard_map/ppermute | solution.py:163
  35.4 1.5 %collective-permute-done.16 = f32[42,256]{1,0:T(8,128)S(1)} collective-permute-done((f32[42,256]{1,0:T(8,128)S(1)}, f32[42,256]{1,0:T(8,128)S(1)}, u32[]{:S(2)}, u32[]{:S(2)}) %collective-permute-start.16) | collective-permute-done | bytes 43040 | tf_op jit(solution)/shard_map/ppermute | solution.py:163
  36.8 6.4 %collective-permute-start.17 = (f32[42,256]{1,0:T(8,128)S(1)}, f32[42,256]{1,0:T(8,128)S(1)}, u32[]{:S(2)}, u32[]{:S(2)}) collective-permute-start(f32[42,256]{1,0:T(8,128)S(1)} %add.60), channel_id=1, source_target_pairs={{0,2},{2,0},{4,6},{6,4},{8,10},{10,8},{12,14},{14,12},{16,18},{18,... | collective-permute-start | bytes 129032 | tf_op jit(solution)/shard_map/ppermute | solution.py:184
  43.2 0.3 collective-permute-start.18
  43.5 2.9 %collective-permute-start.19 = (f32[42,256]{1,0:T(8,128)S(1)}, f32[42,256]{1,0:T(8,128)S(1)}, u32[]{:S(2)}, u32[]{:S(2)}) collective-permute-start(f32[42,256]{1,0:T(8,128)S(1)} %add.60), channel_id=1, source_target_pairs={{0,2},{2,0},{4,6},{6,4},{8,10},{10,8},{12,14},{14,12},{16,18},{18,... | collective-permute-start | bytes 129032 | tf_op jit(solution)/shard_map/ppermute | solution.py:184
  46.4 0.7 %collective-permute-done.18 = f32[42,256]{1,0:T(8,128)S(1)} collective-permute-done((f32[42,256]{1,0:T(8,128)S(1)}, f32[42,256]{1,0:T(8,128)S(1)}, u32[]{:S(2)}, u32[]{:S(2)}) %collective-permute-start.18) | collective-permute-done | bytes 43040 | tf_op jit(solution)/shard_map/ppermute | solution.py:184
  47.1 1.3 %collective-permute-done.19 = f32[42,256]{1,0:T(8,128)S(1)} collective-permute-done((f32[42,256]{1,0:T(8,128)S(1)}, f32[42,256]{1,0:T(8,128)S(1)}, u32[]{:S(2)}, u32[]{:S(2)}) %collective-permute-start.19) | collective-permute-done | bytes 43040 | tf_op jit(solution)/shard_map/ppermute | solution.py:184
  48.4 0.1 collective-permute-start.20
  48.5 1.2 %collective-permute-done.20.refs_2_ = f32[42,128]{1,0:T(8,128)S(1)} collective-permute-done((f32[42,128]{1,0:T(8,128)S(1)}, f32[42,128]{1,0:T(8,128)S(1)}, u32[]{:S(2)}, u32[]{:S(2)}) %collective-permute-start.20) | collective-permute-done | bytes 21536 | tf_op jit(solution)/shard_map/ppermute | solution.py:163
  49.7 0.7 %shard_map.91 = f32[336,128]{1,0:T(8,128)S(1)} custom-call(s32[1]{0:T(128)} %bitcast.refs_0_.half_ref, f32[42,256]{1,0:T(8,128)S(1)} %add_add_fusion.2.refs_1_, f32[42,128]{1,0:T(8,128)S(1)} %collective-permute-done.20.refs_2_, f32[8192,128]{1,0:T(8,128)S(1)} %bitcast.26), custom_call_target="tpu_custom_call" | custom-call | flops 66060288 | bytes 2097152 | tf_op jit(solution)/shard_map/pallas_call | solution.py:118
  50.4 0.2 collective-permute-start.21
  50.6 0.7 %shard_map.90 = (f32[336,128]{1,0:T(8,128)S(1)}, f32[42,128]{1,0:T(8,128)S(1)}) custom-call(s32[1]{0:T(128)} %bitcast.refs_0_.half_ref, f32[42,256]{1,0:T(8,128)S(1)} %add_add_fusion.2.refs_1_, f32[42,128]{1,0:T(8,128)S(1)} %collective-permute-done.20.refs_2_, f32[8192,128]{1,0:T(8,128)S(1)} %bitcast.27), custom_call_target="tpu_custom_call" | custom-call | flops 66060288 | bytes 2097152 | tf_op jit(solution)/shard_map/pallas_call | solution.py:118
  51.3 0.5 collective-permute-done.21
  51.9 1.9 %collective-permute-start.22 = (f32[336,128]{1,0:T(8,128)S(1)}, f32[336,128]{1,0:T(8,128)S(1)}, u32[]{:S(2)}, u32[]{:S(2)}) collective-permute-start(f32[336,128]{1,0:T(8,128)S(1)} %add.64), channel_id=1, source_target_pairs={{0,4},{1,5},{2,6},{3,7},{4,0},{5,1},{6,2},{7,3},{8,12},{9,13},{10,... | collective-permute-start | bytes 516104 | tf_op jit(solution)/shard_map/ppermute | solution.py:163
  53.8 0.2 collective-permute-start.23
  54.0 1.4 %collective-permute-start.24 = (f32[336,128]{1,0:T(8,128)S(1)}, f32[336,128]{1,0:T(8,128)S(1)}, u32[]{:S(2)}, u32[]{:S(2)}) collective-permute-start(f32[336,128]{1,0:T(8,128)S(1)} %add.64), channel_id=1, source_target_pairs={{0,2},{1,7},{2,0},{3,5},{4,6},{5,3},{6,4},{7,1},{8,10},{9,15},{10,... | collective-permute-start | bytes 516104 | tf_op jit(solution)/shard_map/ppermute | solution.py:163
  55.4 3.9 %collective-permute-done.22 = f32[336,128]{1,0:T(8,128)S(1)} collective-permute-done((f32[336,128]{1,0:T(8,128)S(1)}, f32[336,128]{1,0:T(8,128)S(1)}, u32[]{:S(2)}, u32[]{:S(2)}) %collective-permute-start.22) | collective-permute-done | bytes 172064 | tf_op jit(solution)/shard_map/ppermute | solution.py:163
  59.3 2.8 %collective-permute-done.23 = f32[336,128]{1,0:T(8,128)S(1)} collective-permute-done((f32[336,128]{1,0:T(8,128)S(1)}, f32[336,128]{1,0:T(8,128)S(1)}, u32[]{:S(2)}, u32[]{:S(2)}) %collective-permute-start.23) | collective-permute-done | bytes 172064 | tf_op jit(solution)/shard_map/ppermute | solution.py:163
  62.1 1.4 %collective-permute-done.24 = f32[336,128]{1,0:T(8,128)S(1)} collective-permute-done((f32[336,128]{1,0:T(8,128)S(1)}, f32[336,128]{1,0:T(8,128)S(1)}, u32[]{:S(2)}, u32[]{:S(2)}) %collective-permute-start.24) | collective-permute-done | bytes 172064 | tf_op jit(solution)/shard_map/ppermute | solution.py:163
  63.5 0.1 add_add_fusion.value_ref
  63.5 0.5 collective-permute-start.25
  64.1 0.6 copy.13
  64.7 0.7 %shard_map.92.rest_0_ = f32[21,4096]{1,0:T(8,128)} custom-call(s32[1]{0:T(128)} %bitcast.refs_0_.half_ref, f32[336,128]{1,0:T(8,128)S(1)} %add_add_fusion.value_ref, f32[21,4096]{1,0:T(8,128)S(1)} %copy-done.2), custom_call_target="tpu_custom_call" | custom-call | tf_op jit(solution)/shard_map/pallas_call | solution.py:144
  65.5 0.7 %shard_map.93 = f32[21,4096]{1,0:T(8,128)} custom-call(s32[1]{0:T(128)} %bitcast.12.half_ref, f32[336,128]{1,0:T(8,128)S(1)} %collective-permute-done.25.value_ref, f32[21,4096]{1,0:T(8,128)S(1)} %copy-done.2, f32[21,4096]{1,0:T(8,128)} %shard_map.92.rest_0_), custom_call_target="tpu_custom_call", output_to_operand_aliasing={{}: (3, {})} | custom-call | tf_op jit(solution)/shard_map/pallas_call | solution.py:144
  (21 shorter events, 0.2 us)
Async XLA Ops:
  0.6 1.2 %copy-start = (f32[2,1024,128]{2,1,0:T(8,128)S(1)}, f32[2,1024,128]{2,1,0:T(8,128)}, u32[]{:S(2)}) copy-start(f32[2,1024,128]{2,1,0:T(8,128)} %param.7) | copy-start | bytes 3145732
  0.6 12.6 %copy-start.3 = (f32[128,1024]{1,0:T(8,128)S(1)}, f32[128,1024]{1,0:T(8,128)}, u32[]{:S(2)}) copy-start(f32[128,1024]{1,0:T(8,128)} %param.11) | copy-start | bytes 1572868
  2.9 4.4 %collective-permute-start = (f32[21,1024]{1,0:T(8,128)S(1)}, f32[21,1024]{1,0:T(8,128)S(1)}, u32[]{:S(2)}, u32[]{:S(2)}) collective-permute-start(f32[21,1024]{1,0:T(8,128)S(1)} %convolution_bitcast_fusion), channel_id=1, source_target_pairs={{0,1},{1,0},{2,3},{3,2},{4,5},{5,4},{6,7},{7,6},{8,9},{9,8},{10,11... | collective-permute-start | bytes 258056 | tf_op jit(solution)/shard_map/ppermute | solution.py:163
  7.3 7.8 %collective-permute-start.4 = (f32[2,128,1024]{2,1,0:T(8,128)}, f32[2,128,1024]{2,1,0:T(8,128)S(1)}, u32[]{:S(2)}, u32[]{:S(2)}) collective-permute-start(f32[2,128,1024]{2,1,0:T(8,128)} %param.10), channel_id=1, source_target_pairs={{0,1},{1,0},{2,3},{3,2},{4,5},{5,4},{6,7},{7,6},{8,9},{9,8},{10,11... | collective-permute-start | bytes 3145736 | tf_op jit(solution)/shard_map/ppermute | solution.py:163
  7.6 5.6 %collective-permute-start.3 = (f32[168,128]{1,0:T(8,128)S(1)}, f32[168,128]{1,0:T(8,128)S(1)}, u32[]{:S(2)}, u32[]{:S(2)}) collective-permute-start(f32[168,128]{1,0:T(8,128)S(1)} %shard_map.86), channel_id=1, source_target_pairs={{0,2},{1,7},{2,0},{3,5},{4,6},{5,3},{6,4},{7,1},{8,10},{9,15},{10,... | collective-permute-start | bytes 258056 | tf_op jit(solution)/shard_map/ppermute | solution.py:163
  8.6 6.4 %collective-permute-start.1 = (f32[168,128]{1,0:T(8,128)S(1)}, f32[168,128]{1,0:T(8,128)S(1)}, u32[]{:S(2)}, u32[]{:S(2)}) collective-permute-start(f32[168,128]{1,0:T(8,128)S(1)} %shard_map.86), channel_id=1, source_target_pairs={{0,4},{1,5},{2,6},{3,7},{4,0},{5,1},{6,2},{7,3},{8,12},{9,13},{10,... | collective-permute-start | bytes 258056 | tf_op jit(solution)/shard_map/ppermute | solution.py:163
  9.0 6.1 %collective-permute-start.2 = (f32[168,128]{1,0:T(8,128)S(1)}, f32[168,128]{1,0:T(8,128)S(1)}, u32[]{:S(2)}, u32[]{:S(2)}) collective-permute-start(f32[168,128]{1,0:T(8,128)S(1)} %shard_map.86), channel_id=1, source_target_pairs={{0,6},{1,3},{2,4},{3,1},{4,2},{5,7},{6,0},{7,5},{8,14},{9,11},{10,... | collective-permute-start | bytes 258056 | tf_op jit(solution)/shard_map/ppermute | solution.py:163
  13.2 7.3 %collective-permute-start.9 = (f32[128,1024]{1,0:T(8,128)S(1)}, f32[128,1024]{1,0:T(8,128)S(1)}, u32[]{:S(2)}, u32[]{:S(2)}) collective-permute-start(f32[128,1024]{1,0:T(8,128)S(1)} %copy-done.3), channel_id=1, source_target_pairs={{0,1},{1,0},{2,3},{3,2},{4,5},{5,4},{6,7},{7,6},{8,9},{9,8},{10,11... | collective-permute-start | bytes 1572872 | tf_op jit(solution)/shard_map/ppermute | solution.py:163
  15.0 34.6 %copy-start.1 = (f32[4096,2,128]{2,1,0:T(2,128)S(1)}, f32[4096,2,128]{2,1,0:T(2,128)}, u32[]{:S(2)}) copy-start(f32[4096,2,128]{2,1,0:T(2,128)} %param.12) | copy-start | bytes 12582916
  15.7 5.7 %collective-permute-start.6 = (f32[21,256]{1,0:T(8,128)S(1)}, f32[21,256]{1,0:T(8,128)S(1)}, u32[]{:S(2)}, u32[]{:S(2)}) collective-permute-start(f32[21,256]{1,0:T(8,128)S(1)} %get-tuple-element.19.own0.block0_ref), channel_id=1, source_target_pairs={{0,64},{1,5},{2,66},{3,7},{4,68},{5,1},{6,70},{7,3},{8,72},{9,13},... | collective-permute-start | bytes 64520 | tf_op jit(solution)/shard_map/ppermute | solution.py:163
  16.2 5.1 %collective-permute-start.7 = (f32[21,256]{1,0:T(8,128)S(1)}, f32[21,256]{1,0:T(8,128)S(1)}, u32[]{:S(2)}, u32[]{:S(2)}) collective-permute-start(f32[21,256]{1,0:T(8,128)S(1)} %get-tuple-element.19.own0.block0_ref), channel_id=1, source_target_pairs={{0,64},{1,7},{2,66},{3,5},{4,68},{5,3},{6,70},{7,1},{8,72},{9,15},... | collective-permute-start | bytes 64520 | tf_op jit(solution)/shard_map/ppermute | solution.py:163
  18.4 2.9 %collective-permute-start.8 = (f32[21,256]{1,0:T(8,128)S(1)}, f32[21,256]{1,0:T(8,128)S(1)}, u32[]{:S(2)}, u32[]{:S(2)}) collective-permute-start(f32[21,256]{1,0:T(8,128)S(1)} %get-tuple-element.19.own0.block0_ref), channel_id=1, source_target_pairs={{0,64},{1,3},{2,66},{3,1},{4,68},{5,7},{6,70},{7,5},{8,72},{9,11},... | collective-permute-start | bytes 64520 | tf_op jit(solution)/shard_map/ppermute | solution.py:163
  18.4 2.9 %collective-permute-start.5 = (f32[21,256]{1,0:T(8,128)S(1)}, f32[21,256]{1,0:T(8,128)S(1)}, u32[]{:S(2)}, u32[]{:S(2)}) collective-permute-start(f32[21,256]{1,0:T(8,128)S(1)} %get-tuple-element.20), channel_id=1, source_target_pairs={{0,1},{1,0},{2,3},{3,2},{4,5},{5,4},{6,7},{7,6},{8,9},{9,8},{10,11... | collective-permute-start | bytes 64520 | tf_op jit(solution)/shard_map/ppermute | solution.py:163
  21.8 4.3 %collective-permute-start.10 = (f32[21,256]{1,0:T(8,128)S(1)}, f32[21,256]{1,0:T(8,128)S(1)}, u32[]{:S(2)}, u32[]{:S(2)}) collective-permute-start(f32[21,256]{1,0:T(8,128)S(1)} %shard_map.88.own1), channel_id=1, source_target_pairs={{0,64},{1,5},{2,66},{3,7},{4,68},{5,1},{6,70},{7,3},{8,72},{9,13},... | collective-permute-start | bytes 64520 | tf_op jit(solution)/shard_map/ppermute | solution.py:163
  22.5 3.9 %collective-permute-start.11 = (f32[21,256]{1,0:T(8,128)S(1)}, f32[21,256]{1,0:T(8,128)S(1)}, u32[]{:S(2)}, u32[]{:S(2)}) collective-permute-start(f32[21,256]{1,0:T(8,128)S(1)} %shard_map.88.own1), channel_id=1, source_target_pairs={{0,64},{1,7},{2,66},{3,5},{4,68},{5,3},{6,70},{7,1},{8,72},{9,15},... | collective-permute-start | bytes 64520 | tf_op jit(solution)/shard_map/ppermute | solution.py:163
  24.2 2.7 %collective-permute-start.12 = (f32[21,256]{1,0:T(8,128)S(1)}, f32[21,256]{1,0:T(8,128)S(1)}, u32[]{:S(2)}, u32[]{:S(2)}) collective-permute-start(f32[21,256]{1,0:T(8,128)S(1)} %shard_map.88.own1), channel_id=1, source_target_pairs={{0,64},{1,3},{2,66},{3,1},{4,68},{5,7},{6,70},{7,5},{8,72},{9,11},... | collective-permute-start | bytes 64520 | tf_op jit(solution)/shard_map/ppermute | solution.py:163
  27.3 4.5 %collective-permute-start.13 = (f32[42,256]{1,0:T(8,128)S(1)}, f32[42,256]{1,0:T(8,128)S(1)}, u32[]{:S(2)}, u32[]{:S(2)}) collective-permute-start(f32[42,256]{1,0:T(8,128)S(1)} %shard_map.89), channel_id=1, source_target_pairs={{0,2},{1,129},{2,0},{3,131},{4,6},{5,133},{6,4},{7,135},{8,10},{9,... | collective-permute-start | bytes 129032 | tf_op jit(solution)/shard_map/ppermute | solution.py:163
  29.5 4.2 %collective-permute-start.14 = (f32[42,256]{1,0:T(8,128)S(1)}, f32[42,256]{1,0:T(8,128)S(1)}, u32[]{:S(2)}, u32[]{:S(2)}) collective-permute-start(f32[42,256]{1,0:T(8,128)S(1)} %shard_map.89), channel_id=1, source_target_pairs={{0,2},{1,193},{2,0},{3,195},{4,6},{5,197},{6,4},{7,199},{8,10},{9,... | collective-permute-start | bytes 129032 | tf_op jit(solution)/shard_map/ppermute | solution.py:163
  30.3 3.3 %collective-permute-start.15 = (f32[42,256]{1,0:T(8,128)S(1)}, f32[42,256]{1,0:T(8,128)S(1)}, u32[]{:S(2)}, u32[]{:S(2)}) collective-permute-start(f32[42,256]{1,0:T(8,128)S(1)} %shard_map.89), channel_id=1, source_target_pairs={{0,2},{1,65},{2,0},{3,67},{4,6},{5,69},{6,4},{7,71},{8,10},{9,73},... | collective-permute-start | bytes 129032 | tf_op jit(solution)/shard_map/ppermute | solution.py:163
  33.6 3.2 %collective-permute-start.16 = (f32[42,256]{1,0:T(8,128)S(1)}, f32[42,256]{1,0:T(8,128)S(1)}, u32[]{:S(2)}, u32[]{:S(2)}) collective-permute-start(f32[42,256]{1,0:T(8,128)S(1)} %add_add_fusion.3), channel_id=1, source_target_pairs={{0,2},{1,9},{2,0},{3,11},{4,6},{5,13},{6,4},{7,15},{8,10},{9,1},{1... | collective-permute-start | bytes 129032 | tf_op jit(solution)/shard_map/ppermute | solution.py:163
  36.8 9.5 %collective-permute-start.17 = (f32[42,256]{1,0:T(8,128)S(1)}, f32[42,256]{1,0:T(8,128)S(1)}, u32[]{:S(2)}, u32[]{:S(2)}) collective-permute-start(f32[42,256]{1,0:T(8,128)S(1)} %add.60), channel_id=1, source_target_pairs={{0,2},{2,0},{4,6},{6,4},{8,10},{10,8},{12,14},{14,12},{16,18},{18,... | collective-permute-start | bytes 129032 | tf_op jit(solution)/shard_map/ppermute | solution.py:184
  43.2 3.8 %collective-permute-start.18 = (f32[42,256]{1,0:T(8,128)S(1)}, f32[42,256]{1,0:T(8,128)S(1)}, u32[]{:S(2)}, u32[]{:S(2)}) collective-permute-start(f32[42,256]{1,0:T(8,128)S(1)} %add.60), channel_id=1, source_target_pairs={{0,2},{2,0},{4,6},{6,4},{8,10},{10,8},{12,14},{14,12},{16,18},{18,... | collective-permute-start | bytes 129032 | tf_op jit(solution)/shard_map/ppermute | solution.py:184
  43.5 4.9 %collective-permute-start.19 = (f32[42,256]{1,0:T(8,128)S(1)}, f32[42,256]{1,0:T(8,128)S(1)}, u32[]{:S(2)}, u32[]{:S(2)}) collective-permute-start(f32[42,256]{1,0:T(8,128)S(1)} %add.60), channel_id=1, source_target_pairs={{0,2},{2,0},{4,6},{6,4},{8,10},{10,8},{12,14},{14,12},{16,18},{18,... | collective-permute-start | bytes 129032 | tf_op jit(solution)/shard_map/ppermute | solution.py:184
  48.4 1.3 %collective-permute-start.20 = (f32[42,128]{1,0:T(8,128)S(1)}, f32[42,128]{1,0:T(8,128)S(1)}, u32[]{:S(2)}, u32[]{:S(2)}) collective-permute-start(f32[42,128]{1,0:T(8,128)S(1)} %slice.22), channel_id=1, source_target_pairs={{0,1},{1,0},{2,3},{3,2},{4,5},{5,4},{6,7},{7,6},{8,9},{9,8},{10,11... | collective-permute-start | bytes 64520 | tf_op jit(solution)/shard_map/ppermute | solution.py:163
  49.7 15.1 %copy-start.2 = (f32[21,4096]{1,0:T(8,128)S(1)}, f32[21,4096]{1,0:T(8,128)}, u32[]{:S(2)}) copy-start(f32[21,4096]{1,0:T(8,128)} %base_ref.3) | copy-start | bytes 1032196
  50.4 1.5 %collective-permute-start.21 = (f32[336,128]{1,0:T(8,128)S(1)}, f32[336,128]{1,0:T(8,128)S(1)}, u32[]{:S(2)}, u32[]{:S(2)}) collective-permute-start(f32[336,128]{1,0:T(8,128)S(1)} %shard_map.91), channel_id=1, source_target_pairs={{0,1},{1,0},{2,3},{3,2},{4,5},{5,4},{6,7},{7,6},{8,9},{9,8},{10,11... | collective-permute-start | bytes 516104 | tf_op jit(solution)/shard_map/ppermute | solution.py:163
  51.9 7.4 %collective-permute-start.22 = (f32[336,128]{1,0:T(8,128)S(1)}, f32[336,128]{1,0:T(8,128)S(1)}, u32[]{:S(2)}, u32[]{:S(2)}) collective-permute-start(f32[336,128]{1,0:T(8,128)S(1)} %add.64), channel_id=1, source_target_pairs={{0,4},{1,5},{2,6},{3,7},{4,0},{5,1},{6,2},{7,3},{8,12},{9,13},{10,... | collective-permute-start | bytes 516104 | tf_op jit(solution)/shard_map/ppermute | solution.py:163
  53.8 8.3 %collective-permute-start.23 = (f32[336,128]{1,0:T(8,128)S(1)}, f32[336,128]{1,0:T(8,128)S(1)}, u32[]{:S(2)}, u32[]{:S(2)}) collective-permute-start(f32[336,128]{1,0:T(8,128)S(1)} %add.64), channel_id=1, source_target_pairs={{0,6},{1,3},{2,4},{3,1},{4,2},{5,7},{6,0},{7,5},{8,14},{9,11},{10,... | collective-permute-start | bytes 516104 | tf_op jit(solution)/shard_map/ppermute | solution.py:163
  54.0 9.5 %collective-permute-start.24 = (f32[336,128]{1,0:T(8,128)S(1)}, f32[336,128]{1,0:T(8,128)S(1)}, u32[]{:S(2)}, u32[]{:S(2)}) collective-permute-start(f32[336,128]{1,0:T(8,128)S(1)} %add.64), channel_id=1, source_target_pairs={{0,2},{1,7},{2,0},{3,5},{4,6},{5,3},{6,4},{7,1},{8,10},{9,15},{10,... | collective-permute-start | bytes 516104 | tf_op jit(solution)/shard_map/ppermute | solution.py:163
  63.5 1.9 %collective-permute-start.25 = (f32[336,128]{1,0:T(8,128)S(1)}, f32[336,128]{1,0:T(8,128)S(1)}, u32[]{:S(2)}, u32[]{:S(2)}) collective-permute-start(f32[336,128]{1,0:T(8,128)S(1)} %add_add_fusion.value_ref), channel_id=1, source_target_pairs={{0,1},{1,0},{2,3},{3,2},{4,5},{5,4},{6,7},{7,6},{8,9},{9,8},{10,11... | collective-permute-start | bytes 516104 | tf_op jit(solution)/shard_map/ppermute | solution.py:163

commit v6 on v5

--- a/solution.py
+++ b/solution.py
@@ -163,7 +163,7 @@
         return lax.ppermute(value, both, [(i, i ^ masks[i % 2]) for i in range(256)])
 
     def y_sum(value):
-        one, two, three = swap(value, 2, 6), swap(value, 6, 2), swap(value, 4)
+        one, two, three = swap(value, 2), swap(value, 6), swap(value, 4)
         return (three + two) + (one + value)
 
     def lanes(value, start, size):

time: 66.6 us -> 66.6 us (level)
  transfers between devices with their start and end apart: 26 -> 26, of which waited for: 14 -> 13; matrix products, arithmetic and copies ran while one was open for 6% -> 6% of each run, Pallas kernels for 3% -> 3%
where the time goes in v6:
time: 66.6 us; the launch traced here: 66.3 us
  starting transfers between devices  34.9 us (52%)
  waiting for transfers between devices  19.7 us (30%)
  Pallas kernels  4.2 us (6%)
  local copies, waits for them, and re-layouts  2.83 us (4%)
  matrix products  2.06 us (3%)
  other arithmetic  1.63 us (2%)
  between operations  1.01 us (2%)
    ppermute x23, starting transfers between devices, swap(): lax.ppermute(value, both, [(i, i ^ masks[i % 2]) for i in range(256)])  25.4 us
    ppermute x23, waiting for transfers between devices, swap(): lax.ppermute(value, both, [(i, i ^ masks[i % 2]) for i in range(256)])  17.7 us
    ppermute x3, starting transfers between devices, from_z(): return lax.ppermute(value, both, pairs)  9.5 us
    dot_general x2, matrix products, dot(): return jnp.einsum('ij,rj->ri', matrix, value, precision=HIGH)  2.06 us
    ppermute x3, waiting for transfers between devices, from_z(): return lax.ppermute(value, both, pairs)  2 us
    unnamed x9, local copies, waits for them, and re-layouts  1.84 us
    select_n x4, other arithmetic, here(): return lax.optimization_barrier(jnp.where(core >= 0, value, 0.0))  1.48 us
    pallas_call x2, Pallas kernels, trailing_products(): pl.pallas_call(lambda *refs: trailing_kernel(own, *refs), in_specs=[pl.Bl...  1.46 us
  transfers between devices with their start and end apart: 26, of which 13 were waited for; matrix products, arithmetic and copies ran while one was open for 6% of the time, Pallas kernels for 3%

profile of v6, /device:TPU:1, one launch (start us, length us, event | category | flops | bytes accessed | tf_op | source)
XLA Modules:
  0.0 66.3 jit_solution(13776442052456057555)
XLA Ops:
  0.6 0.0 copy-start
  0.7 1.2 %copy-done = f32[2,1024,128]{2,1,0:T(8,128)S(1)} copy-done((f32[2,1024,128]{2,1,0:T(8,128)S(1)}, f32[2,1024,128]{2,1,0:T(8,128)}, u32[]{:S(2)}) %copy-start) | copy-done | bytes 1048600
  1.9 1.0 %convolution_bitcast_fusion = f32[21,1024]{1,0:T(8,128)S(1)} fusion(f32[21,128]{1,0:T(8,128)} %param.8, f32[2,1024,128]{2,1,0:T(8,128)S(1)} %copy-done, s32[]{:T(128)S(6)} %select_n.63), kind=kOutput, calls=%fused_computation | convolution fusion | flops 16515072 | bytes 621060 | tf_op jit(solution)/shard_map/ij,rj->ri/dot_general | solution.py:176
  2.9 3.3 %collective-permute-start = (f32[21,1024]{1,0:T(8,128)S(1)}, f32[21,1024]{1,0:T(8,128)S(1)}, u32[]{:S(2)}, u32[]{:S(2)}) collective-permute-start(f32[21,1024]{1,0:T(8,128)S(1)} %convolution_bitcast_fusion), channel_id=1, source_target_pairs={{0,1},{1,0},{2,3},{3,2},{4,5},{5,4},{6,7},{7,6},{8,9},{9,8},{10,11... | collective-permute-start | bytes 258056 | tf_op jit(solution)/shard_map/ppermute | solution.py:163
  6.2 1.0 %convolution_bitcast_fusion.1.kept_ref = f32[21,1024]{1,0:T(8,128)S(1)} fusion(f32[21,128]{1,0:T(8,128)} %param.8, f32[2,1024,128]{2,1,0:T(8,128)S(1)} %copy-done, s32[]{:T(128)S(6)} %select_n.62), kind=kOutput, calls=%fused_computation.1 | convolution fusion | flops 16515072 | bytes 621060 | tf_op jit(solution)/shard_map/ij,rj->ri/dot_general | solution.py:176
  7.2 0.0 collective-permute-done.taken_ref
  7.3 0.3 collective-permute-start.4
  7.6 1.0 %collective-permute-start.3 = (f32[168,128]{1,0:T(8,128)S(1)}, f32[168,128]{1,0:T(8,128)S(1)}, u32[]{:S(2)}, u32[]{:S(2)}) collective-permute-start(f32[168,128]{1,0:T(8,128)S(1)} %shard_map.86), channel_id=1, source_target_pairs={{0,2},{1,7},{2,0},{3,5},{4,6},{5,3},{6,4},{7,1},{8,10},{9,15},{10,... | collective-permute-start | bytes 258056 | tf_op jit(solution)/shard_map/ppermute | solution.py:163
  8.6 0.3 collective-permute-start.1
  9.0 1.9 %collective-permute-start.2 = (f32[168,128]{1,0:T(8,128)S(1)}, f32[168,128]{1,0:T(8,128)S(1)}, u32[]{:S(2)}, u32[]{:S(2)}) collective-permute-start(f32[168,128]{1,0:T(8,128)S(1)} %shard_map.86), channel_id=1, source_target_pairs={{0,6},{1,3},{2,4},{3,1},{4,2},{5,7},{6,0},{7,5},{8,14},{9,11},{10,... | collective-permute-start | bytes 258056 | tf_op jit(solution)/shard_map/ppermute | solution.py:163
  10.9 1.0 %copy.12 = f32[2,21,1024]{2,1,0:T(8,128)S(1)} copy(f32[2,21,1024]{2,0,1:T(2,128)} %param.9) | data formatting | bytes 344064 | tf_op jit(solution)/shard_map/optimization_barrier | solution.py:202
  11.9 1.3 %select_bitcast_fusion = (f32[128,1024]{1,0:T(8,128)S(1)}, f32[128,1024]{1,0:T(8,128)S(1)}) fusion(f32[2,128,1024]{2,1,0:T(8,128)} %param.10, pred[]{:T(512)S(6)} %ge.2), kind=kLoop, calls=%fused_computation.8 | loop fusion | flops 262144 | bytes 2097153 | tf_op jit(solution)/shard_map/jit(_where)/select_n | solution.py:194
  13.2 0.0 collective-permute-done.3
  13.2 1.8 %collective-permute-start.9 = (f32[128,1024]{1,0:T(8,128)S(1)}, f32[128,1024]{1,0:T(8,128)S(1)}, u32[]{:S(2)}, u32[]{:S(2)}) collective-permute-start(f32[128,1024]{1,0:T(8,128)S(1)} %copy-done.3), channel_id=1, source_target_pairs={{0,1},{1,0},{2,3},{3,2},{4,5},{5,4},{6,7},{7,6},{8,9},{9,8},{10,11... | collective-permute-start | bytes 1572872 | tf_op jit(solution)/shard_map/ppermute | solution.py:163
  15.0 0.0 copy-start.1
  15.1 0.0 collective-permute-done.1
  15.1 0.0 collective-permute-done.4
  15.1 0.1 fusion
  15.2 0.4 shard_map.87
  15.7 0.6 collective-permute-start.6
  16.2 2.2 %collective-permute-start.7 = (f32[21,256]{1,0:T(8,128)S(1)}, f32[21,256]{1,0:T(8,128)S(1)}, u32[]{:S(2)}, u32[]{:S(2)}) collective-permute-start(f32[21,256]{1,0:T(8,128)S(1)} %get-tuple-element.19.own0.block0_ref), channel_id=1, source_target_pairs={{0,64},{1,7},{2,66},{3,5},{4,68},{5,3},{6,70},{7,1},{8,72},{9,15},... | collective-permute-start | bytes 64520 | tf_op jit(solution)/shard_map/ppermute | solution.py:163
  18.4 2.1 %collective-permute-start.5 = (f32[21,256]{1,0:T(8,128)S(1)}, f32[21,256]{1,0:T(8,128)S(1)}, u32[]{:S(2)}, u32[]{:S(2)}) collective-permute-start(f32[21,256]{1,0:T(8,128)S(1)} %get-tuple-element.20), channel_id=1, source_target_pairs={{0,1},{1,0},{2,3},{3,2},{4,5},{5,4},{6,7},{7,6},{8,9},{9,8},{10,11... | collective-permute-start | bytes 64520 | tf_op jit(solution)/shard_map/ppermute | solution.py:163
  20.5 0.0 collective-permute-done.9
  20.5 0.8 %collective-permute-done.5.base_ref = f32[21,256]{1,0:T(8,128)S(1)} collective-permute-done((f32[21,256]{1,0:T(8,128)S(1)}, f32[21,256]{1,0:T(8,128)S(1)}, u32[]{:S(2)}, u32[]{:S(2)}) %collective-permute-start.5) | collective-permute-done | bytes 21536 | tf_op jit(solution)/shard_map/ppermute | solution.py:163
  21.3 0.0 collective-permute-done.6.two0
  21.3 0.0 collective-permute-done.7.three0
  21.3 0.0 collective-permute-done.8.one0
  21.4 0.4 shard_map.88.own1
  21.8 0.7 %collective-permute-start.10 = (f32[21,256]{1,0:T(8,128)S(1)}, f32[21,256]{1,0:T(8,128)S(1)}, u32[]{:S(2)}, u32[]{:S(2)}) collective-permute-start(f32[21,256]{1,0:T(8,128)S(1)} %shard_map.88.own1), channel_id=1, source_target_pairs={{0,64},{1,5},{2,66},{3,7},{4,68},{5,1},{6,70},{7,3},{8,72},{9,13},... | collective-permute-start | bytes 64520 | tf_op jit(solution)/shard_map/ppermute | solution.py:163
  22.5 1.7 %collective-permute-start.11 = (f32[21,256]{1,0:T(8,128)S(1)}, f32[21,256]{1,0:T(8,128)S(1)}, u32[]{:S(2)}, u32[]{:S(2)}) collective-permute-start(f32[21,256]{1,0:T(8,128)S(1)} %shard_map.88.own1), channel_id=1, source_target_pairs={{0,64},{1,7},{2,66},{3,5},{4,68},{5,3},{6,70},{7,1},{8,72},{9,15},... | collective-permute-start | bytes 64520 | tf_op jit(solution)/shard_map/ppermute | solution.py:163
  24.2 0.3 collective-permute-start.12
  24.5 1.5 %collective-permute-done.10.two1 = f32[21,256]{1,0:T(8,128)S(1)} collective-permute-done((f32[21,256]{1,0:T(8,128)S(1)}, f32[21,256]{1,0:T(8,128)S(1)}, u32[]{:S(2)}, u32[]{:S(2)}) %collective-permute-start.10) | collective-permute-done | bytes 21536 | tf_op jit(solution)/shard_map/ppermute | solution.py:163
  26.1 0.3 collective-permute-done.11.three1
  26.4 0.5 collective-permute-done.12.one1
  26.9 0.4 shard_map.89
  27.3 2.1 %collective-permute-start.13 = (f32[42,256]{1,0:T(8,128)S(1)}, f32[42,256]{1,0:T(8,128)S(1)}, u32[]{:S(2)}, u32[]{:S(2)}) collective-permute-start(f32[42,256]{1,0:T(8,128)S(1)} %shard_map.89), channel_id=1, source_target_pairs={{0,2},{1,129},{2,0},{3,131},{4,6},{5,133},{6,4},{7,135},{8,10},{9,... | collective-permute-start | bytes 129032 | tf_op jit(solution)/shard_map/ppermute | solution.py:163
  29.5 0.9 %collective-permute-start.14 = (f32[42,256]{1,0:T(8,128)S(1)}, f32[42,256]{1,0:T(8,128)S(1)}, u32[]{:S(2)}, u32[]{:S(2)}) collective-permute-start(f32[42,256]{1,0:T(8,128)S(1)} %shard_map.89), channel_id=1, source_target_pairs={{0,2},{1,193},{2,0},{3,195},{4,6},{5,197},{6,4},{7,199},{8,10},{9,... | collective-permute-start | bytes 129032 | tf_op jit(solution)/shard_map/ppermute | solution.py:163
  30.3 0.0 collective-permute-start.15
  30.3 1.5 %collective-permute-done.13 = f32[42,256]{1,0:T(8,128)S(1)} collective-permute-done((f32[42,256]{1,0:T(8,128)S(1)}, f32[42,256]{1,0:T(8,128)S(1)}, u32[]{:S(2)}, u32[]{:S(2)}) %collective-permute-start.13) | collective-permute-done | bytes 43040 | tf_op jit(solution)/shard_map/ppermute | solution.py:163
  31.9 1.8 %collective-permute-done.14 = f32[42,256]{1,0:T(8,128)S(1)} collective-permute-done((f32[42,256]{1,0:T(8,128)S(1)}, f32[42,256]{1,0:T(8,128)S(1)}, u32[]{:S(2)}, u32[]{:S(2)}) %collective-permute-start.14) | collective-permute-done | bytes 43040 | tf_op jit(solution)/shard_map/ppermute | solution.py:163
  33.6 1.7 %collective-permute-start.16 = (f32[42,256]{1,0:T(8,128)S(1)}, f32[42,256]{1,0:T(8,128)S(1)}, u32[]{:S(2)}, u32[]{:S(2)}) collective-permute-start(f32[42,256]{1,0:T(8,128)S(1)} %add_add_fusion.3), channel_id=1, source_target_pairs={{0,2},{1,9},{2,0},{3,11},{4,6},{5,13},{6,4},{7,15},{8,10},{9,1},{1... | collective-permute-start | bytes 129032 | tf_op jit(solution)/shard_map/ppermute | solution.py:163
  35.4 1.5 %collective-permute-done.16 = f32[42,256]{1,0:T(8,128)S(1)} collective-permute-done((f32[42,256]{1,0:T(8,128)S(1)}, f32[42,256]{1,0:T(8,128)S(1)}, u32[]{:S(2)}, u32[]{:S(2)}) %collective-permute-start.16) | collective-permute-done | bytes 43040 | tf_op jit(solution)/shard_map/ppermute | solution.py:163
  36.8 6.4 %collective-permute-start.17 = (f32[42,256]{1,0:T(8,128)S(1)}, f32[42,256]{1,0:T(8,128)S(1)}, u32[]{:S(2)}, u32[]{:S(2)}) collective-permute-start(f32[42,256]{1,0:T(8,128)S(1)} %add.60), channel_id=1, source_target_pairs={{0,2},{2,0},{4,6},{6,4},{8,10},{10,8},{12,14},{14,12},{16,18},{18,... | collective-permute-start | bytes 129032 | tf_op jit(solution)/shard_map/ppermute | solution.py:184
  43.2 0.3 collective-permute-start.18
  43.5 2.9 %collective-permute-start.19 = (f32[42,256]{1,0:T(8,128)S(1)}, f32[42,256]{1,0:T(8,128)S(1)}, u32[]{:S(2)}, u32[]{:S(2)}) collective-permute-start(f32[42,256]{1,0:T(8,128)S(1)} %add.60), channel_id=1, source_target_pairs={{0,2},{2,0},{4,6},{6,4},{8,10},{10,8},{12,14},{14,12},{16,18},{18,... | collective-permute-start | bytes 129032 | tf_op jit(solution)/shard_map/ppermute | solution.py:184
  46.4 0.7 %collective-permute-done.18 = f32[42,256]{1,0:T(8,128)S(1)} collective-permute-done((f32[42,256]{1,0:T(8,128)S(1)}, f32[42,256]{1,0:T(8,128)S(1)}, u32[]{:S(2)}, u32[]{:S(2)}) %collective-permute-start.18) | collective-permute-done | bytes 43040 | tf_op jit(solution)/shard_map/ppermute | solution.py:184
  47.1 1.3 %collective-permute-done.19 = f32[42,256]{1,0:T(8,128)S(1)} collective-permute-done((f32[42,256]{1,0:T(8,128)S(1)}, f32[42,256]{1,0:T(8,128)S(1)}, u32[]{:S(2)}, u32[]{:S(2)}) %collective-permute-start.19) | collective-permute-done | bytes 43040 | tf_op jit(solution)/shard_map/ppermute | solution.py:184
  48.4 0.1 collective-permute-start.20
  48.5 1.2 %collective-permute-done.20.refs_2_ = f32[42,128]{1,0:T(8,128)S(1)} collective-permute-done((f32[42,128]{1,0:T(8,128)S(1)}, f32[42,128]{1,0:T(8,128)S(1)}, u32[]{:S(2)}, u32[]{:S(2)}) %collective-permute-start.20) | collective-permute-done | bytes 21536 | tf_op jit(solution)/shard_map/ppermute | solution.py:163
  49.7 0.7 %shard_map.91 = f32[336,128]{1,0:T(8,128)S(1)} custom-call(s32[1]{0:T(128)} %bitcast.refs_0_.half_ref, f32[42,256]{1,0:T(8,128)S(1)} %add_add_fusion.2.refs_1_, f32[42,128]{1,0:T(8,128)S(1)} %collective-permute-done.20.refs_2_, f32[8192,128]{1,0:T(8,128)S(1)} %bitcast.26), custom_call_target="tpu_custom_call" | custom-call | flops 66060288 | bytes 2097152 | tf_op jit(solution)/shard_map/pallas_call | solution.py:118
  50.4 0.2 collective-permute-start.21
  50.6 0.7 %shard_map.90 = (f32[336,128]{1,0:T(8,128)S(1)}, f32[42,128]{1,0:T(8,128)S(1)}) custom-call(s32[1]{0:T(128)} %bitcast.refs_0_.half_ref, f32[42,256]{1,0:T(8,128)S(1)} %add_add_fusion.2.refs_1_, f32[42,128]{1,0:T(8,128)S(1)} %collective-permute-done.20.refs_2_, f32[8192,128]{1,0:T(8,128)S(1)} %bitcast.27), custom_call_target="tpu_custom_call" | custom-call | flops 66060288 | bytes 2097152 | tf_op jit(solution)/shard_map/pallas_call | solution.py:118
  51.3 0.5 collective-permute-done.21
  51.9 1.9 %collective-permute-start.22 = (f32[336,128]{1,0:T(8,128)S(1)}, f32[336,128]{1,0:T(8,128)S(1)}, u32[]{:S(2)}, u32[]{:S(2)}) collective-permute-start(f32[336,128]{1,0:T(8,128)S(1)} %add.64), channel_id=1, source_target_pairs={{0,4},{1,5},{2,6},{3,7},{4,0},{5,1},{6,2},{7,3},{8,12},{9,13},{10,... | collective-permute-start | bytes 516104 | tf_op jit(solution)/shard_map/ppermute | solution.py:163
  53.8 1.6 %collective-permute-start.23 = (f32[336,128]{1,0:T(8,128)S(1)}, f32[336,128]{1,0:T(8,128)S(1)}, u32[]{:S(2)}, u32[]{:S(2)}) collective-permute-start(f32[336,128]{1,0:T(8,128)S(1)} %add.64), channel_id=1, source_target_pairs={{0,6},{1,7},{2,4},{3,5},{4,2},{5,3},{6,0},{7,1},{8,14},{9,15},{10,... | collective-permute-start | bytes 516104 | tf_op jit(solution)/shard_map/ppermute | solution.py:163
  55.4 0.0 collective-permute-start.24
  55.4 3.9 %collective-permute-done.22 = f32[336,128]{1,0:T(8,128)S(1)} collective-permute-done((f32[336,128]{1,0:T(8,128)S(1)}, f32[336,128]{1,0:T(8,128)S(1)}, u32[]{:S(2)}, u32[]{:S(2)}) %collective-permute-start.22) | collective-permute-done | bytes 172064 | tf_op jit(solution)/shard_map/ppermute | solution.py:163
  59.3 4.2 %collective-permute-done.23 = f32[336,128]{1,0:T(8,128)S(1)} collective-permute-done((f32[336,128]{1,0:T(8,128)S(1)}, f32[336,128]{1,0:T(8,128)S(1)}, u32[]{:S(2)}, u32[]{:S(2)}) %collective-permute-start.23) | collective-permute-done | bytes 172064 | tf_op jit(solution)/shard_map/ppermute | solution.py:163
  63.5 0.0 collective-permute-done.24
  63.5 0.1 add_add_fusion.value_ref
  63.5 0.6 collective-permute-start.25
  64.1 0.6 copy.13
  64.7 0.7 %shard_map.92.rest_0_ = f32[21,4096]{1,0:T(8,128)} custom-call(s32[1]{0:T(128)} %bitcast.refs_0_.half_ref, f32[336,128]{1,0:T(8,128)S(1)} %add_add_fusion.value_ref, f32[21,4096]{1,0:T(8,128)S(1)} %copy-done.2), custom_call_target="tpu_custom_call" | custom-call | tf_op jit(solution)/shard_map/pallas_call | solution.py:144
  65.5 0.7 %shard_map.93 = f32[21,4096]{1,0:T(8,128)} custom-call(s32[1]{0:T(128)} %bitcast.12.half_ref, f32[336,128]{1,0:T(8,128)S(1)} %collective-permute-done.25.value_ref, f32[21,4096]{1,0:T(8,128)S(1)} %copy-done.2, f32[21,4096]{1,0:T(8,128)} %shard_map.92.rest_0_), custom_call_target="tpu_custom_call", output_to_operand_aliasing={{}: (3, {})} | custom-call | tf_op jit(solution)/shard_map/pallas_call | solution.py:144
  (21 shorter events, 0.2 us)
Async XLA Ops:
  0.6 1.2 %copy-start = (f32[2,1024,128]{2,1,0:T(8,128)S(1)}, f32[2,1024,128]{2,1,0:T(8,128)}, u32[]{:S(2)}) copy-start(f32[2,1024,128]{2,1,0:T(8,128)} %param.7) | copy-start | bytes 3145732
  0.6 12.6 %copy-start.3 = (f32[128,1024]{1,0:T(8,128)S(1)}, f32[128,1024]{1,0:T(8,128)}, u32[]{:S(2)}) copy-start(f32[128,1024]{1,0:T(8,128)} %param.11) | copy-start | bytes 1572868
  2.9 4.4 %collective-permute-start = (f32[21,1024]{1,0:T(8,128)S(1)}, f32[21,1024]{1,0:T(8,128)S(1)}, u32[]{:S(2)}, u32[]{:S(2)}) collective-permute-start(f32[21,1024]{1,0:T(8,128)S(1)} %convolution_bitcast_fusion), channel_id=1, source_target_pairs={{0,1},{1,0},{2,3},{3,2},{4,5},{5,4},{6,7},{7,6},{8,9},{9,8},{10,11... | collective-permute-start | bytes 258056 | tf_op jit(solution)/shard_map/ppermute | solution.py:163
  7.3 7.8 %collective-permute-start.4 = (f32[2,128,1024]{2,1,0:T(8,128)}, f32[2,128,1024]{2,1,0:T(8,128)S(1)}, u32[]{:S(2)}, u32[]{:S(2)}) collective-permute-start(f32[2,128,1024]{2,1,0:T(8,128)} %param.10), channel_id=1, source_target_pairs={{0,1},{1,0},{2,3},{3,2},{4,5},{5,4},{6,7},{7,6},{8,9},{9,8},{10,11... | collective-permute-start | bytes 3145736 | tf_op jit(solution)/shard_map/ppermute | solution.py:163
  7.6 5.6 %collective-permute-start.3 = (f32[168,128]{1,0:T(8,128)S(1)}, f32[168,128]{1,0:T(8,128)S(1)}, u32[]{:S(2)}, u32[]{:S(2)}) collective-permute-start(f32[168,128]{1,0:T(8,128)S(1)} %shard_map.86), channel_id=1, source_target_pairs={{0,2},{1,7},{2,0},{3,5},{4,6},{5,3},{6,4},{7,1},{8,10},{9,15},{10,... | collective-permute-start | bytes 258056 | tf_op jit(solution)/shard_map/ppermute | solution.py:163
  8.6 6.4 %collective-permute-start.1 = (f32[168,128]{1,0:T(8,128)S(1)}, f32[168,128]{1,0:T(8,128)S(1)}, u32[]{:S(2)}, u32[]{:S(2)}) collective-permute-start(f32[168,128]{1,0:T(8,128)S(1)} %shard_map.86), channel_id=1, source_target_pairs={{0,4},{1,5},{2,6},{3,7},{4,0},{5,1},{6,2},{7,3},{8,12},{9,13},{10,... | collective-permute-start | bytes 258056 | tf_op jit(solution)/shard_map/ppermute | solution.py:163
  9.0 6.1 %collective-permute-start.2 = (f32[168,128]{1,0:T(8,128)S(1)}, f32[168,128]{1,0:T(8,128)S(1)}, u32[]{:S(2)}, u32[]{:S(2)}) collective-permute-start(f32[168,128]{1,0:T(8,128)S(1)} %shard_map.86), channel_id=1, source_target_pairs={{0,6},{1,3},{2,4},{3,1},{4,2},{5,7},{6,0},{7,5},{8,14},{9,11},{10,... | collective-permute-start | bytes 258056 | tf_op jit(solution)/shard_map/ppermute | solution.py:163
  13.2 7.3 %collective-permute-start.9 = (f32[128,1024]{1,0:T(8,128)S(1)}, f32[128,1024]{1,0:T(8,128)S(1)}, u32[]{:S(2)}, u32[]{:S(2)}) collective-permute-start(f32[128,1024]{1,0:T(8,128)S(1)} %copy-done.3), channel_id=1, source_target_pairs={{0,1},{1,0},{2,3},{3,2},{4,5},{5,4},{6,7},{7,6},{8,9},{9,8},{10,11... | collective-permute-start | bytes 1572872 | tf_op jit(solution)/shard_map/ppermute | solution.py:163
  15.0 34.6 %copy-start.1 = (f32[4096,2,128]{2,1,0:T(2,128)S(1)}, f32[4096,2,128]{2,1,0:T(2,128)}, u32[]{:S(2)}) copy-start(f32[4096,2,128]{2,1,0:T(2,128)} %param.12) | copy-start | bytes 12582916
  15.7 5.7 %collective-permute-start.6 = (f32[21,256]{1,0:T(8,128)S(1)}, f32[21,256]{1,0:T(8,128)S(1)}, u32[]{:S(2)}, u32[]{:S(2)}) collective-permute-start(f32[21,256]{1,0:T(8,128)S(1)} %get-tuple-element.19.own0.block0_ref), channel_id=1, source_target_pairs={{0,64},{1,5},{2,66},{3,7},{4,68},{5,1},{6,70},{7,3},{8,72},{9,13},... | collective-permute-start | bytes 64520 | tf_op jit(solution)/shard_map/ppermute | solution.py:163
  16.2 5.1 %collective-permute-start.7 = (f32[21,256]{1,0:T(8,128)S(1)}, f32[21,256]{1,0:T(8,128)S(1)}, u32[]{:S(2)}, u32[]{:S(2)}) collective-permute-start(f32[21,256]{1,0:T(8,128)S(1)} %get-tuple-element.19.own0.block0_ref), channel_id=1, source_target_pairs={{0,64},{1,7},{2,66},{3,5},{4,68},{5,3},{6,70},{7,1},{8,72},{9,15},... | collective-permute-start | bytes 64520 | tf_op jit(solution)/shard_map/ppermute | solution.py:163
  18.4 2.9 %collective-permute-start.8 = (f32[21,256]{1,0:T(8,128)S(1)}, f32[21,256]{1,0:T(8,128)S(1)}, u32[]{:S(2)}, u32[]{:S(2)}) collective-permute-start(f32[21,256]{1,0:T(8,128)S(1)} %get-tuple-element.19.own0.block0_ref), channel_id=1, source_target_pairs={{0,64},{1,3},{2,66},{3,1},{4,68},{5,7},{6,70},{7,5},{8,72},{9,11},... | collective-permute-start | bytes 64520 | tf_op jit(solution)/shard_map/ppermute | solution.py:163
  18.4 2.9 %collective-permute-start.5 = (f32[21,256]{1,0:T(8,128)S(1)}, f32[21,256]{1,0:T(8,128)S(1)}, u32[]{:S(2)}, u32[]{:S(2)}) collective-permute-start(f32[21,256]{1,0:T(8,128)S(1)} %get-tuple-element.20), channel_id=1, source_target_pairs={{0,1},{1,0},{2,3},{3,2},{4,5},{5,4},{6,7},{7,6},{8,9},{9,8},{10,11... | collective-permute-start | bytes 64520 | tf_op jit(solution)/shard_map/ppermute | solution.py:163
  21.8 4.3 %collective-permute-start.10 = (f32[21,256]{1,0:T(8,128)S(1)}, f32[21,256]{1,0:T(8,128)S(1)}, u32[]{:S(2)}, u32[]{:S(2)}) collective-permute-start(f32[21,256]{1,0:T(8,128)S(1)} %shard_map.88.own1), channel_id=1, source_target_pairs={{0,64},{1,5},{2,66},{3,7},{4,68},{5,1},{6,70},{7,3},{8,72},{9,13},... | collective-permute-start | bytes 64520 | tf_op jit(solution)/shard_map/ppermute | solution.py:163
  22.5 3.9 %collective-permute-start.11 = (f32[21,256]{1,0:T(8,128)S(1)}, f32[21,256]{1,0:T(8,128)S(1)}, u32[]{:S(2)}, u32[]{:S(2)}) collective-permute-start(f32[21,256]{1,0:T(8,128)S(1)} %shard_map.88.own1), channel_id=1, source_target_pairs={{0,64},{1,7},{2,66},{3,5},{4,68},{5,3},{6,70},{7,1},{8,72},{9,15},... | collective-permute-start | bytes 64520 | tf_op jit(solution)/shard_map/ppermute | solution.py:163
  24.2 2.7 %collective-permute-start.12 = (f32[21,256]{1,0:T(8,128)S(1)}, f32[21,256]{1,0:T(8,128)S(1)}, u32[]{:S(2)}, u32[]{:S(2)}) collective-permute-start(f32[21,256]{1,0:T(8,128)S(1)} %shard_map.88.own1), channel_id=1, source_target_pairs={{0,64},{1,3},{2,66},{3,1},{4,68},{5,7},{6,70},{7,5},{8,72},{9,11},... | collective-permute-start | bytes 64520 | tf_op jit(solution)/shard_map/ppermute | solution.py:163
  27.3 4.5 %collective-permute-start.13 = (f32[42,256]{1,0:T(8,128)S(1)}, f32[42,256]{1,0:T(8,128)S(1)}, u32[]{:S(2)}, u32[]{:S(2)}) collective-permute-start(f32[42,256]{1,0:T(8,128)S(1)} %shard_map.89), channel_id=1, source_target_pairs={{0,2},{1,129},{2,0},{3,131},{4,6},{5,133},{6,4},{7,135},{8,10},{9,... | collective-permute-start | bytes 129032 | tf_op jit(solution)/shard_map/ppermute | solution.py:163
  29.5 4.2 %collective-permute-start.14 = (f32[42,256]{1,0:T(8,128)S(1)}, f32[42,256]{1,0:T(8,128)S(1)}, u32[]{:S(2)}, u32[]{:S(2)}) collective-permute-start(f32[42,256]{1,0:T(8,128)S(1)} %shard_map.89), channel_id=1, source_target_pairs={{0,2},{1,193},{2,0},{3,195},{4,6},{5,197},{6,4},{7,199},{8,10},{9,... | collective-permute-start | bytes 129032 | tf_op jit(solution)/shard_map/ppermute | solution.py:163
  30.3 3.3 %collective-permute-start.15 = (f32[42,256]{1,0:T(8,128)S(1)}, f32[42,256]{1,0:T(8,128)S(1)}, u32[]{:S(2)}, u32[]{:S(2)}) collective-permute-start(f32[42,256]{1,0:T(8,128)S(1)} %shard_map.89), channel_id=1, source_target_pairs={{0,2},{1,65},{2,0},{3,67},{4,6},{5,69},{6,4},{7,71},{8,10},{9,73},... | collective-permute-start | bytes 129032 | tf_op jit(solution)/shard_map/ppermute | solution.py:163
  33.6 3.2 %collective-permute-start.16 = (f32[42,256]{1,0:T(8,128)S(1)}, f32[42,256]{1,0:T(8,128)S(1)}, u32[]{:S(2)}, u32[]{:S(2)}) collective-permute-start(f32[42,256]{1,0:T(8,128)S(1)} %add_add_fusion.3), channel_id=1, source_target_pairs={{0,2},{1,9},{2,0},{3,11},{4,6},{5,13},{6,4},{7,15},{8,10},{9,1},{1... | collective-permute-start | bytes 129032 | tf_op jit(solution)/shard_map/ppermute | solution.py:163
  36.8 9.5 %collective-permute-start.17 = (f32[42,256]{1,0:T(8,128)S(1)}, f32[42,256]{1,0:T(8,128)S(1)}, u32[]{:S(2)}, u32[]{:S(2)}) collective-permute-start(f32[42,256]{1,0:T(8,128)S(1)} %add.60), channel_id=1, source_target_pairs={{0,2},{2,0},{4,6},{6,4},{8,10},{10,8},{12,14},{14,12},{16,18},{18,... | collective-permute-start | bytes 129032 | tf_op jit(solution)/shard_map/ppermute | solution.py:184
  43.2 3.8 %collective-permute-start.18 = (f32[42,256]{1,0:T(8,128)S(1)}, f32[42,256]{1,0:T(8,128)S(1)}, u32[]{:S(2)}, u32[]{:S(2)}) collective-permute-start(f32[42,256]{1,0:T(8,128)S(1)} %add.60), channel_id=1, source_target_pairs={{0,2},{2,0},{4,6},{6,4},{8,10},{10,8},{12,14},{14,12},{16,18},{18,... | collective-permute-start | bytes 129032 | tf_op jit(solution)/shard_map/ppermute | solution.py:184
  43.5 4.9 %collective-permute-start.19 = (f32[42,256]{1,0:T(8,128)S(1)}, f32[42,256]{1,0:T(8,128)S(1)}, u32[]{:S(2)}, u32[]{:S(2)}) collective-permute-start(f32[42,256]{1,0:T(8,128)S(1)} %add.60), channel_id=1, source_target_pairs={{0,2},{2,0},{4,6},{6,4},{8,10},{10,8},{12,14},{14,12},{16,18},{18,... | collective-permute-start | bytes 129032 | tf_op jit(solution)/shard_map/ppermute | solution.py:184
  48.4 1.3 %collective-permute-start.20 = (f32[42,128]{1,0:T(8,128)S(1)}, f32[42,128]{1,0:T(8,128)S(1)}, u32[]{:S(2)}, u32[]{:S(2)}) collective-permute-start(f32[42,128]{1,0:T(8,128)S(1)} %slice.22), channel_id=1, source_target_pairs={{0,1},{1,0},{2,3},{3,2},{4,5},{5,4},{6,7},{7,6},{8,9},{9,8},{10,11... | collective-permute-start | bytes 64520 | tf_op jit(solution)/shard_map/ppermute | solution.py:163
  49.7 15.1 %copy-start.2 = (f32[21,4096]{1,0:T(8,128)S(1)}, f32[21,4096]{1,0:T(8,128)}, u32[]{:S(2)}) copy-start(f32[21,4096]{1,0:T(8,128)} %base_ref.3) | copy-start | bytes 1032196
  50.4 1.5 %collective-permute-start.21 = (f32[336,128]{1,0:T(8,128)S(1)}, f32[336,128]{1,0:T(8,128)S(1)}, u32[]{:S(2)}, u32[]{:S(2)}) collective-permute-start(f32[336,128]{1,0:T(8,128)S(1)} %shard_map.91), channel_id=1, source_target_pairs={{0,1},{1,0},{2,3},{3,2},{4,5},{5,4},{6,7},{7,6},{8,9},{9,8},{10,11... | collective-permute-start | bytes 516104 | tf_op jit(solution)/shard_map/ppermute | solution.py:163
  51.9 7.4 %collective-permute-start.22 = (f32[336,128]{1,0:T(8,128)S(1)}, f32[336,128]{1,0:T(8,128)S(1)}, u32[]{:S(2)}, u32[]{:S(2)}) collective-permute-start(f32[336,128]{1,0:T(8,128)S(1)} %add.64), channel_id=1, source_target_pairs={{0,4},{1,5},{2,6},{3,7},{4,0},{5,1},{6,2},{7,3},{8,12},{9,13},{10,... | collective-permute-start | bytes 516104 | tf_op jit(solution)/shard_map/ppermute | solution.py:163
  53.8 9.7 %collective-permute-start.23 = (f32[336,128]{1,0:T(8,128)S(1)}, f32[336,128]{1,0:T(8,128)S(1)}, u32[]{:S(2)}, u32[]{:S(2)}) collective-permute-start(f32[336,128]{1,0:T(8,128)S(1)} %add.64), channel_id=1, source_target_pairs={{0,6},{1,7},{2,4},{3,5},{4,2},{5,3},{6,0},{7,1},{8,14},{9,15},{10,... | collective-permute-start | bytes 516104 | tf_op jit(solution)/shard_map/ppermute | solution.py:163
  55.4 8.1 %collective-permute-start.24 = (f32[336,128]{1,0:T(8,128)S(1)}, f32[336,128]{1,0:T(8,128)S(1)}, u32[]{:S(2)}, u32[]{:S(2)}) collective-permute-start(f32[336,128]{1,0:T(8,128)S(1)} %add.64), channel_id=1, source_target_pairs={{0,2},{1,3},{2,0},{3,1},{4,6},{5,7},{6,4},{7,5},{8,10},{9,11},{10,... | collective-permute-start | bytes 516104 | tf_op jit(solution)/shard_map/ppermute | solution.py:163
  63.5 1.9 %collective-permute-start.25 = (f32[336,128]{1,0:T(8,128)S(1)}, f32[336,128]{1,0:T(8,128)S(1)}, u32[]{:S(2)}, u32[]{:S(2)}) collective-permute-start(f32[336,128]{1,0:T(8,128)S(1)} %add_add_fusion.value_ref), channel_id=1, source_target_pairs={{0,1},{1,0},{2,3},{3,2},{4,5},{5,4},{6,7},{7,6},{8,9},{9,8},{10,11... | collective-permute-start | bytes 516104 | tf_op jit(solution)/shard_map/ppermute | solution.py:163

commit v7 on v5

--- a/solution.py
+++ b/solution.py
@@ -204,7 +204,7 @@
     inverses0 = here(other_inverses[0]), here(inverses[0])
     inverses1 = here(other_inverses[1]), here(inverses[1])
     one, two, three = swap(sums, 2, 6), swap(sums, 6, 2), swap(sums, 4)
-    one, coupling = lax.optimization_barrier((one, coupling))
+    three, coupling = lax.optimization_barrier((three, coupling))
     couplings = here(swap(coupling, 1)), here(coupling)
     start = jnp.where(row == 0, lax.dynamic_index_in_dim(rhs, 1 - core, 0, keepdims=False), 0.0)
     sums = (three + two) + (one + sums)

time: 66.6 us -> 67.2 us (level)
  waiting for transfers between devices: 19.8 us -> 21.6 us
  starting transfers between devices: 34.9 us -> 33.7 us
    ppermute x23, waiting for transfers between devices: 17.8 us -> 19.6 us  [swap(): lax.ppermute(value, both, [(i, i ^ masks[i % 2]) for i in range(256)])]
    ppermute x23, starting transfers between devices: 25.4 us -> 24.2 us  [swap(): lax.ppermute(value, both, [(i, i ^ masks[i % 2]) for i in range(256)])]
  transfers between devices with their start and end apart: 26 -> 26, of which waited for: 14 -> 16; matrix products, arithmetic and copies ran while one was open for 6% -> 6% of each run, Pallas kernels for 3% -> 3%
where the time goes in v7:
time: 67.2 us; the launch traced here: 67 us
  starting transfers between devices  33.7 us (50%)
  waiting for transfers between devices  21.6 us (32%)
  Pallas kernels  4.19 us (6%)
  local copies, waits for them, and re-layouts  2.83 us (4%)
  matrix products  2.06 us (3%)
  other arithmetic  1.63 us (2%)
  between operations  1 us (1%)
    ppermute x23, starting transfers between devices, swap(): lax.ppermute(value, both, [(i, i ^ masks[i % 2]) for i in range(256)])  24.2 us
    ppermute x23, waiting for transfers between devices, swap(): lax.ppermute(value, both, [(i, i ^ masks[i % 2]) for i in range(256)])  19.6 us
    ppermute x3, starting transfers between devices, from_z(): return lax.ppermute(value, both, pairs)  9.5 us
    dot_general x2, matrix products, dot(): return jnp.einsum('ij,rj->ri', matrix, value, precision=HIGH)  2.06 us
    ppermute x3, waiting for transfers between devices, from_z(): return lax.ppermute(value, both, pairs)  2 us
    unnamed x9, local copies, waits for them, and re-layouts  1.84 us
    select_n x4, other arithmetic, here(): return lax.optimization_barrier(jnp.where(core >= 0, value, 0.0))  1.48 us
    pallas_call x2, Pallas kernels, trailing_products(): pl.pallas_call(lambda *refs: trailing_kernel(own, *refs), in_specs=[pl.Bl...  1.46 us
  transfers between devices with their start and end apart: 26, of which 16 were waited for; matrix products, arithmetic and copies ran while one was open for 6% of the time, Pallas kernels for 3%

profile of v7, /device:TPU:1, one launch (start us, length us, event | category | flops | bytes accessed | tf_op | source)
XLA Modules:
  0.0 67.0 jit_solution(13603031175029776750)
XLA Ops:
  0.6 0.0 copy-start
  0.7 1.2 %copy-done = f32[2,1024,128]{2,1,0:T(8,128)S(1)} copy-done((f32[2,1024,128]{2,1,0:T(8,128)S(1)}, f32[2,1024,128]{2,1,0:T(8,128)}, u32[]{:S(2)}) %copy-start) | copy-done | bytes 1048600
  1.9 1.0 %convolution_bitcast_fusion = f32[21,1024]{1,0:T(8,128)S(1)} fusion(f32[21,128]{1,0:T(8,128)} %param.8, f32[2,1024,128]{2,1,0:T(8,128)S(1)} %copy-done, s32[]{:T(128)S(6)} %select_n.63), kind=kOutput, calls=%fused_computation | convolution fusion | flops 16515072 | bytes 621060 | tf_op jit(solution)/shard_map/ij,rj->ri/dot_general | solution.py:176
  2.9 3.3 %collective-permute-start = (f32[21,1024]{1,0:T(8,128)S(1)}, f32[21,1024]{1,0:T(8,128)S(1)}, u32[]{:S(2)}, u32[]{:S(2)}) collective-permute-start(f32[21,1024]{1,0:T(8,128)S(1)} %convolution_bitcast_fusion), channel_id=1, source_target_pairs={{0,1},{1,0},{2,3},{3,2},{4,5},{5,4},{6,7},{7,6},{8,9},{9,8},{10,11... | collective-permute-start | bytes 258056 | tf_op jit(solution)/shard_map/ppermute | solution.py:163
  6.2 1.0 %convolution_bitcast_fusion.1.kept_ref = f32[21,1024]{1,0:T(8,128)S(1)} fusion(f32[21,128]{1,0:T(8,128)} %param.8, f32[2,1024,128]{2,1,0:T(8,128)S(1)} %copy-done, s32[]{:T(128)S(6)} %select_n.62), kind=kOutput, calls=%fused_computation.1 | convolution fusion | flops 16515072 | bytes 621060 | tf_op jit(solution)/shard_map/ij,rj->ri/dot_general | solution.py:176
  7.2 0.0 collective-permute-done.taken_ref
  7.3 0.3 collective-permute-start.4
  7.6 1.2 %collective-permute-start.1 = (f32[168,128]{1,0:T(8,128)S(1)}, f32[168,128]{1,0:T(8,128)S(1)}, u32[]{:S(2)}, u32[]{:S(2)}) collective-permute-start(f32[168,128]{1,0:T(8,128)S(1)} %shard_map.86), channel_id=1, source_target_pairs={{0,4},{1,5},{2,6},{3,7},{4,0},{5,1},{6,2},{7,3},{8,12},{9,13},{10,... | collective-permute-start | bytes 258056 | tf_op jit(solution)/shard_map/ppermute | solution.py:163
  8.8 0.4 collective-permute-start.2
  9.2 1.7 %collective-permute-start.3 = (f32[168,128]{1,0:T(8,128)S(1)}, f32[168,128]{1,0:T(8,128)S(1)}, u32[]{:S(2)}, u32[]{:S(2)}) collective-permute-start(f32[168,128]{1,0:T(8,128)S(1)} %shard_map.86), channel_id=1, source_target_pairs={{0,2},{1,7},{2,0},{3,5},{4,6},{5,3},{6,4},{7,1},{8,10},{9,15},{10,... | collective-permute-start | bytes 258056 | tf_op jit(solution)/shard_map/ppermute | solution.py:163
  10.9 1.0 %copy.12 = f32[2,21,1024]{2,1,0:T(8,128)S(1)} copy(f32[2,21,1024]{2,0,1:T(2,128)} %param.9) | data formatting | bytes 344064 | tf_op jit(solution)/shard_map/optimization_barrier | solution.py:202
  11.9 1.3 %select_bitcast_fusion = (f32[128,1024]{1,0:T(8,128)S(1)}, f32[128,1024]{1,0:T(8,128)S(1)}) fusion(f32[2,128,1024]{2,1,0:T(8,128)} %param.10, pred[]{:T(512)S(6)} %ge.2), kind=kLoop, calls=%fused_computation.8 | loop fusion | flops 262144 | bytes 2097153 | tf_op jit(solution)/shard_map/jit(_where)/select_n | solution.py:194
  13.2 0.0 collective-permute-done.1
  13.2 1.5 %collective-permute-start.9 = (f32[128,1024]{1,0:T(8,128)S(1)}, f32[128,1024]{1,0:T(8,128)S(1)}, u32[]{:S(2)}, u32[]{:S(2)}) collective-permute-start(f32[128,1024]{1,0:T(8,128)S(1)} %copy-done.3), channel_id=1, source_target_pairs={{0,1},{1,0},{2,3},{3,2},{4,5},{5,4},{6,7},{7,6},{8,9},{9,8},{10,11... | collective-permute-start | bytes 1572872 | tf_op jit(solution)/shard_map/ppermute | solution.py:163
  14.8 0.0 copy-start.1
  14.8 0.0 collective-permute-done.2
  14.8 0.4 collective-permute-done.3
  15.3 0.1 fusion
  15.4 0.4 shard_map.87
  15.8 1.4 %collective-permute-start.6 = (f32[21,256]{1,0:T(8,128)S(1)}, f32[21,256]{1,0:T(8,128)S(1)}, u32[]{:S(2)}, u32[]{:S(2)}) collective-permute-start(f32[21,256]{1,0:T(8,128)S(1)} %get-tuple-element.19.own0.block0_ref), channel_id=1, source_target_pairs={{0,64},{1,5},{2,66},{3,7},{4,68},{5,1},{6,70},{7,3},{8,72},{9,13},... | collective-permute-start | bytes 64520 | tf_op jit(solution)/shard_map/ppermute | solution.py:163
  17.3 1.0 %collective-permute-start.7 = (f32[21,256]{1,0:T(8,128)S(1)}, f32[21,256]{1,0:T(8,128)S(1)}, u32[]{:S(2)}, u32[]{:S(2)}) collective-permute-start(f32[21,256]{1,0:T(8,128)S(1)} %get-tuple-element.19.own0.block0_ref), channel_id=1, source_target_pairs={{0,64},{1,7},{2,66},{3,5},{4,68},{5,3},{6,70},{7,1},{8,72},{9,15},... | collective-permute-start | bytes 64520 | tf_op jit(solution)/shard_map/ppermute | solution.py:163
  18.2 0.3 collective-permute-start.8
  18.6 1.0 %collective-permute-start.5 = (f32[21,256]{1,0:T(8,128)S(1)}, f32[21,256]{1,0:T(8,128)S(1)}, u32[]{:S(2)}, u32[]{:S(2)}) collective-permute-start(f32[21,256]{1,0:T(8,128)S(1)} %get-tuple-element.20), channel_id=1, source_target_pairs={{0,1},{1,0},{2,3},{3,2},{4,5},{5,4},{6,7},{7,6},{8,9},{9,8},{10,11... | collective-permute-start | bytes 64520 | tf_op jit(solution)/shard_map/ppermute | solution.py:163
  19.6 0.8 %collective-permute-done.5.base_ref = f32[21,256]{1,0:T(8,128)S(1)} collective-permute-done((f32[21,256]{1,0:T(8,128)S(1)}, f32[21,256]{1,0:T(8,128)S(1)}, u32[]{:S(2)}, u32[]{:S(2)}) %collective-permute-start.5) | collective-permute-done | bytes 21536 | tf_op jit(solution)/shard_map/ppermute | solution.py:163
  20.4 0.8 %collective-permute-done.7.three0 = f32[21,256]{1,0:T(8,128)S(1)} collective-permute-done((f32[21,256]{1,0:T(8,128)S(1)}, f32[21,256]{1,0:T(8,128)S(1)}, u32[]{:S(2)}, u32[]{:S(2)}) %collective-permute-start.7) | collective-permute-done | bytes 21536 | tf_op jit(solution)/shard_map/ppermute | solution.py:163
  21.2 0.0 collective-permute-done.8.one0
  21.2 0.4 shard_map.88.own1
  21.6 1.4 %collective-permute-start.10 = (f32[21,256]{1,0:T(8,128)S(1)}, f32[21,256]{1,0:T(8,128)S(1)}, u32[]{:S(2)}, u32[]{:S(2)}) collective-permute-start(f32[21,256]{1,0:T(8,128)S(1)} %shard_map.88.own1), channel_id=1, source_target_pairs={{0,64},{1,5},{2,66},{3,7},{4,68},{5,1},{6,70},{7,3},{8,72},{9,13},... | collective-permute-start | bytes 64520 | tf_op jit(solution)/shard_map/ppermute | solution.py:163
  23.0 1.5 %collective-permute-start.11 = (f32[21,256]{1,0:T(8,128)S(1)}, f32[21,256]{1,0:T(8,128)S(1)}, u32[]{:S(2)}, u32[]{:S(2)}) collective-permute-start(f32[21,256]{1,0:T(8,128)S(1)} %shard_map.88.own1), channel_id=1, source_target_pairs={{0,64},{1,7},{2,66},{3,5},{4,68},{5,3},{6,70},{7,1},{8,72},{9,15},... | collective-permute-start | bytes 64520 | tf_op jit(solution)/shard_map/ppermute | solution.py:163
  24.5 1.4 %collective-permute-done.10.two1 = f32[21,256]{1,0:T(8,128)S(1)} collective-permute-done((f32[21,256]{1,0:T(8,128)S(1)}, f32[21,256]{1,0:T(8,128)S(1)}, u32[]{:S(2)}, u32[]{:S(2)}) %collective-permute-start.10) | collective-permute-done | bytes 21536 | tf_op jit(solution)/shard_map/ppermute | solution.py:163
  25.9 1.0 %collective-permute-done.11.three1 = f32[21,256]{1,0:T(8,128)S(1)} collective-permute-done((f32[21,256]{1,0:T(8,128)S(1)}, f32[21,256]{1,0:T(8,128)S(1)}, u32[]{:S(2)}, u32[]{:S(2)}) %collective-permute-start.11) | collective-permute-done | bytes 21536 | tf_op jit(solution)/shard_map/ppermute | solution.py:163
  26.9 0.5 collective-permute-done.12.one1
  27.3 0.4 shard_map.89
  27.7 2.4 %collective-permute-start.13 = (f32[42,256]{1,0:T(8,128)S(1)}, f32[42,256]{1,0:T(8,128)S(1)}, u32[]{:S(2)}, u32[]{:S(2)}) collective-permute-start(f32[42,256]{1,0:T(8,128)S(1)} %shard_map.89), channel_id=1, source_target_pairs={{0,2},{1,129},{2,0},{3,131},{4,6},{5,133},{6,4},{7,135},{8,10},{9,... | collective-permute-start | bytes 129032 | tf_op jit(solution)/shard_map/ppermute | solution.py:163
  30.1 0.9 %collective-permute-start.14 = (f32[42,256]{1,0:T(8,128)S(1)}, f32[42,256]{1,0:T(8,128)S(1)}, u32[]{:S(2)}, u32[]{:S(2)}) collective-permute-start(f32[42,256]{1,0:T(8,128)S(1)} %shard_map.89), channel_id=1, source_target_pairs={{0,2},{1,193},{2,0},{3,195},{4,6},{5,197},{6,4},{7,199},{8,10},{9,... | collective-permute-start | bytes 129032 | tf_op jit(solution)/shard_map/ppermute | solution.py:163
  31.0 0.0 collective-permute-start.15
  31.0 1.3 %collective-permute-done.13 = f32[42,256]{1,0:T(8,128)S(1)} collective-permute-done((f32[42,256]{1,0:T(8,128)S(1)}, f32[42,256]{1,0:T(8,128)S(1)}, u32[]{:S(2)}, u32[]{:S(2)}) %collective-permute-start.13) | collective-permute-done | bytes 43040 | tf_op jit(solution)/shard_map/ppermute | solution.py:163
  32.3 2.0 %collective-permute-done.14 = f32[42,256]{1,0:T(8,128)S(1)} collective-permute-done((f32[42,256]{1,0:T(8,128)S(1)}, f32[42,256]{1,0:T(8,128)S(1)}, u32[]{:S(2)}, u32[]{:S(2)}) %collective-permute-start.14) | collective-permute-done | bytes 43040 | tf_op jit(solution)/shard_map/ppermute | solution.py:163
  34.3 0.0 collective-permute-done.15
  34.3 1.7 %collective-permute-start.16 = (f32[42,256]{1,0:T(8,128)S(1)}, f32[42,256]{1,0:T(8,128)S(1)}, u32[]{:S(2)}, u32[]{:S(2)}) collective-permute-start(f32[42,256]{1,0:T(8,128)S(1)} %add_add_fusion.3), channel_id=1, source_target_pairs={{0,2},{1,9},{2,0},{3,11},{4,6},{5,13},{6,4},{7,15},{8,10},{9,1},{1... | collective-permute-start | bytes 129032 | tf_op jit(solution)/shard_map/ppermute | solution.py:163
  36.0 1.5 %collective-permute-done.16 = f32[42,256]{1,0:T(8,128)S(1)} collective-permute-done((f32[42,256]{1,0:T(8,128)S(1)}, f32[42,256]{1,0:T(8,128)S(1)}, u32[]{:S(2)}, u32[]{:S(2)}) %collective-permute-start.16) | collective-permute-done | bytes 43040 | tf_op jit(solution)/shard_map/ppermute | solution.py:163
  37.5 6.4 %collective-permute-start.17 = (f32[42,256]{1,0:T(8,128)S(1)}, f32[42,256]{1,0:T(8,128)S(1)}, u32[]{:S(2)}, u32[]{:S(2)}) collective-permute-start(f32[42,256]{1,0:T(8,128)S(1)} %add.60), channel_id=1, source_target_pairs={{0,2},{2,0},{4,6},{6,4},{8,10},{10,8},{12,14},{14,12},{16,18},{18,... | collective-permute-start | bytes 129032 | tf_op jit(solution)/shard_map/ppermute | solution.py:184
  43.9 0.3 collective-permute-start.18
  44.1 2.9 %collective-permute-start.19 = (f32[42,256]{1,0:T(8,128)S(1)}, f32[42,256]{1,0:T(8,128)S(1)}, u32[]{:S(2)}, u32[]{:S(2)}) collective-permute-start(f32[42,256]{1,0:T(8,128)S(1)} %add.60), channel_id=1, source_target_pairs={{0,2},{2,0},{4,6},{6,4},{8,10},{10,8},{12,14},{14,12},{16,18},{18,... | collective-permute-start | bytes 129032 | tf_op jit(solution)/shard_map/ppermute | solution.py:184
  47.0 0.7 %collective-permute-done.18 = f32[42,256]{1,0:T(8,128)S(1)} collective-permute-done((f32[42,256]{1,0:T(8,128)S(1)}, f32[42,256]{1,0:T(8,128)S(1)}, u32[]{:S(2)}, u32[]{:S(2)}) %collective-permute-start.18) | collective-permute-done | bytes 43040 | tf_op jit(solution)/shard_map/ppermute | solution.py:184
  47.7 1.3 %collective-permute-done.19 = f32[42,256]{1,0:T(8,128)S(1)} collective-permute-done((f32[42,256]{1,0:T(8,128)S(1)}, f32[42,256]{1,0:T(8,128)S(1)}, u32[]{:S(2)}, u32[]{:S(2)}) %collective-permute-start.19) | collective-permute-done | bytes 43040 | tf_op jit(solution)/shard_map/ppermute | solution.py:184
  49.0 0.1 collective-permute-start.20
  49.1 1.2 %collective-permute-done.20.refs_2_ = f32[42,128]{1,0:T(8,128)S(1)} collective-permute-done((f32[42,128]{1,0:T(8,128)S(1)}, f32[42,128]{1,0:T(8,128)S(1)}, u32[]{:S(2)}, u32[]{:S(2)}) %collective-permute-start.20) | collective-permute-done | bytes 21536 | tf_op jit(solution)/shard_map/ppermute | solution.py:163
  50.3 0.7 %shard_map.91 = f32[336,128]{1,0:T(8,128)S(1)} custom-call(s32[1]{0:T(128)} %bitcast.refs_0_.half_ref, f32[42,256]{1,0:T(8,128)S(1)} %add_add_fusion.2.refs_1_, f32[42,128]{1,0:T(8,128)S(1)} %collective-permute-done.20.refs_2_, f32[8192,128]{1,0:T(8,128)S(1)} %bitcast.26), custom_call_target="tpu_custom_call" | custom-call | flops 66060288 | bytes 2097152 | tf_op jit(solution)/shard_map/pallas_call | solution.py:118
  51.1 0.2 collective-permute-start.21
  51.3 0.7 %shard_map.90 = (f32[336,128]{1,0:T(8,128)S(1)}, f32[42,128]{1,0:T(8,128)S(1)}) custom-call(s32[1]{0:T(128)} %bitcast.refs_0_.half_ref, f32[42,256]{1,0:T(8,128)S(1)} %add_add_fusion.2.refs_1_, f32[42,128]{1,0:T(8,128)S(1)} %collective-permute-done.20.refs_2_, f32[8192,128]{1,0:T(8,128)S(1)} %bitcast.27), custom_call_target="tpu_custom_call" | custom-call | flops 66060288 | bytes 2097152 | tf_op jit(solution)/shard_map/pallas_call | solution.py:118
  52.0 0.5 collective-permute-done.21
  52.5 1.8 %collective-permute-start.22 = (f32[336,128]{1,0:T(8,128)S(1)}, f32[336,128]{1,0:T(8,128)S(1)}, u32[]{:S(2)}, u32[]{:S(2)}) collective-permute-start(f32[336,128]{1,0:T(8,128)S(1)} %add.64), channel_id=1, source_target_pairs={{0,4},{1,5},{2,6},{3,7},{4,0},{5,1},{6,2},{7,3},{8,12},{9,13},{10,... | collective-permute-start | bytes 516104 | tf_op jit(solution)/shard_map/ppermute | solution.py:163
  54.3 0.4 collective-permute-start.23
  54.7 1.2 %collective-permute-start.24 = (f32[336,128]{1,0:T(8,128)S(1)}, f32[336,128]{1,0:T(8,128)S(1)}, u32[]{:S(2)}, u32[]{:S(2)}) collective-permute-start(f32[336,128]{1,0:T(8,128)S(1)} %add.64), channel_id=1, source_target_pairs={{0,2},{1,7},{2,0},{3,5},{4,6},{5,3},{6,4},{7,1},{8,10},{9,15},{10,... | collective-permute-start | bytes 516104 | tf_op jit(solution)/shard_map/ppermute | solution.py:163
  55.9 4.1 %collective-permute-done.22 = f32[336,128]{1,0:T(8,128)S(1)} collective-permute-done((f32[336,128]{1,0:T(8,128)S(1)}, f32[336,128]{1,0:T(8,128)S(1)}, u32[]{:S(2)}, u32[]{:S(2)}) %collective-permute-start.22) | collective-permute-done | bytes 172064 | tf_op jit(solution)/shard_map/ppermute | solution.py:163
  60.0 2.8 %collective-permute-done.23 = f32[336,128]{1,0:T(8,128)S(1)} collective-permute-done((f32[336,128]{1,0:T(8,128)S(1)}, f32[336,128]{1,0:T(8,128)S(1)}, u32[]{:S(2)}, u32[]{:S(2)}) %collective-permute-start.23) | collective-permute-done | bytes 172064 | tf_op jit(solution)/shard_map/ppermute | solution.py:163
  62.8 1.4 %collective-permute-done.24 = f32[336,128]{1,0:T(8,128)S(1)} collective-permute-done((f32[336,128]{1,0:T(8,128)S(1)}, f32[336,128]{1,0:T(8,128)S(1)}, u32[]{:S(2)}, u32[]{:S(2)}) %collective-permute-start.24) | collective-permute-done | bytes 172064 | tf_op jit(solution)/shard_map/ppermute | solution.py:163
  64.2 0.1 add_add_fusion.value_ref
  64.2 0.5 collective-permute-start.25
  64.8 0.6 copy.13
  65.4 0.7 %shard_map.92.rest_0_ = f32[21,4096]{1,0:T(8,128)} custom-call(s32[1]{0:T(128)} %bitcast.refs_0_.half_ref, f32[336,128]{1,0:T(8,128)S(1)} %add_add_fusion.value_ref, f32[21,4096]{1,0:T(8,128)S(1)} %copy-done.2), custom_call_target="tpu_custom_call" | custom-call | tf_op jit(solution)/shard_map/pallas_call | solution.py:144
  66.1 0.0 collective-permute-done.25.value_ref
  66.1 0.7 %shard_map.93 = f32[21,4096]{1,0:T(8,128)} custom-call(s32[1]{0:T(128)} %bitcast.12.half_ref, f32[336,128]{1,0:T(8,128)S(1)} %collective-permute-done.25.value_ref, f32[21,4096]{1,0:T(8,128)S(1)} %copy-done.2, f32[21,4096]{1,0:T(8,128)} %shard_map.92.rest_0_), custom_call_target="tpu_custom_call", output_to_operand_aliasing={{}: (3, {})} | custom-call | tf_op jit(solution)/shard_map/pallas_call | solution.py:144
  (21 shorter events, 0.2 us)
Async XLA Ops:
  0.6 1.2 %copy-start = (f32[2,1024,128]{2,1,0:T(8,128)S(1)}, f32[2,1024,128]{2,1,0:T(8,128)}, u32[]{:S(2)}) copy-start(f32[2,1024,128]{2,1,0:T(8,128)} %param.7) | copy-start | bytes 3145732
  0.6 12.6 %copy-start.3 = (f32[128,1024]{1,0:T(8,128)S(1)}, f32[128,1024]{1,0:T(8,128)}, u32[]{:S(2)}) copy-start(f32[128,1024]{1,0:T(8,128)} %param.11) | copy-start | bytes 1572868
  2.9 4.4 %collective-permute-start = (f32[21,1024]{1,0:T(8,128)S(1)}, f32[21,1024]{1,0:T(8,128)S(1)}, u32[]{:S(2)}, u32[]{:S(2)}) collective-permute-start(f32[21,1024]{1,0:T(8,128)S(1)} %convolution_bitcast_fusion), channel_id=1, source_target_pairs={{0,1},{1,0},{2,3},{3,2},{4,5},{5,4},{6,7},{7,6},{8,9},{9,8},{10,11... | collective-permute-start | bytes 258056 | tf_op jit(solution)/shard_map/ppermute | solution.py:163
  7.3 8.0 %collective-permute-start.4 = (f32[2,128,1024]{2,1,0:T(8,128)}, f32[2,128,1024]{2,1,0:T(8,128)S(1)}, u32[]{:S(2)}, u32[]{:S(2)}) collective-permute-start(f32[2,128,1024]{2,1,0:T(8,128)} %param.10), channel_id=1, source_target_pairs={{0,1},{1,0},{2,3},{3,2},{4,5},{5,4},{6,7},{7,6},{8,9},{9,8},{10,11... | collective-permute-start | bytes 3145736 | tf_op jit(solution)/shard_map/ppermute | solution.py:163
  7.6 5.6 %collective-permute-start.1 = (f32[168,128]{1,0:T(8,128)S(1)}, f32[168,128]{1,0:T(8,128)S(1)}, u32[]{:S(2)}, u32[]{:S(2)}) collective-permute-start(f32[168,128]{1,0:T(8,128)S(1)} %shard_map.86), channel_id=1, source_target_pairs={{0,4},{1,5},{2,6},{3,7},{4,0},{5,1},{6,2},{7,3},{8,12},{9,13},{10,... | collective-permute-start | bytes 258056 | tf_op jit(solution)/shard_map/ppermute | solution.py:163
  8.8 6.0 %collective-permute-start.2 = (f32[168,128]{1,0:T(8,128)S(1)}, f32[168,128]{1,0:T(8,128)S(1)}, u32[]{:S(2)}, u32[]{:S(2)}) collective-permute-start(f32[168,128]{1,0:T(8,128)S(1)} %shard_map.86), channel_id=1, source_target_pairs={{0,6},{1,3},{2,4},{3,1},{4,2},{5,7},{6,0},{7,5},{8,14},{9,11},{10,... | collective-permute-start | bytes 258056 | tf_op jit(solution)/shard_map/ppermute | solution.py:163
  9.2 6.1 %collective-permute-start.3 = (f32[168,128]{1,0:T(8,128)S(1)}, f32[168,128]{1,0:T(8,128)S(1)}, u32[]{:S(2)}, u32[]{:S(2)}) collective-permute-start(f32[168,128]{1,0:T(8,128)S(1)} %shard_map.86), channel_id=1, source_target_pairs={{0,2},{1,7},{2,0},{3,5},{4,6},{5,3},{6,4},{7,1},{8,10},{9,15},{10,... | collective-permute-start | bytes 258056 | tf_op jit(solution)/shard_map/ppermute | solution.py:163
  13.2 6.3 %collective-permute-start.9 = (f32[128,1024]{1,0:T(8,128)S(1)}, f32[128,1024]{1,0:T(8,128)S(1)}, u32[]{:S(2)}, u32[]{:S(2)}) collective-permute-start(f32[128,1024]{1,0:T(8,128)S(1)} %copy-done.3), channel_id=1, source_target_pairs={{0,1},{1,0},{2,3},{3,2},{4,5},{5,4},{6,7},{7,6},{8,9},{9,8},{10,11... | collective-permute-start | bytes 1572872 | tf_op jit(solution)/shard_map/ppermute | solution.py:163
  14.8 35.5 %copy-start.1 = (f32[4096,2,128]{2,1,0:T(2,128)S(1)}, f32[4096,2,128]{2,1,0:T(2,128)}, u32[]{:S(2)}) copy-start(f32[4096,2,128]{2,1,0:T(2,128)} %param.12) | copy-start | bytes 12582916
  15.8 4.6 %collective-permute-start.6 = (f32[21,256]{1,0:T(8,128)S(1)}, f32[21,256]{1,0:T(8,128)S(1)}, u32[]{:S(2)}, u32[]{:S(2)}) collective-permute-start(f32[21,256]{1,0:T(8,128)S(1)} %get-tuple-element.19.own0.block0_ref), channel_id=1, source_target_pairs={{0,64},{1,5},{2,66},{3,7},{4,68},{5,1},{6,70},{7,3},{8,72},{9,13},... | collective-permute-start | bytes 64520 | tf_op jit(solution)/shard_map/ppermute | solution.py:163
  17.3 3.9 %collective-permute-start.7 = (f32[21,256]{1,0:T(8,128)S(1)}, f32[21,256]{1,0:T(8,128)S(1)}, u32[]{:S(2)}, u32[]{:S(2)}) collective-permute-start(f32[21,256]{1,0:T(8,128)S(1)} %get-tuple-element.19.own0.block0_ref), channel_id=1, source_target_pairs={{0,64},{1,7},{2,66},{3,5},{4,68},{5,3},{6,70},{7,1},{8,72},{9,15},... | collective-permute-start | bytes 64520 | tf_op jit(solution)/shard_map/ppermute | solution.py:163
  18.2 2.9 %collective-permute-start.8 = (f32[21,256]{1,0:T(8,128)S(1)}, f32[21,256]{1,0:T(8,128)S(1)}, u32[]{:S(2)}, u32[]{:S(2)}) collective-permute-start(f32[21,256]{1,0:T(8,128)S(1)} %get-tuple-element.19.own0.block0_ref), channel_id=1, source_target_pairs={{0,64},{1,3},{2,66},{3,1},{4,68},{5,7},{6,70},{7,5},{8,72},{9,11},... | collective-permute-start | bytes 64520 | tf_op jit(solution)/shard_map/ppermute | solution.py:163
  18.6 1.8 %collective-permute-start.5 = (f32[21,256]{1,0:T(8,128)S(1)}, f32[21,256]{1,0:T(8,128)S(1)}, u32[]{:S(2)}, u32[]{:S(2)}) collective-permute-start(f32[21,256]{1,0:T(8,128)S(1)} %get-tuple-element.20), channel_id=1, source_target_pairs={{0,1},{1,0},{2,3},{3,2},{4,5},{5,4},{6,7},{7,6},{8,9},{9,8},{10,11... | collective-permute-start | bytes 64520 | tf_op jit(solution)/shard_map/ppermute | solution.py:163
  21.6 4.3 %collective-permute-start.10 = (f32[21,256]{1,0:T(8,128)S(1)}, f32[21,256]{1,0:T(8,128)S(1)}, u32[]{:S(2)}, u32[]{:S(2)}) collective-permute-start(f32[21,256]{1,0:T(8,128)S(1)} %shard_map.88.own1), channel_id=1, source_target_pairs={{0,64},{1,5},{2,66},{3,7},{4,68},{5,1},{6,70},{7,3},{8,72},{9,13},... | collective-permute-start | bytes 64520 | tf_op jit(solution)/shard_map/ppermute | solution.py:163
  23.0 3.9 %collective-permute-start.11 = (f32[21,256]{1,0:T(8,128)S(1)}, f32[21,256]{1,0:T(8,128)S(1)}, u32[]{:S(2)}, u32[]{:S(2)}) collective-permute-start(f32[21,256]{1,0:T(8,128)S(1)} %shard_map.88.own1), channel_id=1, source_target_pairs={{0,64},{1,7},{2,66},{3,5},{4,68},{5,3},{6,70},{7,1},{8,72},{9,15},... | collective-permute-start | bytes 64520 | tf_op jit(solution)/shard_map/ppermute | solution.py:163
  24.5 2.9 %collective-permute-start.12 = (f32[21,256]{1,0:T(8,128)S(1)}, f32[21,256]{1,0:T(8,128)S(1)}, u32[]{:S(2)}, u32[]{:S(2)}) collective-permute-start(f32[21,256]{1,0:T(8,128)S(1)} %shard_map.88.own1), channel_id=1, source_target_pairs={{0,64},{1,3},{2,66},{3,1},{4,68},{5,7},{6,70},{7,5},{8,72},{9,11},... | collective-permute-start | bytes 64520 | tf_op jit(solution)/shard_map/ppermute | solution.py:163
  27.7 4.5 %collective-permute-start.13 = (f32[42,256]{1,0:T(8,128)S(1)}, f32[42,256]{1,0:T(8,128)S(1)}, u32[]{:S(2)}, u32[]{:S(2)}) collective-permute-start(f32[42,256]{1,0:T(8,128)S(1)} %shard_map.89), channel_id=1, source_target_pairs={{0,2},{1,129},{2,0},{3,131},{4,6},{5,133},{6,4},{7,135},{8,10},{9,... | collective-permute-start | bytes 129032 | tf_op jit(solution)/shard_map/ppermute | solution.py:163
  30.1 4.2 %collective-permute-start.14 = (f32[42,256]{1,0:T(8,128)S(1)}, f32[42,256]{1,0:T(8,128)S(1)}, u32[]{:S(2)}, u32[]{:S(2)}) collective-permute-start(f32[42,256]{1,0:T(8,128)S(1)} %shard_map.89), channel_id=1, source_target_pairs={{0,2},{1,193},{2,0},{3,195},{4,6},{5,197},{6,4},{7,199},{8,10},{9,... | collective-permute-start | bytes 129032 | tf_op jit(solution)/shard_map/ppermute | solution.py:163
  31.0 3.3 %collective-permute-start.15 = (f32[42,256]{1,0:T(8,128)S(1)}, f32[42,256]{1,0:T(8,128)S(1)}, u32[]{:S(2)}, u32[]{:S(2)}) collective-permute-start(f32[42,256]{1,0:T(8,128)S(1)} %shard_map.89), channel_id=1, source_target_pairs={{0,2},{1,65},{2,0},{3,67},{4,6},{5,69},{6,4},{7,71},{8,10},{9,73},... | collective-permute-start | bytes 129032 | tf_op jit(solution)/shard_map/ppermute | solution.py:163
  34.3 3.2 %collective-permute-start.16 = (f32[42,256]{1,0:T(8,128)S(1)}, f32[42,256]{1,0:T(8,128)S(1)}, u32[]{:S(2)}, u32[]{:S(2)}) collective-permute-start(f32[42,256]{1,0:T(8,128)S(1)} %add_add_fusion.3), channel_id=1, source_target_pairs={{0,2},{1,9},{2,0},{3,11},{4,6},{5,13},{6,4},{7,15},{8,10},{9,1},{1... | collective-permute-start | bytes 129032 | tf_op jit(solution)/shard_map/ppermute | solution.py:163
  37.5 9.5 %collective-permute-start.17 = (f32[42,256]{1,0:T(8,128)S(1)}, f32[42,256]{1,0:T(8,128)S(1)}, u32[]{:S(2)}, u32[]{:S(2)}) collective-permute-start(f32[42,256]{1,0:T(8,128)S(1)} %add.60), channel_id=1, source_target_pairs={{0,2},{2,0},{4,6},{6,4},{8,10},{10,8},{12,14},{14,12},{16,18},{18,... | collective-permute-start | bytes 129032 | tf_op jit(solution)/shard_map/ppermute | solution.py:184
  43.9 3.8 %collective-permute-start.18 = (f32[42,256]{1,0:T(8,128)S(1)}, f32[42,256]{1,0:T(8,128)S(1)}, u32[]{:S(2)}, u32[]{:S(2)}) collective-permute-start(f32[42,256]{1,0:T(8,128)S(1)} %add.60), channel_id=1, source_target_pairs={{0,2},{2,0},{4,6},{6,4},{8,10},{10,8},{12,14},{14,12},{16,18},{18,... | collective-permute-start | bytes 129032 | tf_op jit(solution)/shard_map/ppermute | solution.py:184
  44.1 4.9 %collective-permute-start.19 = (f32[42,256]{1,0:T(8,128)S(1)}, f32[42,256]{1,0:T(8,128)S(1)}, u32[]{:S(2)}, u32[]{:S(2)}) collective-permute-start(f32[42,256]{1,0:T(8,128)S(1)} %add.60), channel_id=1, source_target_pairs={{0,2},{2,0},{4,6},{6,4},{8,10},{10,8},{12,14},{14,12},{16,18},{18,... | collective-permute-start | bytes 129032 | tf_op jit(solution)/shard_map/ppermute | solution.py:184
  49.0 1.3 %collective-permute-start.20 = (f32[42,128]{1,0:T(8,128)S(1)}, f32[42,128]{1,0:T(8,128)S(1)}, u32[]{:S(2)}, u32[]{:S(2)}) collective-permute-start(f32[42,128]{1,0:T(8,128)S(1)} %slice.22), channel_id=1, source_target_pairs={{0,1},{1,0},{2,3},{3,2},{4,5},{5,4},{6,7},{7,6},{8,9},{9,8},{10,11... | collective-permute-start | bytes 64520 | tf_op jit(solution)/shard_map/ppermute | solution.py:163
  50.3 15.1 %copy-start.2 = (f32[21,4096]{1,0:T(8,128)S(1)}, f32[21,4096]{1,0:T(8,128)}, u32[]{:S(2)}) copy-start(f32[21,4096]{1,0:T(8,128)} %base_ref.3) | copy-start | bytes 1032196
  51.1 1.5 %collective-permute-start.21 = (f32[336,128]{1,0:T(8,128)S(1)}, f32[336,128]{1,0:T(8,128)S(1)}, u32[]{:S(2)}, u32[]{:S(2)}) collective-permute-start(f32[336,128]{1,0:T(8,128)S(1)} %shard_map.91), channel_id=1, source_target_pairs={{0,1},{1,0},{2,3},{3,2},{4,5},{5,4},{6,7},{7,6},{8,9},{9,8},{10,11... | collective-permute-start | bytes 516104 | tf_op jit(solution)/shard_map/ppermute | solution.py:163
  52.5 7.4 %collective-permute-start.22 = (f32[336,128]{1,0:T(8,128)S(1)}, f32[336,128]{1,0:T(8,128)S(1)}, u32[]{:S(2)}, u32[]{:S(2)}) collective-permute-start(f32[336,128]{1,0:T(8,128)S(1)} %add.64), channel_id=1, source_target_pairs={{0,4},{1,5},{2,6},{3,7},{4,0},{5,1},{6,2},{7,3},{8,12},{9,13},{10,... | collective-permute-start | bytes 516104 | tf_op jit(solution)/shard_map/ppermute | solution.py:163
  54.3 8.5 %collective-permute-start.23 = (f32[336,128]{1,0:T(8,128)S(1)}, f32[336,128]{1,0:T(8,128)S(1)}, u32[]{:S(2)}, u32[]{:S(2)}) collective-permute-start(f32[336,128]{1,0:T(8,128)S(1)} %add.64), channel_id=1, source_target_pairs={{0,6},{1,3},{2,4},{3,1},{4,2},{5,7},{6,0},{7,5},{8,14},{9,11},{10,... | collective-permute-start | bytes 516104 | tf_op jit(solution)/shard_map/ppermute | solution.py:163
  54.7 9.4 %collective-permute-start.24 = (f32[336,128]{1,0:T(8,128)S(1)}, f32[336,128]{1,0:T(8,128)S(1)}, u32[]{:S(2)}, u32[]{:S(2)}) collective-permute-start(f32[336,128]{1,0:T(8,128)S(1)} %add.64), channel_id=1, source_target_pairs={{0,2},{1,7},{2,0},{3,5},{4,6},{5,3},{6,4},{7,1},{8,10},{9,15},{10,... | collective-permute-start | bytes 516104 | tf_op jit(solution)/shard_map/ppermute | solution.py:163
  64.2 1.9 %collective-permute-start.25 = (f32[336,128]{1,0:T(8,128)S(1)}, f32[336,128]{1,0:T(8,128)S(1)}, u32[]{:S(2)}, u32[]{:S(2)}) collective-permute-start(f32[336,128]{1,0:T(8,128)S(1)} %add_add_fusion.value_ref), channel_id=1, source_target_pairs={{0,1},{1,0},{2,3},{3,2},{4,5},{5,4},{6,7},{7,6},{8,9},{9,8},{10,11... | collective-permute-start | bytes 516104 | tf_op jit(solution)/shard_map/ppermute | solution.py:163
